TPU v7x, 32 devices: a whole 2x2x4 slice. The times are simulated.
32 devices in a mesh: seq: 4 (over z), fsdp: 8 (over y, x, core).
Axes of the slice: x: 2, y: 2, z: 4, core: 2. Of those that a mesh axis runs over, the one named last changes fastest.
Arguments:
- inputs: bfloat16 [8, 1024, 1024], P('fsdp', 'seq'), may hold values from -6 to 6
- lengths: int32 [8, 3], P('fsdp'), may hold values from 1 to 1022, as said below
- ffn_in: bfloat16 [1, 2, 1024, 4096], P(None, None, ('seq', 'fsdp')), may hold values from -0.1875 to 0.1875
- ffn_out: bfloat16 [1, 2, 4096, 1024], P(None, None, None, ('seq', 'fsdp')), may hold values from -0.09375 to 0.09375
- qkv_weight: bfloat16 [1, 1024, 3072], P(None, ('seq', 'fsdp')), may hold values from -0.1875 to 0.1875
- out_weight: bfloat16 [1, 1024, 1024], P(None, ('seq', 'fsdp')), may hold values from -1 to 1
- conv_in: bfloat16 [1, 1024, 2048], P(None, ('seq', 'fsdp')), may hold values from -0.1875 to 0.1875
- conv_depth: bfloat16 [1, 31, 1024], P(None, None, ('seq', 'fsdp')), may hold values from -1 to 1
- conv_out: bfloat16 [1, 1024, 1024], P(None, ('seq', 'fsdp')), may hold values from -0.1875 to 0.1875
- norm_gain: bfloat16 [1, 6, 1024], P(None, None, ('seq', 'fsdp')), may hold values from 0.5 to 1.5
- norm_bias: bfloat16 [1, 6, 1024], P(None, None, ('seq', 'fsdp')), may hold values from -4 to 4
- rel_key: bfloat16 [1, 73, 64], replicated, may hold values from -6 to 6
- cotangent: bfloat16 [8, 1024, 1024], P('fsdp', 'seq'), may hold values from -6 to 6
Outputs:
- output: bfloat16 [8, 1024, 1024], P('fsdp', 'seq')
- input_grad: float32 [8, 1024, 1024], P('fsdp', 'seq')
- ffn_in_grad: float32 [1, 2, 1024, 4096], P(None, None, ('seq', 'fsdp'))
- ffn_out_grad: float32 [1, 2, 4096, 1024], P(None, None, None, ('seq', 'fsdp'))
- qkv_grad: float32 [1, 1024, 3072], P(None, ('seq', 'fsdp'))
- out_grad: float32 [1, 1024, 1024], P(None, ('seq', 'fsdp'))
- conv_in_grad: float32 [1, 1024, 2048], P(None, ('seq', 'fsdp'))
- conv_depth_grad: float32 [1, 31, 1024], P(None, None, ('seq', 'fsdp'))
- conv_out_grad: float32 [1, 1024, 1024], P(None, ('seq', 'fsdp'))
- gain_grad: float32 [1, 6, 1024], P(None, None, ('seq', 'fsdp'))
- bias_grad: float32 [1, 6, 1024], P(None, None, ('seq', 'fsdp'))
- rel_grad: float32 [1, 73, 64], replicated
Inputs may be any that keep to these rules, and one draw needn't show every extreme that they name: In each group the 3 clip lengths sum to 1024; one clip, which one drawn from the seed, starts among the group's first 256 positions and ends among its last 256; the other clips are shorter than half of 256. In one group, drawn from the seed, the other clips have length 1, so that its long clip has 1022 tokens.
All inputs are finite; a program needn't handle non-finite values.
Results may differ from a plain program's by a relative error of at most 0.015.
Values may be sent and summed in bfloat16 or wider, within the bound.
No kernel may reach another device: no remote copies, remote signals or barrier semaphores. Data moves between devices by JAX's collectives and lax.ppermute only.
A program may use at most 256 MiB of HBM per device.

v0:
```python
import jax
import jax.numpy as jnp
from jax import lax
from jax.sharding import PartitionSpec as P

HEAD_DIM = 64
KERNEL = 31
LEFT = 64
RIGHT = 8


def passed_along(shard, axis, by):
    count = lax.axis_size(axis)
    pairs = [(i, i + by) for i in range(count) if 0 <= i + by < count]
    return lax.ppermute(shard, axis, pairs)


def layer_norm(values, gain_row, bias_row):
    centered = values - jnp.mean(values, axis=-1, keepdims=True)
    variance = jnp.mean(centered * centered, axis=-1, keepdims=True)
    inverse = lax.rsqrt(variance + 1e-05)
    normal_part = centered * inverse
    return (normal_part * gain_row + bias_row, (normal_part, inverse))


def norm_back(gradient, cached, gain_row):
    normal_part, inverse = cached
    scaled = gradient * gain_row
    inner = jnp.mean(scaled * normal_part, axis=-1, keepdims=True)
    input_grad = inverse * (scaled - jnp.mean(scaled, axis=-1, keepdims=True) - normal_part * inner)
    return (input_grad, jnp.sum(gradient * normal_part, axis=0), jnp.sum(gradient, axis=0))


def swish_slope(values):
    sigmoid_val = jax.nn.sigmoid(values)
    return sigmoid_val * (1.0 + values * (1.0 - sigmoid_val))


def skew_band(rel_scores, key_count):
    head_count, row_count, band_width = rel_scores.shape
    padded = jnp.pad(rel_scores, ((0, 0), (0, 0), (0, key_count + 1 - band_width)))
    flattened = padded.reshape(head_count, row_count * (key_count + 1))[:, : row_count * key_count]
    return flattened.reshape(head_count, row_count, key_count)


def unskew_band(grads, band_width):
    head_count, row_count, key_count = grads.shape
    flattened = jnp.pad(grads.reshape(head_count, row_count * key_count), ((0, 0), (0, row_count)))
    return flattened.reshape(head_count, row_count, key_count + 1)[:, :, :band_width]


def band_scores(query_heads, key_heads, relative, allowed):
    content = jnp.einsum("ihd,jhd->hij", query_heads, key_heads, preferred_element_type=jnp.float32)
    positional = jnp.einsum(
        "ihd,rd->hir", query_heads, relative, preferred_element_type=jnp.float32
    )
    scores = (content + skew_band(positional, key_heads.shape[0])) * query_heads.shape[2] ** (-0.5)
    return jnp.where(allowed[None], scores, -1e30)


def local(
    inputs,
    lengths,
    ffn_in,
    ffn_out,
    qkv_weight,
    out_weight,
    conv_in,
    conv_depth,
    conv_out,
    norm_gain,
    norm_bias,
    rel_key,
    cotangent,
):
    row_count = inputs.shape[1]
    feature_dim = inputs.shape[2]
    layer_count = ffn_in.shape[0]
    margin = KERNEL - 1
    key_count = row_count + LEFT + RIGHT
    scale = HEAD_DIM ** (-0.5)
    first_row = lax.axis_index("seq") * row_count
    clip_ends = jnp.cumsum(lengths[0])

    def clip_of(offset, count_rows):
        positions = first_row + offset + jnp.arange(count_rows, dtype=jnp.int32)
        inside = jnp.sum((positions[:, None] >= clip_ends[None, :]).astype(jnp.int32), axis=1)
        return jnp.where(positions < 0, -1, inside)

    own_ids = clip_of(0, row_count)
    key_ids = clip_of(-LEFT, key_count)
    conv_ids = clip_of(-margin, row_count + margin)
    offsets = jnp.arange(key_count)[None, :] - jnp.arange(row_count)[:, None]
    allowed = (offsets >= 0) & (offsets <= LEFT + RIGHT) & (own_ids[:, None] == key_ids[None, :])
    tap_masks = [
        (conv_ids[tap_index : tap_index + row_count] == own_ids)[:, None]
        for tap_index in range(KERNEL)
    ]
    stream = inputs[0].astype(jnp.float32)
    layer_index = 0
    weights = (
        lax.all_gather(ffn_in[layer_index], ("seq", "fsdp"), axis=1, tiled=True),
        lax.all_gather(ffn_out[layer_index], ("seq", "fsdp"), axis=2, tiled=True),
        lax.all_gather(qkv_weight[layer_index], ("seq", "fsdp"), axis=0, tiled=True),
        lax.all_gather(out_weight[layer_index], ("seq", "fsdp"), axis=0, tiled=True),
        lax.all_gather(conv_in[layer_index], ("seq", "fsdp"), axis=0, tiled=True),
        lax.all_gather(conv_depth[layer_index], ("seq", "fsdp"), axis=1, tiled=True),
        lax.all_gather(conv_out[layer_index], ("seq", "fsdp"), axis=0, tiled=True),
        lax.all_gather(norm_gain[layer_index], ("seq", "fsdp"), axis=1, tiled=True),
        lax.all_gather(norm_bias[layer_index], ("seq", "fsdp"), axis=1, tiled=True),
    )
    w_in, w_down, w_qkv, w_out, w_first, w_taps, w_second, gain_rows, bias_rows = weights
    gains = gain_rows.astype(jnp.float32)
    biases = bias_rows.astype(jnp.float32)
    tap_values = w_taps.astype(jnp.float32)

    def feed_forward(values, which_net, norm_index):
        normed, norm_cache = layer_norm(values, gains[norm_index], biases[norm_index])
        normed_low = normed.astype(jnp.bfloat16)
        pre_act = jnp.dot(normed_low, w_in[which_net], preferred_element_type=jnp.float32)
        act_low = (pre_act * jax.nn.sigmoid(pre_act)).astype(jnp.bfloat16)
        branch = jnp.dot(act_low, w_down[which_net], preferred_element_type=jnp.float32)
        return (values + 0.5 * branch, (norm_cache, normed_low, pre_act, act_low))

    after_ffn, ffn_first = feed_forward(stream, 0, 0)
    normed, attn_norm = layer_norm(after_ffn, gains[1], biases[1])
    attn_input = normed.astype(jnp.bfloat16)
    projected = jnp.dot(attn_input, w_qkv, preferred_element_type=jnp.float32).astype(jnp.bfloat16)
    key_values = projected[:, feature_dim:]
    from_left = passed_along(key_values[row_count - LEFT :], "seq", 1)
    from_right = passed_along(key_values[:RIGHT], "seq", -1)
    window_kv = jnp.concatenate([from_left, key_values, from_right], axis=0)
    query_heads = projected[:, :feature_dim].reshape(row_count, -1, HEAD_DIM)
    key_heads = window_kv[:, :feature_dim].reshape(key_count, -1, HEAD_DIM)
    value_heads = window_kv[:, feature_dim:].reshape(key_count, -1, HEAD_DIM)
    masked = band_scores(query_heads, key_heads, rel_key[layer_index], allowed)
    highest = jnp.max(masked, axis=-1, keepdims=True)
    expanded = jnp.exp(masked - highest)
    summed = jnp.sum(expanded, axis=-1, keepdims=True)
    log_total = highest + jnp.log(summed)
    probs_low = (expanded / summed).astype(jnp.bfloat16)
    attended = (
        jnp.einsum("hij,jhd->ihd", probs_low, value_heads, preferred_element_type=jnp.float32)
        .reshape(row_count, feature_dim)
        .astype(jnp.bfloat16)
    )
    after_attn = after_ffn + jnp.dot(attended, w_out, preferred_element_type=jnp.float32)
    normed, conv_norm = layer_norm(after_attn, gains[2], biases[2])
    conv_input = normed.astype(jnp.bfloat16)
    spread = jnp.dot(conv_input, w_first, preferred_element_type=jnp.float32)
    gate_sig = jax.nn.sigmoid(spread[:, feature_dim:])
    gated_low = (spread[:, :feature_dim] * gate_sig).astype(jnp.bfloat16)
    from_prev = passed_along(gated_low[row_count - margin :], "seq", 1)
    extended = jnp.concatenate([from_prev, gated_low], axis=0)
    filtered = jnp.zeros((row_count, feature_dim), jnp.float32)
    for tap_index in range(KERNEL):
        filtered = (
            filtered
            + jnp.where(tap_masks[tap_index], extended[tap_index : tap_index + row_count], 0)
            * tap_values[tap_index]
        )
    normed_conv, depth_norm = layer_norm(filtered, gains[3], biases[3])
    swished = (normed_conv * jax.nn.sigmoid(normed_conv)).astype(jnp.bfloat16)
    after_conv = after_attn + jnp.dot(swished, w_second, preferred_element_type=jnp.float32)
    fourth, ffn_second = feed_forward(after_conv, 1, 4)
    result, final_norm = layer_norm(fourth, gains[5], biases[5])
    saved = (
        ffn_first,
        attn_norm,
        attn_input,
        projected,
        window_kv,
        log_total,
        attended,
        conv_norm,
        conv_input,
        spread,
        gate_sig,
        extended,
        normed_conv,
        depth_norm,
        swished,
        ffn_second,
        final_norm,
    )
    stream, saved = (result, saved)
    layer_saves = [saved]
    outputs = stream.astype(jnp.bfloat16)[None]
    grad_stream = cotangent[0].astype(jnp.float32)
    reduced = [None] * layer_count
    rel_terms = [None] * layer_count
    for layer_index in reversed(range(layer_count)):
        weights = (
            lax.all_gather(ffn_in[layer_index], ("seq", "fsdp"), axis=1, tiled=True),
            lax.all_gather(ffn_out[layer_index], ("seq", "fsdp"), axis=2, tiled=True),
            lax.all_gather(qkv_weight[layer_index], ("seq", "fsdp"), axis=0, tiled=True),
            lax.all_gather(out_weight[layer_index], ("seq", "fsdp"), axis=0, tiled=True),
            lax.all_gather(conv_in[layer_index], ("seq", "fsdp"), axis=0, tiled=True),
            lax.all_gather(conv_depth[layer_index], ("seq", "fsdp"), axis=1, tiled=True),
            lax.all_gather(conv_out[layer_index], ("seq", "fsdp"), axis=0, tiled=True),
            lax.all_gather(norm_gain[layer_index], ("seq", "fsdp"), axis=1, tiled=True),
            lax.all_gather(norm_bias[layer_index], ("seq", "fsdp"), axis=1, tiled=True),
        )
        relative = rel_key[layer_index]
        (
            backward_w_in,
            backward_w_down,
            backward_w_qkv,
            backward_w_out,
            backward_w_first,
            backward_w_taps,
            backward_w_second,
            backward_gain_rows,
            backward_bias_rows,
        ) = weights
        backward_gains = backward_gain_rows.astype(jnp.float32)
        backward_tap_values = backward_w_taps.astype(jnp.float32)
        (
            backward_ffn_first,
            backward_attn_norm,
            backward_attn_input,
            backward_projected,
            backward_window_kv,
            backward_log_total,
            backward_attended,
            backward_conv_norm,
            backward_conv_input,
            backward_spread,
            backward_gate_sig,
            backward_extended,
            backward_normed_conv,
            backward_depth_norm,
            backward_swished,
            backward_ffn_second,
            backward_final_norm,
        ) = layer_saves[layer_index]

        def feed_back(gradient, which_net, norm_index, cached):
            norm_cache, normed_low, pre_act, act_low = cached
            branch_grad = (0.5 * gradient).astype(jnp.bfloat16)
            grad_down = jnp.einsum(
                "tf,td->fd", act_low, branch_grad, preferred_element_type=jnp.float32
            )
            act_grad = jnp.einsum(
                "td,fd->tf",
                branch_grad,
                backward_w_down[which_net],
                preferred_element_type=jnp.float32,
            )
            pre_grad = (act_grad * swish_slope(pre_act)).astype(jnp.bfloat16)
            grad_in = jnp.einsum(
                "td,tf->df", normed_low, pre_grad, preferred_element_type=jnp.float32
            )
            normed_grad = jnp.einsum(
                "tf,df->td", pre_grad, backward_w_in[which_net], preferred_element_type=jnp.float32
            )
            input_grad, gain_grad, bias_grad = norm_back(
                normed_grad, norm_cache, backward_gains[norm_index]
            )
            return (gradient + input_grad, grad_in, grad_down, gain_grad, bias_grad)

        gain_grads = [None] * 6
        bias_grads = [None] * 6
        grad_fourth, gain_grads[5], bias_grads[5] = norm_back(
            grad_stream, backward_final_norm, backward_gains[5]
        )
        grad_conv_out, in_second, down_second, gain_grads[4], bias_grads[4] = feed_back(
            grad_fourth, 1, 4, backward_ffn_second
        )
        branch_grad = grad_conv_out.astype(jnp.bfloat16)
        backward_grad_second_w = jnp.einsum(
            "tc,td->cd", backward_swished, branch_grad, preferred_element_type=jnp.float32
        )
        swish_grad = jnp.einsum(
            "td,cd->tc", branch_grad, backward_w_second, preferred_element_type=jnp.float32
        )
        filter_grad, gain_grads[3], bias_grads[3] = norm_back(
            swish_grad * swish_slope(backward_normed_conv), backward_depth_norm, backward_gains[3]
        )
        tap_grads = []
        extended_grad = jnp.zeros((row_count + margin, feature_dim), jnp.float32)
        for backward_tap_index in range(KERNEL):
            masked_grad = jnp.where(tap_masks[backward_tap_index], filter_grad, 0.0)
            tap_grads.append(
                jnp.sum(
                    masked_grad
                    * backward_extended[backward_tap_index : backward_tap_index + row_count],
                    axis=0,
                )
            )
            extended_grad = extended_grad + jnp.pad(
                masked_grad * backward_tap_values[backward_tap_index],
                ((backward_tap_index, margin - backward_tap_index), (0, 0)),
            )
        to_prev = passed_along(extended_grad[:margin].astype(jnp.bfloat16), "seq", -1).astype(
            jnp.float32
        )
        gated_grad = extended_grad[margin:] + jnp.pad(to_prev, ((row_count - margin, 0), (0, 0)))
        spread_grad = jnp.concatenate(
            [
                gated_grad * backward_gate_sig,
                gated_grad
                * backward_spread[:, :feature_dim]
                * backward_gate_sig
                * (1.0 - backward_gate_sig),
            ],
            axis=1,
        ).astype(jnp.bfloat16)
        backward_grad_first_w = jnp.einsum(
            "tc,te->ce", backward_conv_input, spread_grad, preferred_element_type=jnp.float32
        )
        normed_grad = jnp.einsum(
            "te,ce->tc", spread_grad, backward_w_first, preferred_element_type=jnp.float32
        )
        input_grad, gain_grads[2], bias_grads[2] = norm_back(
            normed_grad, backward_conv_norm, backward_gains[2]
        )
        grad_attn_out = grad_conv_out + input_grad
        branch_grad = grad_attn_out.astype(jnp.bfloat16)
        backward_grad_out_w = jnp.einsum(
            "tc,td->cd", backward_attended, branch_grad, preferred_element_type=jnp.float32
        )
        attended_grad = (
            jnp.einsum("td,cd->tc", branch_grad, backward_w_out, preferred_element_type=jnp.float32)
            .astype(jnp.bfloat16)
            .reshape(row_count, -1, HEAD_DIM)
        )
        backward_query_heads = backward_projected[:, :feature_dim].reshape(row_count, -1, HEAD_DIM)
        backward_key_heads = backward_window_kv[:, :feature_dim].reshape(key_count, -1, HEAD_DIM)
        backward_value_heads = backward_window_kv[:, feature_dim:].reshape(key_count, -1, HEAD_DIM)
        probs = jnp.exp(
            band_scores(backward_query_heads, backward_key_heads, relative, allowed)
            - backward_log_total
        )
        backward_probs_low = probs.astype(jnp.bfloat16)
        prob_grads = jnp.einsum(
            "ihd,jhd->hij", attended_grad, backward_value_heads, preferred_element_type=jnp.float32
        )
        score_grads = (
            probs * (prob_grads - jnp.sum(prob_grads * probs, axis=-1, keepdims=True))
        ).astype(jnp.bfloat16)
        band_grads = unskew_band(score_grads, LEFT + RIGHT + 1)
        query_grad = (
            jnp.einsum(
                "hij,jhd->ihd", score_grads, backward_key_heads, preferred_element_type=jnp.float32
            )
            + jnp.einsum("hir,rd->ihd", band_grads, relative, preferred_element_type=jnp.float32)
        ) * scale
        relative_grad = (
            jnp.einsum(
                "hir,ihd->rd", band_grads, backward_query_heads, preferred_element_type=jnp.float32
            )
            * scale
        )
        key_grad = (
            jnp.einsum(
                "hij,ihd->jhd",
                score_grads,
                backward_query_heads,
                preferred_element_type=jnp.float32,
            )
            * scale
        )
        value_grad = jnp.einsum(
            "hij,ihd->jhd", backward_probs_low, attended_grad, preferred_element_type=jnp.float32
        )
        window_grad = jnp.concatenate(
            [key_grad.reshape(key_count, feature_dim), value_grad.reshape(key_count, feature_dim)],
            axis=1,
        )
        to_left = passed_along(window_grad[:LEFT].astype(jnp.bfloat16), "seq", -1).astype(
            jnp.float32
        )
        to_right = passed_along(
            window_grad[LEFT + row_count :].astype(jnp.bfloat16), "seq", 1
        ).astype(jnp.float32)
        own_grad = (
            window_grad[LEFT : LEFT + row_count]
            + jnp.pad(to_left, ((row_count - LEFT, 0), (0, 0)))
            + jnp.pad(to_right, ((0, row_count - RIGHT), (0, 0)))
        )
        projected_grad = jnp.concatenate(
            [query_grad.reshape(row_count, feature_dim), own_grad], axis=1
        ).astype(jnp.bfloat16)
        backward_grad_qkv_w = jnp.einsum(
            "tc,te->ce", backward_attn_input, projected_grad, preferred_element_type=jnp.float32
        )
        normed_grad = jnp.einsum(
            "te,ce->tc", projected_grad, backward_w_qkv, preferred_element_type=jnp.float32
        )
        input_grad, gain_grads[1], bias_grads[1] = norm_back(
            normed_grad, backward_attn_norm, backward_gains[1]
        )
        grad_ffn_out = grad_attn_out + input_grad
        grad_input, in_first, down_first, gain_grads[0], bias_grads[0] = feed_back(
            grad_ffn_out, 0, 0, backward_ffn_first
        )
        weight_terms = (
            jnp.stack([in_first, in_second]),
            jnp.stack([down_first, down_second]),
            backward_grad_qkv_w,
            backward_grad_out_w,
            backward_grad_first_w,
            jnp.stack(tap_grads),
            backward_grad_second_w,
            jnp.stack(gain_grads),
            jnp.stack(bias_grads),
        )
        grad_stream, weight_terms, rel_terms[layer_index] = (
            grad_input,
            weight_terms,
            relative_grad,
        )
        (
            grad_in_w,
            grad_down_w,
            grad_qkv_w,
            grad_out_w,
            grad_first_w,
            grad_taps_w,
            grad_second_w,
            grad_gains,
            grad_biases,
        ) = weight_terms
        reduced[layer_index] = (
            lax.psum_scatter(grad_in_w, ("seq", "fsdp"), scatter_dimension=1, tiled=True),
            lax.psum_scatter(grad_down_w, ("seq", "fsdp"), scatter_dimension=2, tiled=True),
            lax.psum_scatter(grad_qkv_w, ("seq", "fsdp"), scatter_dimension=0, tiled=True),
            lax.psum_scatter(grad_out_w, ("seq", "fsdp"), scatter_dimension=0, tiled=True),
            lax.psum_scatter(grad_first_w, ("seq", "fsdp"), scatter_dimension=0, tiled=True),
            lax.psum_scatter(grad_taps_w, ("seq", "fsdp"), scatter_dimension=1, tiled=True),
            lax.psum_scatter(grad_second_w, ("seq", "fsdp"), scatter_dimension=0, tiled=True),
            lax.psum_scatter(grad_gains, ("seq", "fsdp"), scatter_dimension=1, tiled=True),
            lax.psum_scatter(grad_biases, ("seq", "fsdp"), scatter_dimension=1, tiled=True),
        )
    rel_total = lax.psum(jnp.stack(rel_terms), ("seq", "fsdp"))
    stacked = [jnp.stack([reduced[0][member]]) for member in range(9)]
    return (
        outputs,
        grad_stream[None],
        stacked[0],
        stacked[1],
        stacked[2],
        stacked[3],
        stacked[4],
        stacked[5],
        stacked[6],
        stacked[7],
        stacked[8],
        rel_total,
    )


def solution(mesh):
    placed = (
        P("fsdp", "seq", None),
        P("fsdp", None),
        P(None, None, ("seq", "fsdp"), None),
        P(None, None, None, ("seq", "fsdp")),
        P(None, ("seq", "fsdp"), None),
        P(None, ("seq", "fsdp"), None),
        P(None, ("seq", "fsdp"), None),
        P(None, None, ("seq", "fsdp")),
        P(None, ("seq", "fsdp"), None),
        P(None, None, ("seq", "fsdp")),
        P(None, None, ("seq", "fsdp")),
        P(),
        P("fsdp", "seq", None),
    )
    return jax.shard_map(
        local,
        mesh=mesh,
        in_specs=placed,
        out_specs=(
            P("fsdp", "seq", None),
            P("fsdp", "seq", None),
            P(None, None, ("seq", "fsdp"), None),
            P(None, None, None, ("seq", "fsdp")),
            P(None, ("seq", "fsdp"), None),
            P(None, ("seq", "fsdp"), None),
            P(None, ("seq", "fsdp"), None),
            P(None, None, ("seq", "fsdp")),
            P(None, ("seq", "fsdp"), None),
            P(None, None, ("seq", "fsdp")),
            P(None, None, ("seq", "fsdp")),
            P(),
        ),
        check_vma=False,
    )
```

profile of v0, /device:TPU:0, one launch (start us, length us, event | category | flops | bytes accessed | tf_op | source)
XLA Modules:
  0.0 2429.3 jit_solution(15151455690398963398)
XLA Ops:
  15.0 46.3 %all-gather.7 = bf16[1,31,1024]{1,0,2:T(2,128)(2,1)S(1)} all-gather(bf16[1,31,32]{1,0,2:T(2,128)(2,1)S(1)} %copy.84), channel_id=9, replica_groups=mesh['seq'=4,'fsdp'=8] {'seq','fsdp'}, dimensions={2}, use_global_device_ids=true | all-gather | bytes 65472 | tf_op jit(solution)/shard_map/all_gather | solution.py:107
  61.8 44.3 %slice_reduce_fusion.35 = (f32[1024]{0:T(1024)S(1)}, f32[1024]{0:T(1024)S(1)}, f32[1024]{0:T(1024)S(1)}, f32[1024]{0:T(1024)S(1)}, f32[1024]{0:T(1024)S(1)}, /*i...) fusion(f32[1,31,1024]{1,0,2:T(1,128)S(1)} %convert_element_type.505), kind=kLoop, calls=%fused_computation.327 | loop fusion | bytes 98304 | tf_op jit(solution)/shard_map/slice | solution.py:160
  106.1 77.1 %slice_reduce_fusion.36 = (f32[1024]{0:T(1024)S(1)}, f32[1024]{0:T(1024)S(1)}, f32[1024]{0:T(1024)S(1)}, f32[1024]{0:T(1024)S(1)}, f32[1024]{0:T(1024)S(1)}, /*i...) fusion(f32[1,31,1024]{1,0,2:T(1,128)S(1)} %convert_element_type.505), kind=kLoop, calls=%fused_computation.328 | loop fusion | bytes 155648 | tf_op jit(solution)/shard_map/slice | solution.py:160
  184.9 40.4 %all-gather.1 = bf16[1,6,1024]{1,0,2:T(2,128)(2,1)S(1)} all-gather(bf16[1,6,32]{1,0,2:T(2,128)(2,1)S(1)} %copy.78), channel_id=3, replica_groups=mesh['seq'=4,'fsdp'=8] {'seq','fsdp'}, dimensions={2}, use_global_device_ids=true | all-gather | bytes 12672 | tf_op jit(solution)/shard_map/all_gather | solution.py:110
  225.8 18.0 slice_reduce_fusion
  243.8 40.1 %all-gather = bf16[1,6,1024]{1,0,2:T(2,128)(2,1)S(1)} all-gather(bf16[1,6,32]{1,0,2:T(2,128)(2,1)S(1)} %copy.77), channel_id=2, replica_groups=mesh['seq'=4,'fsdp'=8] {'seq','fsdp'}, dimensions={2}, use_global_device_ids=true | all-gather | bytes 12672 | tf_op jit(solution)/shard_map/all_gather | solution.py:109
  284.5 17.9 slice_reduce_fusion.1
  302.4 8.0 fusion.1
  310.4 7.3 fusion.165
  352.1 9.7 reshape.355
  383.0 59.8 %all-gather.24.cloned.1.call-done = bf16[1,1024,2048]{2,1,0:T(8,128)(2,1)} async-done(((bf16[1,32,2048]{2,1,0:T(8,128)(2,1)}), bf16[1,1024,2048]{2,1,0:T(8,128)(2,1)}) %all-gather.24.cloned.1.call-update) | async-done | bytes 4194320 | tf_op jit(solution)/shard_map/all_gather | solution.py:106
  452.4 8.4 fusion.163
  461.2 39.4 %all-gather.26.cloned.1.call-done = bf16[1,1024,1024]{2,1,0:T(8,128)(2,1)} async-done(((bf16[1,32,1024]{2,1,0:T(8,128)(2,1)}), bf16[1,1024,1024]{2,1,0:T(8,128)(2,1)}) %all-gather.26.cloned.1.call-update) | async-done | bytes 2097168 | tf_op jit(solution)/shard_map/all_gather | solution.py:108
  509.3 7.5 fusion.169
  524.1 6.7 multiply_reduce_fusion.1
  554.5 8.1 pad_add_fusion
  564.4 10.9 convolution_bitcast_fusion
  613.3 8.5 reshape.358
  630.7 9.7 collective-permute-done.5
  650.3 6.7 fusion.14
  662.0 10.5 convolution_bitcast_fusion.1
  673.8 23.6 pad_maximum_fusion.1
  697.4 49.4 %copy.88 = f32[2,4096,1024]{1,0,2:T(2,128)} copy(f32[2,4096,1024]{2,1,0:T(8,128)} %pad_maximum_fusion.1) | data formatting | bytes 67108864 | tf_op jit(solution)/shard_map/stack | solution.py:400
  779.6 11.7 pad_maximum_fusion
  793.9 41.1 %psum.7 = f32[1,73,64]{1,2,0:T(8,128)} all-reduce(f32[1,73,64]{1,2,0:T(8,128)S(1)} %fusion.75), channel_id=1, replica_groups=mesh['seq'=4,'fsdp'=8] {'seq','fsdp'}, use_global_device_ids=true, to_apply=%region_83.84 | all-reduce | flops 4672 | bytes 37376 | tf_op jit(solution)/shard_map/psum | solution.py:436
  844.7 131.1 %reduce-scatter.27.cloned.1.call-done = f32[32,6]{1,0:T(8,128)} async-done(((f32[1024,6]{1,0:T(8,128)}), f32[32,6]{1,0:T(8,128)}) %reduce-scatter.27.cloned.1.call-update) | async-done | bytes 784
  977.2 500.8 %all-reduce.39.cloned.1.call-done = f32[2,4096,1024]{1,0,2:T(2,128)} async-done(((f32[2,4096,1024]{1,0,2:T(2,128)}), f32[2,4096,1024]{1,0,2:T(2,128)}) %all-reduce.39.cloned.1.call-update) | async-done | bytes 33554448
  1480.8 140.6 %reduce-scatter.23.cloned.1.call-done = f32[32,1024]{1,0:T(8,128)} async-done(((f32[1024,1024]{1,0:T(8,128)}), f32[32,1024]{1,0:T(8,128)}) %reduce-scatter.23.cloned.1.call-update) | async-done | bytes 131088 | tf_op jit(solution)/shard_map/reduce_scatter | solution.py:432
  1621.4 139.5 %reduce-scatter.19.cloned.1.call-done = f32[32,1024]{1,0:T(8,128)} async-done(((f32[1024,1024]{1,0:T(8,128)}), f32[32,1024]{1,0:T(8,128)}) %reduce-scatter.19.cloned.1.call-update) | async-done | bytes 131088 | tf_op jit(solution)/shard_map/reduce_scatter | solution.py:429
  1760.9 147.6 %reduce-scatter.21.cloned.1.call-done = f32[32,2048]{1,0:T(8,128)} async-done(((f32[1024,2048]{1,0:T(8,128)}), f32[32,2048]{1,0:T(8,128)}) %reduce-scatter.21.cloned.1.call-update) | async-done | bytes 262160 | tf_op jit(solution)/shard_map/reduce_scatter | solution.py:430
  1908.5 157.8 %reduce-scatter.17.cloned.1.call-done = f32[32,3072]{1,0:T(8,128)} async-done(((f32[1024,3072]{1,0:T(8,128)}), f32[32,3072]{1,0:T(8,128)}) %reduce-scatter.17.cloned.1.call-update) | async-done | bytes 393232 | tf_op jit(solution)/shard_map/reduce_scatter | solution.py:428
  2066.3 356.2 %reduce-scatter.15.cloned.1.call-done = f32[2,32,4096]{2,1,0:T(8,128)} async-done(((f32[2,1024,4096]{2,1,0:T(8,128)}), f32[2,32,4096]{2,1,0:T(8,128)}) %reduce-scatter.15.cloned.1.call-update) | async-done | bytes 1048592 | tf_op jit(solution)/shard_map/reduce_scatter | solution.py:426
  (448 shorter events, 228.5 us)
Async XLA Ops:
  7.2 325.9 %copy-start = (bf16[1,73,64]{1,2,0:T(8,128)(2,1)S(1)}, bf16[1,73,64]{1,2,0:T(8,128)(2,1)}, u32[]{:S(2)}) copy-start(bf16[1,73,64]{1,2,0:T(8,128)(2,1)} %param.24) | copy-start | bytes 28036
  7.2 295.2 %all-gather.16.cloned.1.call-start = ((), (), s32[]{:S(2)}) async-start(), calls=%async_computation.13 | async-start | bytes 17301504 | tf_op jit(solution)/shard_map/all_gather | solution.py:102
  7.9 302.5 %all-gather.18.cloned.1.call-start = ((), (), s32[]{:S(2)}) async-start(), calls=%async_computation.14 | async-start | bytes 17301504 | tf_op jit(solution)/shard_map/all_gather | solution.py:103
  8.7 312.8 %all-gather.20.cloned.1.call-start = ((), (), s32[]{:S(2)}) async-start(), calls=%async_computation.15 | async-start | bytes 6488064 | tf_op jit(solution)/shard_map/all_gather | solution.py:104
  9.4 370.7 %all-gather.22.cloned.1.call-start = ((), (), s32[]{:S(2)}) async-start(), calls=%async_computation.16 | async-start | bytes 2162688 | tf_op jit(solution)/shard_map/all_gather | solution.py:105
  10.0 432.8 %all-gather.24.cloned.1.call-start = ((), (), s32[]{:S(2)}) async-start(), calls=%async_computation.17 | async-start | bytes 4325376 | tf_op jit(solution)/shard_map/all_gather | solution.py:106
  10.6 489.9 %all-gather.26.cloned.1.call-start = ((), (), s32[]{:S(2)}) async-start(), calls=%async_computation.18 | async-start | bytes 2162688 | tf_op jit(solution)/shard_map/all_gather | solution.py:108
  11.2 823.9 %reduce-scatter.25.cloned.1.call-start = ((), (), s32[]{:S(2)}) async-start(), calls=%async_computation.19 | async-start | bytes 540672
  13.5 438.7 %copy-start.75 = (pred[256]{0:T(512)(128)(4,1)}, pred[256]{0:T(512)(128)(4,1)S(1)}, u32[]{:S(2)}) copy-start(pred[256]{0:T(512)(128)(4,1)S(1)} %get-tuple-element.232) | copy-start | bytes 772
  14.2 438.0 %copy-start.69 = (pred[256]{0:T(512)(128)(4,1)}, pred[256]{0:T(512)(128)(4,1)S(1)}, u32[]{:S(2)}) copy-start(pred[256]{0:T(512)(128)(4,1)S(1)} %get-tuple-element.222) | copy-start | bytes 772
  14.2 438.0 %copy-start.71 = (pred[256]{0:T(512)(128)(4,1)}, pred[256]{0:T(512)(128)(4,1)S(1)}, u32[]{:S(2)}) copy-start(pred[256]{0:T(512)(128)(4,1)S(1)} %get-tuple-element.223) | copy-start | bytes 772
  14.2 438.0 %copy-start.73 = (pred[256]{0:T(512)(128)(4,1)}, pred[256]{0:T(512)(128)(4,1)S(1)}, u32[]{:S(2)}) copy-start(pred[256]{0:T(512)(128)(4,1)S(1)} %get-tuple-element.228) | copy-start | bytes 772
  243.8 199.0 %copy-start.56 = (f32[1024]{0:T(1024)}, f32[1024]{0:T(1024)S(1)}, u32[]{:S(2)}) copy-start(f32[1024]{0:T(1024)S(1)} %get-tuple-element.135) | copy-start | bytes 12292
  243.8 259.5 %copy-start.54 = (f32[1024]{0:T(1024)}, f32[1024]{0:T(1024)S(1)}, u32[]{:S(2)}) copy-start(f32[1024]{0:T(1024)S(1)} %get-tuple-element.133) | copy-start | bytes 12292
  302.4 228.4 %copy-start.50 = (f32[1024]{0:T(1024)}, f32[1024]{0:T(1024)S(1)}, u32[]{:S(2)}) copy-start(f32[1024]{0:T(1024)S(1)} %get-tuple-element.127) | copy-start | bytes 12292
  326.3 42.1 %collective-permute-start.1 = (bf16[8,2048]{1,0:T(8,128)(2,1)S(1)}, bf16[8,2048]{1,0:T(8,128)(2,1)S(1)}, u32[]{:S(2)}, u32[]{:S(2)}) collective-permute-start(bf16[8,2048]{1,0:T(8,128)(2,1)S(1)} %slice.632), channel_id=1, source_target_pairs={{8,0},{16,8},{24,16},{9,1},{17,9},{25,17},{10,2},{18,10},{26,18},{... | collective-permute-start | bytes 98312 | tf_op jit(solution)/shard_map/ppermute | solution.py:15
  327.6 40.8 %collective-permute-start = (bf16[64,2048]{1,0:T(8,128)(2,1)S(1)}, bf16[64,2048]{1,0:T(8,128)(2,1)}, u32[]{:S(2)}, u32[]{:S(2)}) collective-permute-start(bf16[64,2048]{1,0:T(8,128)(2,1)S(1)} %slice.630), channel_id=1, source_target_pairs={{0,8},{8,16},{16,24},{1,9},{9,17},{17,25},{2,10},{10,18},{18,26},{... | collective-permute-start | bytes 786440 | tf_op jit(solution)/shard_map/ppermute | solution.py:15
  333.1 262.9 %copy-start.18 = (bf16[256,1024]{0,1:T(8,128)(2,1)}, bf16[256,1024]{0,1:T(8,128)(2,1)S(1)}, u32[]{:S(2)}) copy-start(bf16[256,1024]{0,1:T(8,128)(2,1)S(1)} %copy.80) | copy-start | bytes 1572868
  382.7 198.7 %copy-start.3 = (f32[256,1024]{1,0:T(8,128)}, f32[256,1024]{1,0:T(8,128)S(1)}, u32[]{:S(2)}) copy-start(f32[256,1024]{1,0:T(8,128)S(1)} %get-tuple-element.246) | copy-start | bytes 3145732
  446.9 5.2 collective-permute-start.2
  562.6 13.9 collective-permute-start.3
  576.5 266.8 %reduce-scatter.29.cloned.1.call-start = ((), (), s32[]{:S(2)}) async-start(), calls=%async_computation.21 | async-start | bytes 540672
  621.8 18.6 collective-permute-start.4
  623.2 17.2 collective-permute-start.5
  661.9 313.9 %reduce-scatter.27.cloned.1.call-start = ((), (), s32[]{:S(2)}) async-start(), calls=%async_computation.20 | async-start | bytes 540672
  673.5 804.4 %all-reduce.39.cloned.1.call-start = ((), (), s32[]{:S(2)}) async-start(), calls=%async_computation.22 | async-start | bytes 67108864
  746.9 874.5 %reduce-scatter.23.cloned.1.call-start = ((), (), s32[]{:S(2)}) async-start(), calls=%async_computation.12 | async-start | bytes 4325376 | tf_op jit(solution)/shard_map/reduce_scatter | solution.py:432
  752.4 1008.5 %reduce-scatter.19.cloned.1.call-start = ((), (), s32[]{:S(2)}) async-start(), calls=%async_computation.10 | async-start | bytes 4325376 | tf_op jit(solution)/shard_map/reduce_scatter | solution.py:429
  756.1 1152.4 %reduce-scatter.21.cloned.1.call-start = ((), (), s32[]{:S(2)}) async-start(), calls=%async_computation.11 | async-start | bytes 8650752 | tf_op jit(solution)/shard_map/reduce_scatter | solution.py:430
  762.2 1304.1 %reduce-scatter.17.cloned.1.call-start = ((), (), s32[]{:S(2)}) async-start(), calls=%async_computation.9 | async-start | bytes 12976128 | tf_op jit(solution)/shard_map/reduce_scatter | solution.py:428
  770.2 1652.3 %reduce-scatter.15.cloned.1.call-start = ((), (), s32[]{:S(2)}) async-start(), calls=%async_computation.8 | async-start | bytes 34603008 | tf_op jit(solution)/shard_map/reduce_scatter | solution.py:426
  836.4 1586.1 %copy-start.1 = (bf16[1,73,64]{1,2,0:T(8,128)(2,1)S(1)}, bf16[1,73,64]{1,2,0:T(8,128)(2,1)}, u32[]{:S(2)}) copy-start(bf16[1,73,64]{1,2,0:T(8,128)(2,1)} %param.24) | copy-start | bytes 28036
  (122 other events, 1769.0 us)
Sparse Core Ops, SparseCore 0:
  10.9 119.2 all-gather.15
  133.2 115.2 all-gather.17
  251.3 70.1 all-gather.19
  324.2 54.9 all-gather.21
  381.9 60.8 all-gather.23
  445.5 54.9 all-gather.25
  576.6 134.4 reduce-scatter.24
  713.4 129.8 reduce-scatter.28
  845.6 130.1 reduce-scatter.26
  983.1 494.8 all-reduce.38
  1480.8 140.5 reduce-scatter.22
  1624.1 136.7 reduce-scatter.18
  1763.7 144.7 reduce-scatter.20
  1915.0 151.3 reduce-scatter.16
  2069.1 353.3 reduce-scatter.14
where the time goes:
time: 2440 us; the launch traced here: 2430 us
  waiting for transfers between devices  1700 us (70%)
  local copies, waits for them, and re-layouts  291 us (12%)
  blocking collectives  168 us (7%)
  matrix products  144 us (6%)
  other arithmetic  93.5 us (4%)
    unnamed x19, waiting for transfers between devices  641 us
    reduce_scatter x1, waiting for transfers between devices, local(): lax.psum_scatter(grad_in_w, ('seq', 'fsdp'), scatter_dimension=1, tiled=T...  356 us
    reduce_scatter x1, waiting for transfers between devices, local(): lax.psum_scatter(grad_qkv_w, ('seq', 'fsdp'), scatter_dimension=0, tiled=...  158 us
    reduce_scatter x1, waiting for transfers between devices, local(): lax.psum_scatter(grad_first_w, ('seq', 'fsdp'), scatter_dimension=0, tile...  148 us
    reduce_scatter x1, waiting for transfers between devices, local(): lax.psum_scatter(grad_second_w, ('seq', 'fsdp'), scatter_dimension=0, til...  141 us
    reduce_scatter x1, waiting for transfers between devices, local(): lax.psum_scatter(grad_out_w, ('seq', 'fsdp'), scatter_dimension=0, tiled=...  139 us
    slice x2, local copies, waits for them, and re-layouts, local(): tap_values[tap_index]  121 us
    all_gather x1, waiting for transfers between devices, local(): lax.all_gather(conv_in[layer_index], ('seq', 'fsdp'), axis=0, tiled=True)  59.8 us
  transfers between devices with their start and end apart: 21, of which 13 were waited for; matrix products, arithmetic and copies ran while one was open for 19% of the time, Pallas kernels for 0%

commit v1 on v0

v1 whole, which is shorter than its diff:
```python
import jax
import jax.numpy as jnp
from jax import lax
from jax.sharding import PartitionSpec as P

HEAD_DIM = 64
KERNEL = 31
LEFT = 64
RIGHT = 8
BF = jnp.bfloat16
F32 = jnp.float32


class Place:
    def __init__(self):
        self.seq_size = lax.axis_size("seq")
        self.fsdp_size = lax.axis_size("fsdp")
        self.chips = self.fsdp_size // 2
        self.seq = lax.axis_index("seq")
        fsdp = lax.axis_index("fsdp")
        self.core = lax.rem(fsdp, 2)
        self.chip = lax.div(fsdp, 2)
        self.bits = self.chips.bit_length() - 1
        self.half = self.seq_size // 2

    def sibling(self, shard):
        return lax.ppermute(shard, "fsdp", [(i, i ^ 1) for i in range(self.fsdp_size)])

    def hop(self, shard, bit):
        return lax.ppermute(shard, "fsdp", [(i, i ^ (2 << bit)) for i in range(self.fsdp_size)])

    def along(self, shard, by):
        pairs = [(i, i + by) for i in range(self.seq_size) if 0 <= i + by < self.seq_size]
        return lax.ppermute(shard, "seq", pairs)

    def swap_seq(self, blocks):
        return lax.all_to_all(blocks, "seq", 0, 0, tiled=True)

    def bit(self, bit):
        return lax.rem(lax.div(self.chip, 1 << bit), 2)

    def both(self, mine):
        return jnp.stack([mine, self.sibling(mine)])

    def mine_of(self, partial):
        return partial[0] + self.sibling(partial[1].astype(BF)).astype(F32)

    def by_core(self, mine, other, axis):
        return jnp.where(
            self.core == 0,
            jnp.concatenate([mine, other], axis),
            jnp.concatenate([other, mine], axis),
        )

    def core_part(self, array, axis, which):
        size = array.shape[axis] // 2
        return lax.dynamic_slice_in_dim(array, which * size, size, axis)


def tie(array, *marks):
    ready = None
    for mark in marks:
        if mark is None:
            continue
        equal = mark == mark
        ready = equal if ready is None else jnp.logical_and(ready, equal)
    return array if ready is None else jnp.where(ready, array, jnp.zeros_like(array))


def tip(array):
    return array[(0,) * array.ndim]


def gather_plane(place, part, turn, marks):
    bits = place.bits
    current = part.reshape((part.shape[0],) + (1,) * bits + part.shape[1:])
    for step in range(bits):
        bit = (turn + step) % bits
        axis = bits - bit
        other = place.hop(current, bit)
        marks.append(tip(other))
        current = jnp.where(
            place.bit(bit) == 0,
            jnp.concatenate([current, other], axis),
            jnp.concatenate([other, current], axis),
        )
    return current.reshape((part.shape[0], place.chips) + part.shape[1:])


def scatter_plane(place, full, turn, marks):
    bits = place.bits
    current = full.reshape((full.shape[0],) + (2,) * bits + full.shape[2:])
    for step in range(bits):
        bit = (turn + step) % bits
        axis = bits - bit
        me = place.bit(bit)
        keep = lax.dynamic_slice_in_dim(current, me, 1, axis)
        sent = lax.dynamic_slice_in_dim(current, 1 - me, 1, axis)
        got = place.hop(sent, bit)
        marks.append(tip(got))
        current = (keep.astype(F32) + got.astype(F32)).astype(BF)
    return current.reshape((full.shape[0],) + full.shape[2:])


def wide_to_seq(wide, half):
    n = wide.shape[-1] // 2
    return jnp.stack([wide[..., :n], wide[..., n:]], 1).reshape((2 * half,) + wide.shape[1:-1] + (n,))


def seq_to_wide(narrow, half):
    pairs = narrow.reshape((half, 2) + narrow.shape[1:])
    return jnp.concatenate([pairs[:, 0], pairs[:, 1]], -1)


def layer_norm(values, gain_row, bias_row):
    centered = values - jnp.mean(values, axis=-1, keepdims=True)
    variance = jnp.mean(centered * centered, axis=-1, keepdims=True)
    inverse = lax.rsqrt(variance + 1e-05)
    normal_part = centered * inverse
    return (normal_part * gain_row + bias_row, (normal_part, inverse))


def norm_back(gradient, cached, gain_row):
    normal_part, inverse = cached
    scaled = gradient * gain_row
    inner = jnp.mean(scaled * normal_part, axis=-1, keepdims=True)
    input_grad = inverse * (scaled - jnp.mean(scaled, axis=-1, keepdims=True) - normal_part * inner)
    return (input_grad, jnp.sum(gradient * normal_part, axis=0), jnp.sum(gradient, axis=0))


def split_layer_norm(place, values, gain_row, bias_row):
    count = values.shape[-1]
    own_mean = jnp.mean(values, axis=-1, keepdims=True)
    own_square = jnp.sum((values - own_mean) ** 2, axis=-1, keepdims=True)
    stats = jnp.concatenate([own_mean, own_square], -1)
    others = place.sibling(stats)[::-1]
    mean = 0.5 * (own_mean + others[..., :1])
    square = own_square + others[..., 1:]
    square = square + count * ((own_mean - mean) ** 2 + (others[..., :1] - mean) ** 2)
    inverse = lax.rsqrt(square / (2 * count) + 1e-05)
    normal_part = (values - mean) * inverse
    return (normal_part * gain_row + bias_row, (normal_part, inverse))


def split_norm_back(place, gradient, cached, gain_row):
    normal_part, inverse = cached
    count = gradient.shape[-1]
    scaled = gradient * gain_row
    sums = jnp.concatenate(
        [
            jnp.sum(scaled, axis=-1, keepdims=True),
            jnp.sum(scaled * normal_part, axis=-1, keepdims=True),
        ],
        -1,
    )
    sums = (sums + place.sibling(sums)[::-1]) / (2 * count)
    input_grad = inverse * (scaled - sums[..., :1] - normal_part * sums[..., 1:])
    return (
        input_grad,
        jnp.sum(gradient * normal_part, axis=(0, 1)),
        jnp.sum(gradient, axis=(0, 1)),
    )


def swish_slope(values):
    sigmoid_val = jax.nn.sigmoid(values)
    return sigmoid_val * (1.0 + values * (1.0 - sigmoid_val))


def skew_band(rel_scores, key_count):
    head_count, row_count, band_width = rel_scores.shape
    padded = jnp.pad(rel_scores, ((0, 0), (0, 0), (0, key_count + 1 - band_width)))
    flattened = padded.reshape(head_count, row_count * (key_count + 1))[:, : row_count * key_count]
    return flattened.reshape(head_count, row_count, key_count)


def unskew_band(grads, band_width):
    head_count, row_count, key_count = grads.shape
    flattened = jnp.pad(grads.reshape(head_count, row_count * key_count), ((0, 0), (0, row_count)))
    return flattened.reshape(head_count, row_count, key_count + 1)[:, :, :band_width]


def dot(left, right, left_axis, right_axis):
    return lax.dot_general(
        left, right, (((left_axis,), (right_axis,)), ((), ())), preferred_element_type=F32
    )


def band_scores(query_heads, key_heads, relative, allowed):
    content = jnp.einsum("hid,hjd->hij", query_heads, key_heads, preferred_element_type=F32)
    positional = jnp.einsum("hid,rd->hir", query_heads, relative, preferred_element_type=F32)
    scores = (content + skew_band(positional, key_heads.shape[1])) * HEAD_DIM ** (-0.5)
    return jnp.where(allowed, scores, -1e30)


def local(
    inputs,
    lengths,
    ffn_in,
    ffn_out,
    qkv_weight,
    out_weight,
    conv_in,
    conv_depth,
    conv_out,
    norm_gain,
    norm_bias,
    rel_key,
    cotangent,
):
    place = Place()
    seq_size, chips, half = place.seq_size, place.chips, place.half
    core = place.core
    row_count, dim = inputs.shape[1:]
    hid = ffn_in.shape[3] // 2
    quarter = hid // 2
    width = dim // 2
    rows = 2 * ffn_in.shape[2]
    margin = KERNEL - 1
    key_count = row_count + LEFT + RIGHT
    scale = HEAD_DIM ** (-0.5)
    tap_first, tap_last = 12, 12 + KERNEL

    small = jnp.concatenate([norm_gain[0], norm_bias[0], conv_depth[0]], 0)
    small_count = small.shape[0]
    small = jnp.pad(small, ((0, 128 - small_count), (0, 0))).T
    out_rows = jnp.swapaxes(ffn_out[0], 1, 2)

    def halves(which):
        qkv3 = qkv_weight[0].reshape(-1, 3, dim)
        conv2 = conv_in[0].reshape(-1, 2, dim)
        pick = lambda array: place.core_part(array, array.ndim - 1, which)
        flat = lambda array: array.reshape(array.shape[0], -1)
        return [
            pick(ffn_in[0, 0]),
            pick(out_rows[0]),
            flat(pick(qkv3)),
            flat(pick(conv2)),
            pick(ffn_in[0, 1]),
            pick(out_rows[1]),
        ]

    sent_parts = halves(1 - core) + [out_weight[0], conv_out[0], small]
    kept_parts = halves(core) + [out_weight[0], conv_out[0], small]
    received = place.sibling(jnp.concatenate(sent_parts, 1))
    block_parts, start = [], 0
    for kept in kept_parts:
        stop = start + kept.shape[1]
        block_parts.append(place.by_core(kept, received[:, start:stop], 0))
        start = stop
    b_in0, b_down0, b_qkv, b_first, b_in1, b_down1, b_out, b_second, b_small = block_parts

    chunks = [
        ([b_in0[:, :quarter], b_small], [b_down0[:, :quarter]], ()),
        ([b_in0[:, quarter:]], [b_down0[:, quarter:]], ()),
        ([b_qkv], [b_first], (b_out, b_second)),
        ([b_in1[:, :quarter]], [b_down1[:, :quarter]], ()),
        ([b_in1[:, quarter:]], [b_down1[:, quarter:]], ()),
    ]
    gathered, z_mark, hop_marks = [], None, []
    for index, (left, right, wide) in enumerate(chunks):
        block = jnp.concatenate(list(left) + list(right) + list(wide), 1)
        waits = [z_mark]
        if index >= 2:
            waits += hop_marks[index - 2][0::place.bits]
        if index >= 3:
            waits += hop_marks[index - 3]
        block = tie(block, *waits)
        spread = place.swap_seq(jnp.broadcast_to(block[None], (seq_size,) + block.shape))
        z_mark = tip(spread)
        marks = []
        n_left = sum(part.shape[1] for part in left)
        n_right = sum(part.shape[1] for part in right)
        left_part, right_part = spread[..., :n_left], spread[..., n_left : n_left + n_right]
        if wide:
            chosen = lax.dynamic_slice_in_dim(spread[..., n_left + n_right :], core * half, half, 0)
            w0, w1 = chosen[..., :dim], chosen[..., dim:]
            left_part = jnp.concatenate([left_part, wide_to_seq(w0, half)], -1)
            right_part = jnp.concatenate([right_part, wide_to_seq(w1, half)], -1)
        left_full = gather_plane(place, left_part, 0, marks)
        right_full = gather_plane(place, right_part, 1, marks)
        hop_marks.append(marks)
        gathered.append((left_full, right_full))

    def as_rows(full):
        return full.reshape(-1, full.shape[-1])

    w_in = [[None, None], [None, None]]
    w_down = [[None, None], [None, None]]
    for net, base in ((0, 0), (1, 3)):
        for part in range(2):
            w_in[net][part] = as_rows(gathered[base + part][0][..., :quarter])
            w_down[net][part] = as_rows(gathered[base + part][1])
    small_all = as_rows(gathered[0][0][..., quarter:])[:, :small_count].T.astype(F32)
    n_qkv, n_first = b_qkv.shape[1], b_first.shape[1]
    w_qkv = as_rows(gathered[2][0][..., :n_qkv])
    w_out = as_rows(seq_to_wide(gathered[2][0][..., n_qkv:], half))
    w_first = as_rows(gathered[2][1][..., :n_first])
    w_second = as_rows(seq_to_wide(gathered[2][1][..., n_first:], half))
    gains, biases = small_all[:6], small_all[6:12]
    tap_values = place.core_part(small_all[tap_first:tap_last], 1, core)
    gain3 = place.core_part(gains[3], 0, core)
    bias3 = place.core_part(biases[3], 0, core)

    group_lengths = jnp.concatenate([lengths, place.sibling(lengths)], 0)
    clips = group_lengths.shape[1]
    order = jnp.arange(clips)
    clip_ends = jnp.sum(
        jnp.where(order[None, :, None] >= order[None, None, :], group_lengths[:, None, :], 0), axis=2
    )
    first_row = place.seq * row_count

    def clip_of(offset, count_rows):
        positions = first_row + offset + jnp.arange(count_rows, dtype=jnp.int32)
        inside = jnp.sum(
            (positions[None, :, None] >= clip_ends[:, None, :]).astype(jnp.int32), axis=2
        )
        return jnp.where(positions[None] < 0, -1, inside)

    own_ids = clip_of(0, row_count)
    key_ids = clip_of(-LEFT, key_count)
    conv_ids = clip_of(-margin, row_count + margin)
    offsets = jnp.arange(key_count)[None, :] - jnp.arange(row_count)[:, None]
    allowed = ((offsets >= 0) & (offsets <= LEFT + RIGHT))[None] & (
        own_ids[:, :, None] == key_ids[:, None, :]
    )
    heads = width // HEAD_DIM
    allowed = jnp.broadcast_to(allowed[:, None], (2, heads, row_count, key_count)).reshape(
        2 * heads, row_count, key_count
    )
    tap_masks = [
        (conv_ids[:, tap : tap + row_count] == own_ids)[:, :, None] for tap in range(KERNEL)
    ]

    def to_heads(array):
        count = array.shape[1]
        return (
            array.reshape(2, count, heads, HEAD_DIM)
            .transpose(0, 2, 1, 3)
            .reshape(2 * heads, count, HEAD_DIM)
        )

    def from_heads(array):
        count = array.shape[1]
        return (
            array.reshape(2, heads, count, HEAD_DIM)
            .transpose(0, 2, 1, 3)
            .reshape(2, count, heads * HEAD_DIM)
        )

    def flat2(array):
        return array.reshape(2 * row_count, -1)

    def pair2(array):
        return array.reshape(2, row_count, -1)

    def feed_forward(values, net, norm_index):
        normed, norm_cache = layer_norm(values, gains[norm_index], biases[norm_index])
        normed_low = flat2(place.both(normed.astype(BF)))
        pres, acts, branch = [], [], 0.0
        for part in range(2):
            pre_act = dot(normed_low, w_in[net][part], 1, 0)
            act_low = (pre_act * jax.nn.sigmoid(pre_act)).astype(BF)
            branch = branch + dot(act_low, w_down[net][part], 1, 1)
            pres.append(pre_act)
            acts.append(act_low)
        total = place.mine_of(pair2(branch))
        return (values + 0.5 * total, (norm_cache, normed_low, pres, acts))

    stream = inputs[0].astype(F32)
    after_ffn, ffn_first = feed_forward(stream, 0, 0)
    normed, attn_norm = layer_norm(after_ffn, gains[1], biases[1])
    attn_input = flat2(place.both(normed.astype(BF)))
    projected = pair2(dot(attn_input, w_qkv, 1, 0).astype(BF))
    key_values = projected[..., width:]
    from_left = place.along(key_values[:, row_count - LEFT :], 1)
    from_right = place.along(key_values[:, :RIGHT], -1)
    window_kv = jnp.concatenate([from_left, key_values, from_right], axis=1)
    query_heads = to_heads(projected[..., :width])
    key_heads = to_heads(window_kv[..., :width])
    value_heads = to_heads(window_kv[..., width:])
    relative = rel_key[0]
    masked = band_scores(query_heads, key_heads, relative, allowed)
    highest = jnp.max(masked, axis=-1, keepdims=True)
    expanded = jnp.exp(masked - highest)
    summed = jnp.sum(expanded, axis=-1, keepdims=True)
    log_total = highest + jnp.log(summed)
    probs_low = (expanded / summed).astype(BF)
    attended = from_heads(
        jnp.einsum("hij,hjd->hid", probs_low, value_heads, preferred_element_type=F32).astype(BF)
    )
    attended = flat2(attended)
    after_attn = after_ffn + place.mine_of(pair2(dot(attended, w_out, 1, 0)))
    normed, conv_norm = layer_norm(after_attn, gains[2], biases[2])
    conv_input = flat2(place.both(normed.astype(BF)))
    spread_pre = pair2(dot(conv_input, w_first, 1, 0))
    value_part, gate_sig = spread_pre[..., :width], jax.nn.sigmoid(spread_pre[..., width:])
    gated_low = (value_part * gate_sig).astype(BF)
    from_prev = place.along(gated_low[:, row_count - margin :], 1)
    extended = jnp.concatenate([from_prev, gated_low], axis=1)
    filtered = jnp.zeros((2, row_count, width), F32)
    for tap in range(KERNEL):
        filtered = (
            filtered
            + jnp.where(tap_masks[tap], extended[:, tap : tap + row_count], 0) * tap_values[tap]
        )
    normed_conv, depth_norm = split_layer_norm(place, filtered, gain3, bias3)
    swished = (normed_conv * jax.nn.sigmoid(normed_conv)).astype(BF)
    after_conv = after_attn + place.mine_of(pair2(dot(flat2(swished), w_second, 1, 0)))
    fourth, ffn_second = feed_forward(after_conv, 1, 4)
    result, final_norm = layer_norm(fourth, gains[5], biases[5])
    outputs = result.astype(BF)[None]

    reduced, first_mark, second_marks = [], None, []

    def blocks_of(array):
        return array.reshape(seq_size, chips, rows, array.shape[1])

    def wide_blocks_of(array):
        return wide_to_seq(array.reshape(half, chips, rows, array.shape[1]), half)

    def scatter(left, right, wide_left, wide_right):
        nonlocal first_mark
        index = len(second_marks)
        outs, marks = [], []
        for turn, (plain, wide) in enumerate(((left, wide_left), (right, wide_right))):
            parts = [blocks_of(array) for array in plain] + [wide_blocks_of(array) for array in wide]
            full = jnp.concatenate(parts, -1) if len(parts) > 1 else parts[0]
            full = tie(full, first_mark, second_marks[index - 2] if index >= 2 else None)
            outs.append(scatter_plane(place, full, turn, marks))
        first_mark = marks[0]
        second_marks.append(marks[place.bits - 1])
        to_swap, splits = [], []
        for part, plain, wide in ((outs[0], left, wide_left), (outs[1], right, wide_right)):
            n_plain = sum(array.shape[1] for array in plain)
            if n_plain:
                to_swap.append(part[..., :n_plain])
                splits += [array.shape[1] for array in plain]
            if wide:
                chosen = seq_to_wide(part[..., n_plain:], half)
                placed = jnp.zeros((seq_size,) + chosen.shape[1:], BF)
                to_swap.append(lax.dynamic_update_slice_in_dim(placed, chosen, core * half, 0))
                splits += [array.shape[1] for array in wide]
        swapped = place.swap_seq(jnp.concatenate(to_swap, -1))
        total = jnp.sum(swapped.astype(F32), 0)
        results, start = [], 0
        for n in splits:
            results.append(total[:, start : start + n])
            start += n
        return results

    grad_stream = cotangent[0].astype(F32)
    gain_grads = [None] * 6
    bias_grads = [None] * 6

    def feed_back(gradient, net, norm_index, cached):
        norm_cache, normed_low, pres, acts = cached
        branch_grad = flat2(place.both((0.5 * gradient).astype(BF)))
        downs, ins, normed_grad = [], [], 0.0
        for part in range(2):
            downs.append(dot(branch_grad, acts[part], 0, 0).astype(BF))
        pre_grads = []
        for part in range(2):
            act_grad = dot(branch_grad, w_down[net][part], 1, 0)
            pre_grads.append((act_grad * swish_slope(pres[part])).astype(BF))
        for part in range(2):
            normed_grad = normed_grad + dot(pre_grads[part], w_in[net][part], 1, 1)
        for part in range(2):
            ins.append(dot(normed_low, pre_grads[part], 0, 0).astype(BF))
        normed_grad = place.mine_of(pair2(normed_grad))
        input_grad, gain_grad, bias_grad = norm_back(normed_grad, norm_cache, gains[norm_index])
        reduced_down = scatter([downs[0]], [downs[1]], [], [])
        reduced_in = scatter([ins[0]], [ins[1]], [], [])
        return (
            gradient + input_grad,
            jnp.concatenate(reduced_in, 1),
            jnp.concatenate(reduced_down, 1),
            gain_grad,
            bias_grad,
        )

    grad_fourth, gain_grads[5], bias_grads[5] = norm_back(grad_stream, final_norm, gains[5])
    grad_conv_out, in_second, down_second, gain_grads[4], bias_grads[4] = feed_back(
        grad_fourth, 1, 4, ffn_second
    )
    branch_grad = flat2(place.both(grad_conv_out.astype(BF)))
    second_grad = dot(flat2(swished), branch_grad, 0, 0).astype(BF)
    swish_grad = pair2(dot(branch_grad, w_second, 1, 1))
    filter_grad, gain3_grad, bias3_grad = split_norm_back(
        place, swish_grad * swish_slope(normed_conv), depth_norm, gain3
    )
    tap_grads = []
    extended_grad = jnp.zeros((2, row_count + margin, width), F32)
    for tap in range(KERNEL):
        masked_grad = jnp.where(tap_masks[tap], filter_grad, 0.0)
        tap_grads.append(
            jnp.sum(masked_grad * extended[:, tap : tap + row_count], axis=(0, 1))
        )
        extended_grad = extended_grad + jnp.pad(
            masked_grad * tap_values[tap], ((0, 0), (tap, margin - tap), (0, 0))
        )
    to_prev = place.along(extended_grad[:, :margin].astype(BF), -1).astype(F32)
    gated_grad = extended_grad[:, margin:] + jnp.pad(
        to_prev, ((0, 0), (row_count - margin, 0), (0, 0))
    )
    spread_grad = flat2(
        jnp.concatenate(
            [gated_grad * gate_sig, gated_grad * value_part * gate_sig * (1.0 - gate_sig)], axis=2
        ).astype(BF)
    )
    first_grad = dot(conv_input, spread_grad, 0, 0).astype(BF)
    normed_grad = place.mine_of(pair2(dot(spread_grad, w_first, 1, 1)))
    input_grad, gain_grads[2], bias_grads[2] = norm_back(normed_grad, conv_norm, gains[2])
    first_sum, second_sum = scatter([first_grad], [], [], [second_grad])
    grad_attn_out = grad_conv_out + input_grad
    branch_grad = flat2(place.both(grad_attn_out.astype(BF)))
    out_grad = dot(attended, branch_grad, 0, 0).astype(BF)
    attended_grad = to_heads(pair2(dot(branch_grad, w_out, 1, 1).astype(BF)))
    probs = jnp.exp(band_scores(query_heads, key_heads, relative, allowed) - log_total)
    backward_probs_low = probs.astype(BF)
    prob_grads = jnp.einsum("hid,hjd->hij", attended_grad, value_heads, preferred_element_type=F32)
    score_grads = (
        probs * (prob_grads - jnp.sum(prob_grads * probs, axis=-1, keepdims=True))
    ).astype(BF)
    band_grads = unskew_band(score_grads, LEFT + RIGHT + 1)
    query_grad = (
        jnp.einsum("hij,hjd->hid", score_grads, key_heads, preferred_element_type=F32)
        + jnp.einsum("hir,rd->hid", band_grads, relative, preferred_element_type=F32)
    ) * scale
    relative_grad = (
        jnp.einsum("hir,hid->rd", band_grads, query_heads, preferred_element_type=F32) * scale
    )
    key_grad = (
        jnp.einsum("hij,hid->hjd", score_grads, query_heads, preferred_element_type=F32) * scale
    )
    value_grad = jnp.einsum(
        "hij,hid->hjd", backward_probs_low, attended_grad, preferred_element_type=F32
    )
    window_grad = jnp.concatenate([from_heads(key_grad), from_heads(value_grad)], axis=2)
    to_left = place.along(window_grad[:, :LEFT].astype(BF), -1).astype(F32)
    to_right = place.along(window_grad[:, LEFT + row_count :].astype(BF), 1).astype(F32)
    own_grad = (
        window_grad[:, LEFT : LEFT + row_count]
        + jnp.pad(to_left, ((0, 0), (row_count - LEFT, 0), (0, 0)))
        + jnp.pad(to_right, ((0, 0), (0, row_count - RIGHT), (0, 0)))
    )
    projected_grad = flat2(jnp.concatenate([from_heads(query_grad), own_grad], axis=2).astype(BF))
    qkv_grad = dot(attn_input, projected_grad, 0, 0).astype(BF)
    normed_grad = place.mine_of(pair2(dot(projected_grad, w_qkv, 1, 1)))
    input_grad, gain_grads[1], bias_grads[1] = norm_back(normed_grad, attn_norm, gains[1])
    qkv_a, qkv_b, out_sum = scatter(
        [qkv_grad[:, : 2 * width]], [qkv_grad[:, 2 * width :]], [], [out_grad]
    )
    grad_ffn_out = grad_attn_out + input_grad
    grad_input, in_first, down_first, gain_grads[0], bias_grads[0] = feed_back(
        grad_ffn_out, 0, 0, ffn_first
    )

    def spread_core(half_rows):
        return place.by_core(half_rows, jnp.zeros_like(half_rows), 1)

    gain_grads[3] = spread_core(gain3_grad[None])[0]
    bias_grads[3] = spread_core(bias3_grad[None])[0]
    small_grads = jnp.concatenate(
        [jnp.stack(gain_grads), jnp.stack(bias_grads), spread_core(jnp.stack(tap_grads))], 0
    )
    small_grads = jnp.pad(small_grads, ((0, 128 - small_count), (0, 0))).T
    small_full = small_grads.reshape((seq_size,) + (2,) * place.bits + (rows, 128))
    for bit in range(place.bits):
        axis = place.bits - bit
        me = place.bit(bit)
        keep = lax.dynamic_slice_in_dim(small_full, me, 1, axis)
        sent = lax.dynamic_slice_in_dim(small_full, 1 - me, 1, axis)
        small_full = keep + place.hop(sent, bit)
    small_total = jnp.sum(place.swap_seq(small_full.reshape(seq_size, rows, 128)), 0)
    small_sum = place.core_part(small_total, 0, core) + place.sibling(
        place.core_part(small_total, 0, 1 - core)
    )
    small_sum = small_sum[:, :small_count].T

    rel_total = relative_grad + place.sibling(relative_grad)
    for bit in range(place.bits):
        rel_total = rel_total + place.hop(rel_total, bit)
    rel_total = jnp.sum(
        place.swap_seq(jnp.broadcast_to(rel_total[None], (seq_size,) + rel_total.shape)), 0
    )

    def own_rows(total):
        other = place.sibling(place.core_part(total, 0, 1 - core))
        return place.core_part(total, 0, core), other

    def join(total, count):
        mine, other = own_rows(total)
        n = mine.shape[1] // count
        mine = mine.reshape(-1, count, n)
        other = other.reshape(-1, count, n)
        return place.by_core(mine, other, 2).reshape(mine.shape[0], -1)

    def owner_rows(total):
        mine, other = own_rows(total)
        return jnp.where(lax.div(place.seq, half) == core, mine, other)

    ffn_in_grad = jnp.stack([join(in_first, 1), join(in_second, 1)])
    ffn_out_grad = jnp.swapaxes(jnp.stack([join(down_first, 1), join(down_second, 1)]), 1, 2)
    return (
        outputs,
        grad_input[None],
        ffn_in_grad[None],
        ffn_out_grad[None],
        join(jnp.concatenate([qkv_a, qkv_b], 1), 3)[None],
        owner_rows(out_sum)[None],
        join(first_sum, 2)[None],
        small_sum[None, tap_first:tap_last],
        owner_rows(second_sum)[None],
        small_sum[None, :6],
        small_sum[None, 6:12],
        rel_total[None],
    )


def solution(mesh):
    spread = ("seq", "fsdp")
    split_rows = P(None, spread, None)
    split_last = P(None, None, spread)
    placed = (
        P("fsdp", "seq", None),
        P("fsdp", None),
        P(None, None, spread, None),
        P(None, None, None, spread),
        split_rows,
        split_rows,
        split_rows,
        split_last,
        split_rows,
        split_last,
        split_last,
        P(),
        P("fsdp", "seq", None),
    )
    return jax.shard_map(
        local,
        mesh=mesh,
        in_specs=placed,
        out_specs=(
            P("fsdp", "seq", None),
            P("fsdp", "seq", None),
            P(None, None, spread, None),
            P(None, None, None, spread),
            split_rows,
            split_rows,
            split_rows,
            split_last,
            split_rows,
            split_last,
            split_last,
            P(),
        ),
        check_vma=False,
    )
```

time: 2440 us -> 896 us (0.37)
  waiting for transfers between devices: 1700 us -> 242 us
  blocking collectives: 168 us -> 0 us
  starting transfers between devices: 19.2 us -> 142 us
  other arithmetic: 93.5 us -> 178 us
  local copies, waits for them, and re-layouts: 291 us -> 211 us
  matrix products: 144 us -> 78.6 us
    reduce_scatter x5 -> x0, waiting for transfers between devices: 942 us -> none  [the longest x1 356 us: local(): lax.psum_scatter(grad_in_w, ('seq', 'fsdp'), scatter_dimension=1, tiled=T...]
    unnamed x19 -> x0, waiting for transfers between devices: 641 us -> none
    ppermute x6 -> x84, waiting for transfers between devices: 11.6 us -> 177 us  [the longest x48 168 us: hop(): lax.ppermute(shard, 'fsdp', [(i, i ^ 2 << bit) for i in range(self.fsdp_s...]
    all_gather x3 -> x0, blocking collectives: 127 us -> none  [the longest x1 46.3 us: local(): lax.all_gather(conv_depth[layer_index], ('seq', 'fsdp'), axis=1, tiled=True)]
    all_gather x6 -> x0, waiting for transfers between devices: 103 us -> none  [the longest x1 59.8 us: local(): lax.all_gather(conv_in[layer_index], ('seq', 'fsdp'), axis=0, tiled=True)]
    slice x15 -> x74, local copies, waits for them, and re-layouts: 127 us -> 39 us  [the longest x23 21.9 us: tip(): return array[(0,) * array.ndim]]
    dot_general x33 -> x44, matrix products: 144 us -> 76.8 us  [the longest x36 58.6 us: dot(): lax.dot_general(left, right, (((left_axis,), (right_axis,)), ((), ())), p...]
    all_to_all x0 -> x13, waiting for transfers between devices: none -> 65.3 us  [swap_seq(): return lax.all_to_all(blocks, 'seq', 0, 0, tiled=True)]
  transfers between devices with their start and end apart: 21 -> 97, of which waited for: 13 -> 28; matrix products, arithmetic and copies ran while one was open for 19% -> 47% of each run, Pallas kernels for 0% -> 0%
where the time goes in v1:
time: 896 us; the launch traced here: 887 us
  waiting for transfers between devices  242 us (27%)
  local copies, waits for them, and re-layouts  211 us (24%)
  other arithmetic  178 us (20%)
  starting transfers between devices  142 us (16%)
  matrix products  78.6 us (9%)
  between operations  35.7 us (4%)
    ppermute x48, waiting for transfers between devices, hop(): lax.ppermute(shard, 'fsdp', [(i, i ^ 2 << bit) for i in range(self.fsdp_s...  168 us
    all_to_all x13, waiting for transfers between devices, swap_seq(): return lax.all_to_all(blocks, 'seq', 0, 0, tiled=True)  65.3 us
    all_to_all x13, starting transfers between devices, swap_seq(): return lax.all_to_all(blocks, 'seq', 0, 0, tiled=True)  61.8 us
    dot_general x36, matrix products, dot(): lax.dot_general(left, right, (((left_axis,), (right_axis,)), ((), ())), p...  58.6 us
    ppermute x48, starting transfers between devices, hop(): lax.ppermute(shard, 'fsdp', [(i, i ^ 2 << bit) for i in range(self.fsdp_s...  57.7 us
    unnamed x528, local copies, waits for them, and re-layouts  47.1 us
    select_n x20, other arithmetic, gather_plane(): jnp.where(place.bit(bit) == 0, jnp.concatenate([current, other], axis), j...  38.4 us
    slice x23, local copies, waits for them, and re-layouts, tip(): return array[(0,) * array.ndim]  21.9 us
  transfers between devices with their start and end apart: 97, of which 28 were waited for; matrix products, arithmetic and copies ran while one was open for 47% of the time, Pallas kernels for 0%

profile of v1, /device:TPU:0, one launch (start us, length us, event | category | flops | bytes accessed | tf_op | source)
XLA Modules:
  0.0 887.2 jit_solution(12216140108562301408)
XLA Ops:
  19.2 6.2 all-to-all-start
  29.2 23.6 %all-to-all-done = bf16[4,64,2176]{2,1,0:T(8,128)(2,1)S(1)} async-done(((bf16[4,64,2176]{2,1,0:T(8,128)(2,1)}), bf16[4,64,2176]{2,1,0:T(8,128)(2,1)S(1)}, u32[]{:S(2)}, u32[]{:S(2)}) %all-to-all-start) | async-done | bytes 1114144 | tf_op jit(solution)/shard_map/all_to_all | solution.py:37
  63.7 10.1 %collective-permute-done.1 = bf16[4,1,1,64,1152]{4,3,0,2,1:T(8,128)(2,1)S(1)} collective-permute-done((bf16[4,1,1,64,1152]{4,3,0,2,1:T(8,128)(2,1)S(1)}, bf16[4,1,1,64,1152]{4,3,0,2,1:T(8,128)(2,1)S(1)}, u32[]{:S(2)}, u32[]{:S(2)}) %collective-permute-start.1) | collective-permute-done | bytes 589856 | tf_op jit(solution)/shard_map/ppermute | solution.py:30
  96.3 8.0 collective-permute-done.2
  123.9 14.8 %collective-permute-done.9 = bf16[4,2,1,64,1024]{4,3,0,2,1:T(8,128)(2,1)S(1)} collective-permute-done((bf16[4,2,1,64,1024]{4,3,0,2,1:T(8,128)(2,1)S(1)}, bf16[4,2,1,64,1024]{4,3,0,2,1:T(8,128)(2,1)S(1)}, u32[]{:S(2)}, u32[]{:S(2)}) %collective-permute-start.9) | collective-permute-done | bytes 1048608 | tf_op jit(solution)/shard_map/ppermute | solution.py:30
  178.8 4.8 all-to-all-start.3
  191.9 17.9 %all-to-all-done.3 = bf16[4,64,2048]{2,1,0:T(8,128)(2,1)S(1)} async-done(((bf16[4,64,2048]{2,1,0:T(8,128)(2,1)}), bf16[4,64,2048]{2,1,0:T(8,128)(2,1)S(1)}, u32[]{:S(2)}, u32[]{:S(2)}) %all-to-all-start.3) | async-done | bytes 1048608 | tf_op jit(solution)/shard_map/all_to_all | solution.py:37
  214.3 38.5 %collective-permute-done.19 = bf16[4,1,1,64,1536]{4,3,0,2,1:T(8,128)(2,1)} collective-permute-done((bf16[4,1,1,64,1536]{4,3,0,2,1:T(8,128)(2,1)S(1)}, bf16[4,1,1,64,1536]{4,3,0,2,1:T(8,128)(2,1)}, u32[]{:S(2)}, u32[]{:S(2)}) %collective-permute-start.19) | collective-permute-done | bytes 786464 | tf_op jit(solution)/shard_map/ppermute | solution.py:30
  266.6 5.1 all-to-all-start.4
  292.8 5.4 collective-permute-start.15
  304.5 4.9 pad.169.clone
  309.4 6.5 reshape.1887
  316.0 5.2 slice.1102
  321.1 9.8 %reshape.1888 = f32[16,256,328]{2,1,0:T(8,128)} reshape(f32[16,83968]{1,0:T(8,128)} %slice.1102) | data formatting | bytes 10747904 | tf_op jit(solution)/shard_map/reshape | solution.py:174
  330.9 6.3 copy.249
  371.6 9.3 %fusion.159 = (f32[2,256]{1,0:T(2,128)S(1)}, f32[2,256,512]{2,1,0:T(8,128)S(1)}) fusion(f32[512]{0:T(512)S(1)} %copy-done.173, bf16[2,256,512]{2,1,0:T(8,128)(2,1)S(1)} %multiply_convert_fusion.14, pred[2,256]{1,0:T(4,128)(4,1)} %get-tuple-element.296, f32[512]{0:T(512)S(1)} %copy-done.171, bf16[2,30,512]{2,1,0:T(8,128)(2,1)S(1)} %collective-permute-done.21, ...), kind=kLoop, calls=%fused_computation.674 | loop fusion | flops 63962624 | bytes 1715712 | tf_op jit(solution)/shard_map/reduce_sum | solution.py:133
  396.8 22.4 %collective-permute-done.30 = bf16[4,1,2,64,1024]{4,3,0,2,1:T(8,128)(2,1)S(1)} collective-permute-done((bf16[4,1,2,64,1024]{4,3,0,2,1:T(8,128)(2,1)S(1)}, bf16[4,1,2,64,1024]{4,3,0,2,1:T(8,128)(2,1)S(1)}, u32[]{:S(2)}, u32[]{:S(2)}) %collective-permute-start.30) | collective-permute-done | bytes 1048608 | tf_op jit(solution)/shard_map/ppermute | solution.py:30
  453.6 20.3 %collective-permute-done.46 = bf16[4,2,1,64,1024]{4,3,2,1,0:T(8,128)(2,1)S(1)} collective-permute-done((bf16[4,2,1,64,1024]{4,3,2,1,0:T(8,128)(2,1)S(1)}, bf16[4,2,1,64,1024]{4,3,2,1,0:T(8,128)(2,1)S(1)}, u32[]{:S(2)}, u32[]{:S(2)}) %collective-permute-start.46) | collective-permute-done | bytes 1048608 | tf_op jit(solution)/shard_map/ppermute | solution.py:30
  512.6 8.3 pad_add_fusion
  559.1 4.8 fusion.3
  574.1 7.7 reshape.1901
  585.3 10.1 %reshape.1902 = bf16[16,256,329]{2,1,0:T(8,128)(2,1)} reshape(bf16[16,84224]{1,0:T(8,128)(2,1)} %pad.203) | data formatting | bytes 5390336 | tf_op jit(solution)/shard_map/reshape | solution.py:180
  634.4 5.2 all-to-all-start.8
  658.1 9.8 %collective-permute-done.75 = bf16[4,1,1,64,512]{4,3,2,1,0:T(8,128)(2,1)S(1)} collective-permute-done((bf16[4,1,1,64,512]{4,3,2,1,0:T(8,128)(2,1)S(1)}, bf16[4,1,1,64,512]{4,3,2,1,0:T(8,128)(2,1)S(1)}, u32[]{:S(2)}, u32[]{:S(2)}) %collective-permute-start.75) | collective-permute-done | bytes 262176 | tf_op jit(solution)/shard_map/ppermute | solution.py:30
  671.0 5.3 all-to-all-start.6
  736.6 4.9 all-to-all-start.11
  747.4 4.9 all-to-all-start.10
  764.8 12.2 %collective-permute-done.64 = bf16[4,1,2,64,1024]{4,3,0,2,1:T(8,128)(2,1)} collective-permute-done((bf16[4,1,2,64,1024]{4,3,0,2,1:T(8,128)(2,1)}, bf16[4,1,2,64,1024]{4,3,0,2,1:T(8,128)(2,1)}, u32[]{:S(2)}, u32[]{:S(2)}) %collective-permute-start.64) | collective-permute-done | bytes 1048608 | tf_op jit(solution)/shard_map/ppermute | solution.py:30
  780.0 5.0 all-to-all-start.9
  809.6 18.2 %collective-permute-done.63 = bf16[4,1,1,64,1024]{4,3,0,2,1:T(8,128)(2,1)} collective-permute-done((bf16[4,1,1,64,1024]{4,3,0,2,1:T(8,128)(2,1)}, bf16[4,1,1,64,1024]{4,3,0,2,1:T(8,128)(2,1)}, u32[]{:S(2)}, u32[]{:S(2)}) %collective-permute-start.63) | collective-permute-done | bytes 524320 | tf_op jit(solution)/shard_map/ppermute | solution.py:30
  831.9 4.8 all-to-all-start.7
  866.3 17.8 %all-to-all-done.5 = bf16[4,64,2048]{2,1,0:T(8,128)(2,1)S(1)} async-done(((bf16[4,64,2048]{2,1,0:T(8,128)(2,1)}), bf16[4,64,2048]{2,1,0:T(8,128)(2,1)S(1)}, u32[]{:S(2)}, u32[]{:S(2)}) %all-to-all-start.5) | async-done | bytes 1048608 | tf_op jit(solution)/shard_map/all_to_all | solution.py:37
  (1115 shorter events, 513.4 us)
Async XLA Ops:
  19.2 33.6 %all-to-all-start = ((bf16[4,64,2176]{2,1,0:T(8,128)(2,1)}), bf16[4,64,2176]{2,1,0:T(8,128)(2,1)S(1)}, u32[]{:S(2)}, u32[]{:S(2)}) async-start(bf16[4,64,2176]{2,1,0:T(8,128)(2,1)} %broadcast_in_dim.552), calls=%async_computation | async-start | bytes 2228224 | tf_op jit(solution)/shard_map/all_to_all | solution.py:37
  80.3 39.0 %collective-permute-start.5 = (bf16[4,2,1,64,1024]{4,3,2,1,0:T(8,128)(2,1)}, bf16[4,2,1,64,1024]{4,3,2,1,0:T(8,128)(2,1)}, u32[]{:S(2)}, u32[]{:S(2)}) collective-permute-start(bf16[4,2,1,64,1024]{4,3,2,1,0:T(8,128)(2,1)} %maximum_select_fusion.14), channel_id=1, source_target_pairs={{0,2},{1,3},{2,0},{3,1},{4,6},{5,7},{6,4},{7,5},{8,10},{9,11},{10,... | collective-permute-start | bytes 3145736 | tf_op jit(solution)/shard_map/ppermute | solution.py:30
  92.2 56.4 %all-to-all-start.2 = ((bf16[4,64,4608]{2,1,0:T(8,128)(2,1)}), bf16[4,64,4608]{2,1,0:T(8,128)(2,1)S(1)}, u32[]{:S(2)}, u32[]{:S(2)}) async-start(bf16[4,64,4608]{2,1,0:T(8,128)(2,1)} %broadcast_in_dim.563), calls=%async_computation.2 | async-start | bytes 4718592 | tf_op jit(solution)/shard_map/all_to_all | solution.py:37
  150.2 33.7 %collective-permute-start.13 = (bf16[4,1,1,64,2048]{4,3,0,2,1:T(8,128)(2,1)S(1)}, bf16[4,1,1,64,2048]{4,3,0,2,1:T(8,128)(2,1)}, u32[]{:S(2)}, u32[]{:S(2)}) collective-permute-start(bf16[4,1,1,64,2048]{4,3,0,2,1:T(8,128)(2,1)S(1)} %maximum_bitcast_fusion), channel_id=1, source_target_pairs={{0,2},{1,3},{2,0},{3,1},{4,6},{5,7},{6,4},{7,5},{8,10},{9,11},{10,... | collective-permute-start | bytes 3145736 | tf_op jit(solution)/shard_map/ppermute | solution.py:30
  187.1 91.9 %collective-permute-start.14 = (bf16[4,1,2,64,2048]{4,3,0,2,1:T(8,128)(2,1)}, bf16[4,1,2,64,2048]{4,3,0,2,1:T(8,128)(2,1)}, u32[]{:S(2)}, u32[]{:S(2)}) collective-permute-start(bf16[4,1,2,64,2048]{4,3,0,2,1:T(8,128)(2,1)} %maximum_select_fusion.6), channel_id=1, source_target_pairs={{0,4},{1,5},{2,6},{3,7},{4,0},{5,1},{6,2},{7,3},{8,12},{9,13},{10,... | collective-permute-start | bytes 6291464 | tf_op jit(solution)/shard_map/ppermute | solution.py:30
  188.8 64.0 %collective-permute-start.19 = (bf16[4,1,1,64,1536]{4,3,0,2,1:T(8,128)(2,1)S(1)}, bf16[4,1,1,64,1536]{4,3,0,2,1:T(8,128)(2,1)}, u32[]{:S(2)}, u32[]{:S(2)}) collective-permute-start(bf16[4,1,1,64,1536]{4,3,0,2,1:T(8,128)(2,1)S(1)} %maximum_bitcast_fusion.3), channel_id=1, source_target_pairs={{0,4},{1,5},{2,6},{3,7},{4,0},{5,1},{6,2},{7,3},{8,12},{9,13},{10,... | collective-permute-start | bytes 2359304 | tf_op jit(solution)/shard_map/ppermute | solution.py:30
  210.7 61.1 %collective-permute-start.27 = (bf16[4,1,1,64,1024]{4,3,2,1,0:T(8,128)(2,1)S(1)}, bf16[4,1,1,64,1024]{4,3,2,1,0:T(8,128)(2,1)}, u32[]{:S(2)}, u32[]{:S(2)}) collective-permute-start(bf16[4,1,1,64,1024]{4,3,2,1,0:T(8,128)(2,1)S(1)} %get-tuple-element.205), channel_id=1, source_target_pairs={{0,4},{1,5},{2,6},{3,7},{4,0},{5,1},{6,2},{7,3},{8,12},{9,13},{10,... | collective-permute-start | bytes 1572872 | tf_op jit(solution)/shard_map/ppermute | solution.py:30
  259.6 88.1 %collective-permute-start.20 = (bf16[4,2,1,64,1536]{4,3,0,2,1:T(8,128)(2,1)}, bf16[4,2,1,64,1536]{4,3,0,2,1:T(8,128)(2,1)}, u32[]{:S(2)}, u32[]{:S(2)}) collective-permute-start(bf16[4,2,1,64,1536]{4,3,0,2,1:T(8,128)(2,1)} %maximum_select_fusion.12), channel_id=1, source_target_pairs={{0,2},{1,3},{2,0},{3,1},{4,6},{5,7},{6,4},{7,5},{8,10},{9,11},{10,... | collective-permute-start | bytes 4718600 | tf_op jit(solution)/shard_map/ppermute | solution.py:30
  266.6 89.4 %all-to-all-start.4 = ((bf16[4,64,2048]{2,1,0:T(8,128)(2,1)}), bf16[4,64,2048]{2,1,0:T(8,128)(2,1)}, u32[]{:S(2)}, u32[]{:S(2)}) async-start(bf16[4,64,2048]{2,1,0:T(8,128)(2,1)} %broadcast_in_dim.601), calls=%async_computation.4 | async-start | bytes 2097152 | tf_op jit(solution)/shard_map/all_to_all | solution.py:37
  273.1 95.0 %collective-permute-start.28 = (bf16[4,2,1,64,1024]{4,3,2,1,0:T(8,128)(2,1)S(1)}, bf16[4,2,1,64,1024]{4,3,2,1,0:T(8,128)(2,1)}, u32[]{:S(2)}, u32[]{:S(2)}) collective-permute-start(bf16[4,2,1,64,1024]{4,3,2,1,0:T(8,128)(2,1)S(1)} %maximum_select_fusion.18), channel_id=1, source_target_pairs={{0,2},{1,3},{2,0},{3,1},{4,6},{5,7},{6,4},{7,5},{8,10},{9,11},{10,... | collective-permute-start | bytes 3145736 | tf_op jit(solution)/shard_map/ppermute | solution.py:30
  277.5 103.8 %collective-permute-start.26 = (bf16[4,1,2,64,1024]{4,3,0,2,1:T(8,128)(2,1)}, bf16[4,1,2,64,1024]{4,3,0,2,1:T(8,128)(2,1)}, u32[]{:S(2)}, u32[]{:S(2)}) collective-permute-start(bf16[4,1,2,64,1024]{4,3,0,2,1:T(8,128)(2,1)} %maximum_select_fusion.17), channel_id=1, source_target_pairs={{0,4},{1,5},{2,6},{3,7},{4,0},{5,1},{6,2},{7,3},{8,12},{9,13},{10,... | collective-permute-start | bytes 3145736 | tf_op jit(solution)/shard_map/ppermute | solution.py:30
  291.4 45.8 %collective-permute-start.16 = (bf16[2,8,1024]{1,2,0:T(8,128)(2,1)}, bf16[2,8,1024]{1,2,0:T(8,128)(2,1)}, u32[]{:S(2)}, u32[]{:S(2)}) collective-permute-start(bf16[2,8,1024]{1,2,0:T(8,128)(2,1)} %copy.304), channel_id=1, source_target_pairs={{8,0},{16,8},{24,16},{9,1},{17,9},{25,17},{10,2},{18,10},{26,18},{... | collective-permute-start | bytes 98312 | tf_op jit(solution)/shard_map/ppermute | solution.py:34
  292.8 44.4 %collective-permute-start.15 = (bf16[2,64,1024]{1,2,0:T(8,128)(2,1)}, bf16[2,64,1024]{1,2,0:T(8,128)(2,1)}, u32[]{:S(2)}, u32[]{:S(2)}) collective-permute-start(bf16[2,64,1024]{1,2,0:T(8,128)(2,1)} %copy.302), channel_id=1, source_target_pairs={{0,8},{8,16},{16,24},{1,9},{9,17},{17,25},{2,10},{10,18},{18,26},{... | collective-permute-start | bytes 786440 | tf_op jit(solution)/shard_map/ppermute | solution.py:34
  358.4 34.2 %collective-permute-start.29 = (bf16[4,1,1,64,1024]{4,3,0,2,1:T(8,128)(2,1)}, bf16[4,1,1,64,1024]{4,3,0,2,1:T(8,128)(2,1)}, u32[]{:S(2)}, u32[]{:S(2)}) collective-permute-start(bf16[4,1,1,64,1024]{4,3,0,2,1:T(8,128)(2,1)} %get-tuple-element.206), channel_id=1, source_target_pairs={{0,2},{1,3},{2,0},{3,1},{4,6},{5,7},{6,4},{7,5},{8,10},{9,11},{10,... | collective-permute-start | bytes 1572872 | tf_op jit(solution)/shard_map/ppermute | solution.py:30
  449.0 42.4 %collective-permute-start.67 = (bf16[4,1,2,64,1024]{4,3,0,2,1:T(8,128)(2,1)S(1)}, bf16[4,1,2,64,1024]{4,3,0,2,1:T(8,128)(2,1)S(1)}, u32[]{:S(2)}, u32[]{:S(2)}) collective-permute-start(bf16[4,1,2,64,1024]{4,3,0,2,1:T(8,128)(2,1)S(1)} %copy.321), channel_id=1, source_target_pairs={{0,4},{1,5},{2,6},{3,7},{4,0},{5,1},{6,2},{7,3},{8,12},{9,13},{10,... | collective-permute-start | bytes 3145736 | tf_op jit(solution)/shard_map/ppermute | solution.py:30
  482.1 49.4 %collective-permute-start.48 = (bf16[4,1,1,64,1024]{4,3,2,1,0:T(8,128)(2,1)}, bf16[4,1,1,64,1024]{4,3,2,1,0:T(8,128)(2,1)}, u32[]{:S(2)}, u32[]{:S(2)}) collective-permute-start(bf16[4,1,1,64,1024]{4,3,2,1,0:T(8,128)(2,1)} %constant_dynamic-slice_fusion.40), channel_id=1, source_target_pairs={{0,4},{1,5},{2,6},{3,7},{4,0},{5,1},{6,2},{7,3},{8,12},{9,13},{10,... | collective-permute-start | bytes 1572872 | tf_op jit(solution)/shard_map/ppermute | solution.py:30
  487.0 53.6 %collective-permute-start.47 = (bf16[4,2,1,64,1024]{4,3,2,1,0:T(8,128)(2,1)}, bf16[4,2,1,64,1024]{4,3,2,1,0:T(8,128)(2,1)}, u32[]{:S(2)}, u32[]{:S(2)}) collective-permute-start(bf16[4,2,1,64,1024]{4,3,2,1,0:T(8,128)(2,1)} %constant_dynamic-slice_fusion.41), channel_id=1, source_target_pairs={{0,2},{1,3},{2,0},{3,1},{4,6},{5,7},{6,4},{7,5},{8,10},{9,11},{10,... | collective-permute-start | bytes 3145736 | tf_op jit(solution)/shard_map/ppermute | solution.py:30
  487.9 60.9 %collective-permute-start.60 = (bf16[4,1,2,64,1024]{4,3,0,2,1:T(8,128)(2,1)}, bf16[4,1,2,64,1024]{4,3,0,2,1:T(8,128)(2,1)}, u32[]{:S(2)}, u32[]{:S(2)}) collective-permute-start(bf16[4,1,2,64,1024]{4,3,0,2,1:T(8,128)(2,1)} %copy.316), channel_id=1, source_target_pairs={{0,4},{1,5},{2,6},{3,7},{4,0},{5,1},{6,2},{7,3},{8,12},{9,13},{10,... | collective-permute-start | bytes 3145736 | tf_op jit(solution)/shard_map/ppermute | solution.py:30
  493.7 41.6 %collective-permute-start.68 = (bf16[4,1,1,64,1024]{4,3,0,2,1:T(8,128)(2,1)}, bf16[4,1,1,64,1024]{4,3,0,2,1:T(8,128)(2,1)}, u32[]{:S(2)}, u32[]{:S(2)}) collective-permute-start(bf16[4,1,1,64,1024]{4,3,0,2,1:T(8,128)(2,1)} %constant_dynamic-slice_fusion.15), channel_id=1, source_target_pairs={{0,2},{1,3},{2,0},{3,1},{4,6},{5,7},{6,4},{7,5},{8,10},{9,11},{10,... | collective-permute-start | bytes 1572872 | tf_op jit(solution)/shard_map/ppermute | solution.py:30
  545.7 106.3 %collective-permute-start.50 = (bf16[4,1,1,64,1024]{4,3,2,1,0:T(8,128)(2,1)}, bf16[4,1,1,64,1024]{4,3,2,1,0:T(8,128)(2,1)}, u32[]{:S(2)}, u32[]{:S(2)}) collective-permute-start(bf16[4,1,1,64,1024]{4,3,2,1,0:T(8,128)(2,1)} %constant_dynamic-slice_fusion.38), channel_id=1, source_target_pairs={{0,4},{1,5},{2,6},{3,7},{4,0},{5,1},{6,2},{7,3},{8,12},{9,13},{10,... | collective-permute-start | bytes 1572872 | tf_op jit(solution)/shard_map/ppermute | solution.py:30
  548.3 99.5 %collective-permute-start.74 = (bf16[4,1,2,64,512]{4,3,2,1,0:T(8,128)(2,1)}, bf16[4,1,2,64,512]{4,3,2,1,0:T(8,128)(2,1)}, u32[]{:S(2)}, u32[]{:S(2)}) collective-permute-start(bf16[4,1,2,64,512]{4,3,2,1,0:T(8,128)(2,1)} %constant_dynamic-slice_fusion.8), channel_id=1, source_target_pairs={{0,4},{1,5},{2,6},{3,7},{4,0},{5,1},{6,2},{7,3},{8,12},{9,13},{10,... | collective-permute-start | bytes 1572872 | tf_op jit(solution)/shard_map/ppermute | solution.py:30
  552.3 100.9 %collective-permute-start.61 = (bf16[4,1,1,64,1024]{4,3,0,2,1:T(8,128)(2,1)}, bf16[4,1,1,64,1024]{4,3,0,2,1:T(8,128)(2,1)}, u32[]{:S(2)}, u32[]{:S(2)}) collective-permute-start(bf16[4,1,1,64,1024]{4,3,0,2,1:T(8,128)(2,1)} %constant_dynamic-slice_fusion.25), channel_id=1, source_target_pairs={{0,2},{1,3},{2,0},{3,1},{4,6},{5,7},{6,4},{7,5},{8,10},{9,11},{10,... | collective-permute-start | bytes 1572872 | tf_op jit(solution)/shard_map/ppermute | solution.py:30
  634.4 36.6 %all-to-all-start.8 = ((bf16[4,64,2048]{2,1,0:T(8,128)(2,1)}), bf16[4,64,2048]{2,1,0:T(8,128)(2,1)}, u32[]{:S(2)}, u32[]{:S(2)}) async-start(bf16[4,64,2048]{2,1,0:T(8,128)(2,1)} %pad_maximum_fusion.18), calls=%async_computation.8 | async-start | bytes 2097152 | tf_op jit(solution)/shard_map/all_to_all | solution.py:37
  640.2 38.0 %collective-permute-start.49 = (bf16[4,2,1,64,1024]{4,3,2,1,0:T(8,128)(2,1)}, bf16[4,2,1,64,1024]{4,3,2,1,0:T(8,128)(2,1)}, u32[]{:S(2)}, u32[]{:S(2)}) collective-permute-start(bf16[4,2,1,64,1024]{4,3,2,1,0:T(8,128)(2,1)} %constant_dynamic-slice_fusion.39), channel_id=1, source_target_pairs={{0,2},{1,3},{2,0},{3,1},{4,6},{5,7},{6,4},{7,5},{8,10},{9,11},{10,... | collective-permute-start | bytes 3145736 | tf_op jit(solution)/shard_map/ppermute | solution.py:30
  671.0 41.2 %all-to-all-start.6 = ((bf16[4,64,2048]{2,1,0:T(8,128)(2,1)}), bf16[4,64,2048]{2,1,0:T(8,128)(2,1)}, u32[]{:S(2)}, u32[]{:S(2)}) async-start(bf16[4,64,2048]{2,1,0:T(8,128)(2,1)} %pad_maximum_fusion.16), calls=%async_computation.6 | async-start | bytes 2097152 | tf_op jit(solution)/shard_map/all_to_all | solution.py:37
  688.8 35.3 %collective-permute-start.70 = (bf16[4,1,2,64,1024]{4,3,0,2,1:T(8,128)(2,1)}, bf16[4,1,2,64,1024]{4,3,0,2,1:T(8,128)(2,1)}, u32[]{:S(2)}, u32[]{:S(2)}) collective-permute-start(bf16[4,1,2,64,1024]{4,3,0,2,1:T(8,128)(2,1)} %constant_dynamic-slice_fusion.13), channel_id=1, source_target_pairs={{0,4},{1,5},{2,6},{3,7},{4,0},{5,1},{6,2},{7,3},{8,12},{9,13},{10,... | collective-permute-start | bytes 3145736 | tf_op jit(solution)/shard_map/ppermute | solution.py:30
  714.6 39.0 %collective-permute-start.62 = (f32[32,2048]{1,0:T(8,128)}, f32[32,2048]{1,0:T(8,128)}, u32[]{:S(2)}, u32[]{:S(2)}) collective-permute-start(f32[32,2048]{1,0:T(8,128)} %get-tuple-element.238), channel_id=1, source_target_pairs={{0,1},{1,0},{2,3},{3,2},{4,5},{5,4},{6,7},{7,6},{8,9},{9,8},{10,11... | collective-permute-start | bytes 786440 | tf_op jit(solution)/shard_map/ppermute | solution.py:27
  746.6 40.8 %collective-permute-start.53 = (bf16[4,2,1,64,1024]{4,3,0,2,1:T(8,128)(2,1)}, bf16[4,2,1,64,1024]{4,3,0,2,1:T(8,128)(2,1)}, u32[]{:S(2)}, u32[]{:S(2)}) collective-permute-start(bf16[4,2,1,64,1024]{4,3,0,2,1:T(8,128)(2,1)} %copy.311), channel_id=1, source_target_pairs={{0,2},{1,3},{2,0},{3,1},{4,6},{5,7},{6,4},{7,5},{8,10},{9,11},{10,... | collective-permute-start | bytes 3145736 | tf_op jit(solution)/shard_map/ppermute | solution.py:30
  780.0 51.9 %all-to-all-start.9 = ((bf16[4,64,2560]{2,1,0:T(8,128)(2,1)}), bf16[4,64,2560]{2,1,0:T(8,128)(2,1)S(1)}, u32[]{:S(2)}, u32[]{:S(2)}) async-start(bf16[4,64,2560]{2,1,0:T(8,128)(2,1)} %pad_maximum_fusion.2), calls=%async_computation.9 | async-start | bytes 2621440 | tf_op jit(solution)/shard_map/all_to_all | solution.py:37
  794.8 35.5 %collective-permute-start.57 = (bf16[4,1,2,64,1024]{4,3,2,1,0:T(8,128)(2,1)}, bf16[4,1,2,64,1024]{4,3,2,1,0:T(8,128)(2,1)}, u32[]{:S(2)}, u32[]{:S(2)}) collective-permute-start(bf16[4,1,2,64,1024]{4,3,2,1,0:T(8,128)(2,1)} %constant_dynamic-slice_fusion.30), channel_id=1, source_target_pairs={{0,4},{1,5},{2,6},{3,7},{4,0},{5,1},{6,2},{7,3},{8,12},{9,13},{10,... | collective-permute-start | bytes 3145736 | tf_op jit(solution)/shard_map/ppermute | solution.py:30
  801.9 44.1 %collective-permute-start.80 = (f32[32,1024]{1,0:T(8,128)}, f32[32,1024]{1,0:T(8,128)}, u32[]{:S(2)}, u32[]{:S(2)}) collective-permute-start(f32[32,1024]{1,0:T(8,128)} %constant_dynamic-slice_fusion), channel_id=1, source_target_pairs={{0,1},{1,0},{2,3},{3,2},{4,5},{5,4},{6,7},{7,6},{8,9},{9,8},{10,11... | collective-permute-start | bytes 393224 | tf_op jit(solution)/shard_map/ppermute | solution.py:27
  805.2 33.9 %collective-permute-start.55 = (bf16[4,2,1,64,1024]{4,3,0,2,1:T(8,128)(2,1)}, bf16[4,2,1,64,1024]{4,3,0,2,1:T(8,128)(2,1)}, u32[]{:S(2)}, u32[]{:S(2)}) collective-permute-start(bf16[4,2,1,64,1024]{4,3,0,2,1:T(8,128)(2,1)} %copy.314), channel_id=1, source_target_pairs={{0,2},{1,3},{2,0},{3,1},{4,6},{5,7},{6,4},{7,5},{8,10},{9,11},{10,... | collective-permute-start | bytes 3145736 | tf_op jit(solution)/shard_map/ppermute | solution.py:30
  (315 other events, 2873.8 us)

commit v2 on v1

v2 whole, which is shorter than its diff:
```python
import functools

import jax
import jax.numpy as jnp
from jax import lax
from jax.experimental import pallas as pl
from jax.experimental.layout import Layout, with_layout_constraint
from jax.experimental.pallas import tpu as pltpu
from jax.sharding import Mesh
from jax.sharding import PartitionSpec as P

HEAD_DIM = 64
KERNEL = 31
LEFT = 64
RIGHT = 8
BLOCK = 128
SPAN = 256
EDGE = 32
BF = jnp.bfloat16
F32 = jnp.float32


class Place:
    def __init__(self):
        self.seq_size = lax.axis_size("seq")
        self.chips = lax.axis_size("plane")
        self.seq = lax.axis_index("seq")
        self.chip = lax.axis_index("plane")
        self.core = lax.axis_index("core")
        self.bits = self.chips.bit_length() - 1

    def sibling(self, shard):
        return lax.ppermute(shard, "core", [(0, 1), (1, 0)])

    def hop(self, shard, bit):
        return lax.ppermute(shard, "plane", [(i, i ^ (1 << bit)) for i in range(self.chips)])

    def along(self, shard, by):
        pairs = [(i, i + by) for i in range(self.seq_size) if 0 <= i + by < self.seq_size]
        return lax.ppermute(shard, "seq", pairs)

    def swap_seq(self, blocks):
        return lax.all_to_all(blocks, "seq", 0, 0, tiled=True)

    def bit(self, bit):
        return lax.rem(lax.div(self.chip, 1 << bit), 2)

    def both(self, mine):
        return jnp.stack([mine, self.sibling(mine)])

    def from_sibling(self, partial):
        return self.sibling(partial[1].astype(BF))

    def by_core(self, mine, other, axis):
        return jnp.where(
            self.core == 0,
            jnp.concatenate([mine, other], axis),
            jnp.concatenate([other, mine], axis),
        )

    def core_part(self, array, axis, which):
        size = array.shape[axis] // 2
        return lax.dynamic_slice_in_dim(array, which * size, size, axis)


def tie(array, *marks):
    ready = None
    for mark in marks:
        if mark is None:
            continue
        equal = mark == mark
        ready = equal if ready is None else jnp.logical_and(ready, equal)
    return array if ready is None else jnp.where(ready, array, jnp.zeros_like(array))


def tip(array):
    return array[(0,) * array.ndim]


def gather_plane(place, part, turn, marks):
    bits = place.bits
    current = part.reshape((part.shape[0],) + (1,) * bits + part.shape[1:])
    for step in range(bits):
        bit = (turn + step) % bits
        axis = bits - bit
        other = place.hop(current, bit)
        marks.append(tip(other))
        current = jnp.where(
            place.bit(bit) == 0,
            jnp.concatenate([current, other], axis),
            jnp.concatenate([other, current], axis),
        )
    return current.reshape((part.shape[0], place.chips) + part.shape[1:])


def scatter_plane(place, full, turn, marks):
    bits = place.bits
    current = full.reshape((full.shape[0],) + (2,) * bits + full.shape[2:])
    for step in range(bits):
        bit = (turn + step) % bits
        axis = bits - bit
        me = place.bit(bit)
        keep = lax.dynamic_slice_in_dim(current, me, 1, axis)
        sent = lax.dynamic_slice_in_dim(current, 1 - me, 1, axis)
        got = place.hop(sent, bit)
        marks.append(tip(got))
        current = (keep.astype(F32) + got.astype(F32)).astype(full.dtype)
    return current.reshape((full.shape[0],) + full.shape[2:])


def clip_index(positions, ends_ref, group, clips):
    inside = jnp.zeros(positions.shape, jnp.int32)
    for clip in range(clips):
        inside = inside + (positions >= ends_ref[group, clip]).astype(jnp.int32)
    return jnp.where(positions < 0, -1, inside)


def dot_nt(left, right):
    return lax.dot_general(left, right, (((1,), (1,)), ((), ())), preferred_element_type=F32)


def dot_nn(left, right):
    return lax.dot_general(left, right, (((1,), (0,)), ((), ())), preferred_element_type=F32)


def dot_tn(left, right):
    return lax.dot_general(left, right, (((0,), (0,)), ((), ())), preferred_element_type=F32)


def band_mask(ends_ref, base_ref, block, clips):
    group = pl.program_id(0)
    start = base_ref[0] + block * BLOCK
    query_at = start + lax.broadcasted_iota(jnp.int32, (BLOCK, 1), 0)
    key_at = start - LEFT + lax.broadcasted_iota(jnp.int32, (1, SPAN), 1)
    apart = lax.broadcasted_iota(jnp.int32, (BLOCK, SPAN), 1) - lax.broadcasted_iota(
        jnp.int32, (BLOCK, SPAN), 0
    )
    query_ids = clip_index(query_at, ends_ref, group, clips)
    key_ids = clip_index(key_at, ends_ref, group, clips)
    return (apart >= 0) & (apart <= LEFT + RIGHT) & (query_ids == key_ids)


def fill_window(window, left_ref, own_ref, right_ref):
    count = own_ref.shape[1]
    window[0:LEFT] = left_ref[0]
    window[LEFT : LEFT + count] = own_ref[0]
    window[LEFT + count :] = right_ref[0]


def band_probs(query, keys, relative, mask):
    scores = dot_nt(query, keys)
    positional = pltpu.roll(dot_nt(query, relative), 0, 1, stride=1, stride_axis=0)
    scores = jnp.where(mask, (scores + positional) * HEAD_DIM ** (-0.5), -1e30)
    expanded = jnp.exp(scores - jnp.max(scores, axis=1, keepdims=True))
    return expanded / jnp.sum(expanded, axis=1, keepdims=True)


def attend_kernel(
    clips, ends_ref, base_ref, q_ref, k_ref, v_ref, kl_ref, vl_ref, kr_ref, vr_ref, rel_ref,
    out_ref, probs_ref, keys, values,
):
    fill_window(keys, kl_ref, k_ref, kr_ref)
    fill_window(values, vl_ref, v_ref, vr_ref)
    low_lane = lax.broadcasted_iota(jnp.int32, (BLOCK, 2 * HEAD_DIM), 1) < HEAD_DIM
    for block in range(q_ref.shape[1] // BLOCK):
        at = block * BLOCK
        mask = band_mask(ends_ref, base_ref, block, clips)
        query = q_ref[0, at : at + BLOCK]
        zero = jnp.zeros_like(query)
        outs = []
        queries = jnp.where(low_lane, query, zero), jnp.where(low_lane, zero, query)
        for one, query_one in enumerate(queries):
            probs = band_probs(query_one, keys[at : at + SPAN], rel_ref[...], mask).astype(BF)
            probs_ref[0, 0, block, one] = probs
            outs.append(dot_nn(probs, values[at : at + SPAN]))
        out_ref[0, at : at + BLOCK] = jnp.where(low_lane, outs[0], outs[1]).astype(BF)


def attend_back_kernel(
    q_ref, k_ref, v_ref, kl_ref, vl_ref, kr_ref, vr_ref, rel_ref, do_ref, probs_ref,
    dq_ref, dk_ref, dv_ref, dkl_ref, dvl_ref, dkr_ref, dvr_ref, drel_ref,
    keys, values, key_sum, value_sum,
):
    scale = HEAD_DIM ** (-0.5)
    count = q_ref.shape[1]
    fill_window(keys, kl_ref, k_ref, kr_ref)
    fill_window(values, vl_ref, v_ref, vr_ref)
    key_sum[...] = jnp.zeros_like(key_sum)
    value_sum[...] = jnp.zeros_like(value_sum)

    @pl.when((pl.program_id(0) == 0) & (pl.program_id(1) == 0))
    def _():
        drel_ref[...] = jnp.zeros_like(drel_ref)

    low_lane = lax.broadcasted_iota(jnp.int32, (BLOCK, 2 * HEAD_DIM), 1) < HEAD_DIM
    row = lax.broadcasted_iota(jnp.int32, (BLOCK, BLOCK), 0)
    column = lax.broadcasted_iota(jnp.int32, (BLOCK, BLOCK), 1)
    flip = (row + column == BLOCK - 1).astype(F32).astype(BF)
    for block in range(count // BLOCK):
        at = block * BLOCK
        query = q_ref[0, at : at + BLOCK]
        grad = do_ref[0, at : at + BLOCK]
        zero = jnp.zeros_like(query)
        some_keys = keys[at : at + SPAN]
        outs, key_part, value_part, rel_part = [], None, None, None
        for low in (True, False):
            pick = (lambda a: jnp.where(low_lane, a, zero)) if low else (
                lambda a: jnp.where(low_lane, zero, a)
            )
            query_one, grad_one = pick(query), pick(grad)
            probs_low = probs_ref[0, 0, block, 0 if low else 1]
            probs = probs_low.astype(F32)
            prob_grads = dot_nt(grad_one, values[at : at + SPAN])
            inner = jnp.sum(prob_grads * probs, axis=1, keepdims=True)
            score_grads = (probs * (prob_grads - inner)).astype(BF)
            turned = pltpu.roll(
                dot_nn(flip, score_grads), SPAN - BLOCK + 1, 1, stride=1, stride_axis=0
            )
            by_offset = dot_nn(flip, turned[:, :BLOCK].astype(BF)).astype(BF)
            outs.append(dot_nn(score_grads, some_keys) + dot_nn(by_offset, rel_ref[0:BLOCK]))
            parts = (
                dot_tn(score_grads, query_one),
                dot_tn(probs_low, grad_one),
                dot_tn(by_offset, query_one),
            )
            if low:
                key_part, value_part, rel_part = parts
            else:
                key_part, value_part, rel_part = (
                    key_part + parts[0],
                    value_part + parts[1],
                    rel_part + parts[2],
                )
        dq_ref[0, at : at + BLOCK] = (jnp.where(low_lane, outs[0], outs[1]) * scale).astype(BF)
        key_sum[at : at + SPAN] += key_part * scale
        value_sum[at : at + SPAN] += value_part
        drel_ref[...] += rel_part * scale
    for total, left, own, right in (
        (key_sum, dkl_ref, dk_ref, dkr_ref),
        (value_sum, dvl_ref, dv_ref, dvr_ref),
    ):
        left[0] = total[0:LEFT].astype(BF)
        own[0] = total[LEFT : LEFT + count]
        right[0] = total[LEFT + count :].astype(BF)


def attend_specs(groups, count, pairs):
    lanes = 2 * HEAD_DIM
    smem = pl.BlockSpec(memory_space=pltpu.SMEM)

    def own(at):
        return pl.BlockSpec((1, count, lanes), lambda g, h: (g, 0, at * pairs + h))

    def edge(at):
        return pl.BlockSpec((1, LEFT, lanes), lambda g, h: (g, 0, at * pairs + h))

    rel = pl.BlockSpec((SPAN, lanes), lambda g, h: (0, 0))
    probs = pl.BlockSpec(
        (1, 1, count // BLOCK, 2, BLOCK, SPAN), lambda g, h: (g, h, 0, 0, 0, 0)
    )
    specs = [smem, smem, own(0), own(1), own(2), edge(0), edge(1), edge(0), edge(1), rel]
    return specs, own, edge, probs


def attend(ends, base, projected, left, right, relative):
    groups, count, _ = projected.shape
    pairs = projected.shape[2] // (6 * HEAD_DIM)
    specs, own, _, probs = attend_specs(groups, count, pairs)
    window = pltpu.VMEM((count + 2 * LEFT, 2 * HEAD_DIM), BF)
    return pl.pallas_call(
        functools.partial(attend_kernel, ends.shape[1]),
        grid=(groups, pairs),
        in_specs=specs,
        out_specs=[own(0), probs],
        out_shape=[
            jax.ShapeDtypeStruct((groups, count, projected.shape[2] // 3), BF),
            jax.ShapeDtypeStruct((groups, pairs, count // BLOCK, 2, BLOCK, SPAN), BF),
        ],
        scratch_shapes=[window, window],
        name="attend",
    )(ends, base, projected, projected, projected, left, left, right, right, relative)


def attend_back(projected, left, right, relative, grad, probs):
    groups, count, _ = projected.shape
    width = projected.shape[2] // 3
    pairs = width // (2 * HEAD_DIM)
    specs, own, edge, saved = attend_specs(groups, count, pairs)
    window = pltpu.VMEM((count + 2 * LEFT, 2 * HEAD_DIM), BF)
    total = pltpu.VMEM((count + 2 * LEFT, 2 * HEAD_DIM), F32)
    rel_sum = pl.BlockSpec((BLOCK, 2 * HEAD_DIM), lambda g, h: (0, 0))
    shape = lambda rows, dtype: jax.ShapeDtypeStruct((groups, rows, width), dtype)
    return pl.pallas_call(
        attend_back_kernel,
        grid=(groups, pairs),
        in_specs=specs[2:] + [own(0), saved],
        out_specs=[own(0), own(0), own(0), edge(0), edge(0), edge(0), edge(0), rel_sum],
        out_shape=[
            shape(count, BF),
            shape(count, F32),
            shape(count, F32),
            shape(LEFT, BF),
            shape(LEFT, BF),
            shape(LEFT, BF),
            shape(LEFT, BF),
            jax.ShapeDtypeStruct((BLOCK, 2 * HEAD_DIM), F32),
        ],
        scratch_shapes=[window, window, total, total],
        name="attend_back",
    )(projected, projected, projected, left, left, right, right, relative, grad, probs)


def products_kernel(steps, first_ref, second_ref, *refs):
    right_refs, out_ref, turned = refs[:-2], refs[-2], refs[-1]
    at = pl.program_id(0)

    @pl.when(at == 0)
    def _():
        turned[...] = first_ref[...].T

    @pl.when(at == 2 * steps)
    def _():
        turned[...] = second_ref[...].T

    for number, right_ref in enumerate(right_refs):

        @pl.when((at >= number * steps) & (at < (number + 1) * steps))
        def _(right_ref=right_ref):
            out_ref[...] = dot_nn(turned[...], right_ref[...]).astype(BF)


def products(first, second, rights):
    count, dim = first.shape
    step = 512
    steps = rights[0].shape[1] // step
    whole = pl.BlockSpec((count, dim), lambda i: (0, 0))

    def part(number):
        return pl.BlockSpec(
            (count, step), lambda i: (0, jnp.clip(i - number * steps, 0, steps - 1))
        )

    return pl.pallas_call(
        functools.partial(products_kernel, steps),
        grid=(4 * steps,),
        in_specs=[whole, whole] + [part(number) for number in range(4)],
        out_specs=pl.BlockSpec((dim, step), lambda i: (0, i)),
        out_shape=jax.ShapeDtypeStruct((dim, 4 * steps * step), BF),
        scratch_shapes=[pltpu.VMEM((dim, count), BF)],
        name="products",
    )(first, second, *rights)


def norm_parts(values):
    centered = values - jnp.mean(values, axis=1, keepdims=True)
    variance = jnp.mean(centered * centered, axis=1, keepdims=True)
    inverse = lax.rsqrt(variance + 1e-05)
    return centered * inverse, inverse


def norm_kernel(share, *refs):
    if share:
        base_ref, own_ref, other_ref, gain_ref, bias_ref, stream_ref, low_ref = refs
        stream = base_ref[...] + share * (own_ref[0] + other_ref[...].astype(F32))
        stream_ref[...] = stream
    else:
        base_ref, gain_ref, bias_ref, low_ref = refs
        stream = base_ref[...]
    normal_part, _ = norm_parts(stream)
    low_ref[...] = (normal_part * gain_ref[...] + bias_ref[...]).astype(BF)


def norm_back_kernel(share, scale, *refs):
    if share:
        stream_ref, own_ref, other_ref, gain_ref, through_ref, grad_ref, low_ref = refs[:7]
        gradient = own_ref[0] + other_ref[...].astype(F32)
    else:
        stream_ref, own_ref, gain_ref, grad_ref, low_ref = refs[:5]
        gradient = own_ref[...].astype(F32)
    gain_grad_ref, bias_grad_ref = refs[-2:]
    normal_part, inverse = norm_parts(stream_ref[...])
    scaled = gradient * gain_ref[...]
    inner = jnp.mean(scaled * normal_part, axis=1, keepdims=True)
    total = inverse * (scaled - jnp.mean(scaled, axis=1, keepdims=True) - normal_part * inner)
    if share:
        total = total + through_ref[...]
    grad_ref[...] = total
    low_ref[...] = (scale * total).astype(BF)

    @pl.when(pl.program_id(0) == 0)
    def _():
        gain_grad_ref[...] = jnp.zeros_like(gain_grad_ref)
        bias_grad_ref[...] = jnp.zeros_like(bias_grad_ref)

    gain_grad_ref[...] += jnp.sum(gradient * normal_part, axis=0, keepdims=True)
    bias_grad_ref[...] += jnp.sum(gradient, axis=0, keepdims=True)


def row_specs(dim):
    step = 64
    rows = pl.BlockSpec((step, dim), lambda i: (i, 0))
    first = pl.BlockSpec((1, step, dim), lambda i: (0, i, 0))
    line = pl.BlockSpec((1, dim), lambda i: (0, 0))
    return step, rows, first, line


def add_and_norm(base, share, own, other, gain, bias):
    count, dim = base.shape
    step, rows, first, line = row_specs(dim)
    low = jax.ShapeDtypeStruct((count, dim), BF)
    if not share:
        return pl.pallas_call(
            functools.partial(norm_kernel, share),
            grid=(count // step,),
            in_specs=[rows, line, line],
            out_specs=rows,
            out_shape=low,
            name="norm",
        )(base, gain, bias)
    return pl.pallas_call(
        functools.partial(norm_kernel, share),
        grid=(count // step,),
        in_specs=[rows, first, rows, line, line],
        out_specs=[rows, rows],
        out_shape=[jax.ShapeDtypeStruct((count, dim), F32), low],
        name="add_and_norm",
    )(base, own, other, gain, bias)


def norm_and_add_back(stream, own, other, gain, through, scale):
    count, dim = stream.shape
    step, rows, first, line = row_specs(dim)
    share = through is not None
    specs = [rows, first, rows, line, rows] if share else [rows, rows, line]
    args = (stream, own, other, gain, through) if share else (stream, own, gain)
    return pl.pallas_call(
        functools.partial(norm_back_kernel, share, scale),
        grid=(count // step,),
        in_specs=specs,
        out_specs=[rows, rows, line, line],
        out_shape=[
            jax.ShapeDtypeStruct((count, dim), F32),
            jax.ShapeDtypeStruct((count, dim), BF),
            jax.ShapeDtypeStruct((1, dim), F32),
            jax.ShapeDtypeStruct((1, dim), F32),
        ],
        name="norm_back",
    )(*args)


def split_layer_norm(place, values, gain_row, bias_row):
    count = values.shape[-1]
    own_mean = jnp.mean(values, axis=-1, keepdims=True)
    own_square = jnp.sum((values - own_mean) ** 2, axis=-1, keepdims=True)
    stats = jnp.concatenate([own_mean, own_square], -1)
    others = place.sibling(stats)[::-1]
    mean = 0.5 * (own_mean + others[..., :1])
    square = own_square + others[..., 1:]
    square = square + count * ((own_mean - mean) ** 2 + (others[..., :1] - mean) ** 2)
    inverse = lax.rsqrt(square / (2 * count) + 1e-05)
    normal_part = (values - mean) * inverse
    return (normal_part * gain_row + bias_row, (normal_part, inverse))


def split_norm_sums(place, gradient, normal_part, gain_row):
    scaled = gradient * gain_row
    sums = jnp.concatenate(
        [
            jnp.sum(scaled, axis=-1, keepdims=True),
            jnp.sum(scaled * normal_part, axis=-1, keepdims=True),
        ],
        -1,
    )
    return (sums + place.sibling(sums)[::-1]) / (2 * gradient.shape[-1])


def swish_slope(values):
    sigmoid_val = jax.nn.sigmoid(values)
    return sigmoid_val * (1.0 + values * (1.0 - sigmoid_val))


def clip_bounds(positions, ends_ref, group, clips):
    start = jnp.zeros(positions.shape, jnp.int32)
    stop = jnp.full(positions.shape, 1 << 30, jnp.int32)
    for clip in range(clips):
        end = ends_ref[group, clip]
        start = jnp.maximum(start, jnp.where(positions >= end, end, 0))
        stop = jnp.minimum(stop, jnp.where(positions < end, end, 1 << 30))
    return start, jnp.where(positions < 0, positions, stop)


def taps_kernel(clips, ends_ref, base_ref, prev_ref, glu_ref, taps_ref, out_ref, window):
    count = glu_ref.shape[1]
    group = pl.program_id(0)
    window[0:EDGE] = prev_ref[0].astype(F32)
    window[EDGE:] = glu_ref[0].astype(F32)
    at = base_ref[0] + lax.broadcasted_iota(jnp.int32, (count, 1), 0)
    start, _ = clip_bounds(at, ends_ref, group, clips)
    age = jnp.broadcast_to(at - start, (count, 128))
    total = jnp.zeros((count, 128), F32)
    for tap in range(KERNEL):
        first = tap + EDGE - KERNEL + 1
        values = window[first : first + count] * taps_ref[tap : tap + 1]
        total = total + jnp.where(age >= KERNEL - 1 - tap, values, 0.0)
    out_ref[0] = total


def taps_back_kernel(
    clips, ends_ref, base_ref, prev_ref, glu_ref, taps_ref, grad_ref, normal_ref, inverse_ref, sums_ref,
    gain_ref, dglu_ref, dprev_ref, dtaps_ref, dgain_ref, dbias_ref, window, spread,
):
    count = glu_ref.shape[1]
    group = pl.program_id(1)

    @pl.when(group == 0)
    def _():
        dtaps_ref[...] = jnp.zeros_like(dtaps_ref)
        dgain_ref[...] = jnp.zeros_like(dgain_ref)
        dbias_ref[...] = jnp.zeros_like(dbias_ref)

    window[0:EDGE] = prev_ref[0].astype(F32)
    window[EDGE:] = glu_ref[0].astype(F32)
    grad, normal_part = grad_ref[0], normal_ref[0]
    dgain_ref[...] += jnp.sum(grad * normal_part, axis=0, keepdims=True)
    dbias_ref[...] += jnp.sum(grad, axis=0, keepdims=True)
    own = inverse_ref[0] * (
        grad * gain_ref[...] - sums_ref[0, :, 0:1] - normal_part * sums_ref[0, :, 1:2]
    )
    spread[0:EDGE] = jnp.zeros((EDGE, 128), F32)
    spread[EDGE : EDGE + count] = own
    spread[EDGE + count :] = jnp.zeros((EDGE, 128), F32)
    at = base_ref[0] + lax.broadcasted_iota(jnp.int32, (count, 1), 0)
    start, _ = clip_bounds(at, ends_ref, group, clips)
    age = jnp.broadcast_to(at - start, (count, 128))
    source = base_ref[0] - EDGE + lax.broadcasted_iota(jnp.int32, (count + EDGE, 1), 0)
    _, stop = clip_bounds(source, ends_ref, group, clips)
    remain = jnp.broadcast_to(stop - source, (count + EDGE, 128))
    total = jnp.zeros((count + EDGE, 128), F32)
    for tap in range(KERNEL):
        back = KERNEL - 1 - tap
        first = EDGE - back
        kept = jnp.where(age >= back, own, 0.0) * window[first : first + count]
        dtaps_ref[tap : tap + 1] += jnp.sum(kept, axis=0, keepdims=True)
        values = spread[back : back + count + EDGE] * taps_ref[tap : tap + 1]
        total = total + jnp.where(remain > back, values, 0.0)
    dprev_ref[0] = total[0:EDGE].astype(BF)
    dglu_ref[0] = total[EDGE:]


def taps_specs(count, order):
    smem = pl.BlockSpec(memory_space=pltpu.SMEM)
    lanes = pl.BlockSpec((1, count, 128), lambda *at: (at[order[0]], 0, at[order[1]]))
    edge = pl.BlockSpec((1, EDGE, 128), lambda *at: (at[order[0]], 0, at[order[1]]))
    taps = pl.BlockSpec((EDGE, 128), lambda *at: (0, at[order[1]]))
    return smem, lanes, edge, taps


def taps_forward(ends, base, prev, glu, taps):
    groups, count, width = glu.shape
    smem, lanes, edge, tap_lanes = taps_specs(count, (0, 1))
    return pl.pallas_call(
        functools.partial(taps_kernel, ends.shape[1]),
        grid=(groups, width // 128),
        in_specs=[smem, smem, edge, lanes, tap_lanes],
        out_specs=lanes,
        out_shape=jax.ShapeDtypeStruct((groups, count, width), F32),
        scratch_shapes=[pltpu.VMEM((count + EDGE, 128), F32)],
        name="taps",
    )(ends, base, prev, glu, taps)


def taps_back(ends, base, prev, glu, taps, grad, normal_part, inverse, sums, gain):
    groups, count, width = glu.shape
    smem, lanes, edge, tap_lanes = taps_specs(count, (1, 0))
    row_one = pl.BlockSpec((1, count, 1), lambda c, g: (g, 0, 0))
    row_two = pl.BlockSpec((1, count, 2), lambda c, g: (g, 0, 0))
    line = pl.BlockSpec((1, 128), lambda c, g: (0, c))
    shape = jax.ShapeDtypeStruct
    return pl.pallas_call(
        functools.partial(taps_back_kernel, ends.shape[1]),
        grid=(width // 128, groups),
        in_specs=[smem, smem, edge, lanes, tap_lanes, lanes, lanes, row_one, row_two, line],
        out_specs=[lanes, edge, tap_lanes, line, line],
        out_shape=[
            shape((groups, count, width), F32),
            shape((groups, EDGE, width), BF),
            shape((EDGE, width), F32),
            shape((1, width), F32),
            shape((1, width), F32),
        ],
        scratch_shapes=[
            pltpu.VMEM((count + EDGE, 128), F32),
            pltpu.VMEM((count + 2 * EDGE, 128), F32),
        ],
        name="taps_back",
    )(ends, base, prev, glu, taps, grad, normal_part, inverse, sums, gain)


def dot(left, right, left_axis, right_axis):
    return lax.dot_general(
        left, right, (((left_axis,), (right_axis,)), ((), ())), preferred_element_type=F32
    )


def row_major(array):
    return with_layout_constraint(array, Layout(tuple(range(array.ndim))))


def local(
    inputs,
    lengths,
    ffn_in,
    ffn_out,
    qkv_weight,
    out_weight,
    conv_in,
    conv_depth,
    conv_out,
    norm_gain,
    norm_bias,
    rel_key,
    cotangent,
):
    place = Place()
    seq_size, chips, core = place.seq_size, place.chips, place.core
    row_count, dim = inputs.shape[1:]
    hid = ffn_in.shape[3] // 2
    quarter = hid // 2
    width = dim // 2
    rows = 2 * ffn_in.shape[2]
    tap_first, tap_last = 12, 12 + KERNEL

    small = jnp.concatenate([norm_gain[0], norm_bias[0], conv_depth[0]], 0)
    small_count = small.shape[0]
    small = jnp.pad(small, ((0, 128 - small_count), (0, 0))).T
    out_rows = jnp.swapaxes(ffn_out[0], 1, 2)

    def pick(array, count, which):
        parts = array.reshape(array.shape[0], count, -1)
        return place.core_part(parts, 2, which).reshape(array.shape[0], -1)

    def ffn_parts(net, part, which):
        span = slice(part * quarter, (part + 1) * quarter)
        return [pick(ffn_in[0, net], 1, which)[:, span], pick(out_rows[net], 1, which)[:, span]]

    def attention_parts(which):
        return [
            pick(qkv_weight[0], 3, which),
            pick(conv_in[0], 2, which),
            pick(out_weight[0], 1, which),
            pick(conv_out[0], 1, which),
        ]

    def chip_block(kept, sent):
        kept, sent = jnp.concatenate(kept, 1), jnp.concatenate(sent, 1)
        return place.by_core(kept, place.sibling(sent), 0)

    other = 1 - core
    first_block = chip_block(
        ffn_parts(0, 0, core) + [small], ffn_parts(0, 0, other) + [small]
    )
    later_block = chip_block(
        ffn_parts(0, 1, core) + attention_parts(core) + ffn_parts(1, 0, core) + ffn_parts(1, 1, core),
        ffn_parts(0, 1, other)
        + attention_parts(other)
        + ffn_parts(1, 0, other)
        + ffn_parts(1, 1, other),
    )
    n_attention = 7 * width
    attention_block = later_block[:, 2 * quarter : 2 * quarter + n_attention]
    attention_all = lax.all_gather(attention_block, ("seq", "plane"), axis=0, tiled=True)
    at = [0, quarter]
    at += [2 * quarter + n_attention + part * quarter for part in range(4)]
    pieces = [later_block[:, start : start + quarter] for start in at]
    chunks = [
        (
            [first_block[:, :quarter], first_block[:, 2 * quarter :]],
            [first_block[:, quarter : 2 * quarter]],
        ),
        ([pieces[0]], [pieces[1]]),
        ([pieces[2]], [pieces[3]]),
        ([pieces[4]], [pieces[5]]),
    ]
    gathered, z_marks, firsts, seconds = [], [], [], []

    def fetch(*waits):
        index = len(gathered)
        left, right = chunks[index]
        block = tie(jnp.concatenate(left + right, 1), *z_marks[-1:], *waits)
        spread = place.swap_seq(jnp.broadcast_to(block[None], (seq_size,) + block.shape))
        z_marks.append(tip(spread))
        marks = []
        n_left = sum(part.shape[1] for part in left)
        parts = tie(spread[..., :n_left], *seconds[-1:]), tie(spread[..., n_left:], *seconds[-1:])
        fulls = [gather_plane(place, part, turn, marks) for turn, part in enumerate(parts)]
        firsts.append(marks[place.bits])
        seconds.append(marks[-1])
        gathered.append([full.reshape(dim, -1) for full in fulls])

    fetch()
    fetch()
    small_all = gathered[0][0][:, quarter:].T.astype(F32)
    gains, biases = small_all[:6, None], small_all[6:12, None]
    tap_values = place.core_part(small_all[tap_first:tap_last], 1, core)
    gain3 = place.core_part(small_all[3], 0, core)
    bias3 = place.core_part(small_all[9], 0, core)
    w_qkv = attention_all[:, : 3 * width]
    w_first = attention_all[:, 3 * width : 5 * width]
    columns = attention_all[:, 5 * width :]
    from_other = place.sibling(place.core_part(columns, 0, other))
    columns = place.core_part(columns, 0, core)
    w_out = place.by_core(columns[:, :width], from_other[:, :width], 1)
    w_second = place.by_core(columns[:, width:], from_other[:, width:], 1)

    group_lengths = jnp.concatenate([lengths, place.sibling(lengths)], 0)
    clips = group_lengths.shape[1]
    order = jnp.arange(clips)
    clip_ends = jnp.sum(
        jnp.where(order[None, :, None] >= order[None, None, :], group_lengths[:, None, :], 0), axis=2
    )
    first_row = place.seq * row_count

    def weights_of(net, part):
        left, right = gathered[2 * net + part]
        return left[:, :quarter], right

    def flat2(array):
        return array.reshape(2 * row_count, -1)

    def pair2(array):
        return array.reshape(2, row_count, -1)

    def feed_forward(normed, net):
        normed_low = flat2(place.both(normed))
        pres, acts, branch = [], [], 0.0
        for part in range(2):
            w_in, w_down = weights_of(net, part)
            pre_act = dot(normed_low, w_in, 1, 0)
            act_low = (pre_act * jax.nn.sigmoid(pre_act)).astype(BF)
            if net == 0 and part == 0:
                fetch(tip(act_low))
            branch = branch + dot(act_low, w_down, 1, 1)
            pres.append(pre_act)
            acts.append(act_low)
        return pair2(branch), (normed_low, pres, acts)

    def joined(base, share, branch, norm_index, *marks):
        received = place.from_sibling(branch)
        gain = tie(gains[norm_index], *marks)
        return add_and_norm(base, share, branch, received, gain, biases[norm_index])

    stream = inputs[0].astype(F32)
    normed = add_and_norm(stream, 0.0, None, None, gains[0], biases[0])
    branch, ffn_first = feed_forward(normed, 0)
    after_ffn, normed = joined(stream, 0.5, branch, 1)
    fetch(tip(normed))
    attn_input = flat2(place.both(normed))
    projected = pair2(dot(attn_input, w_qkv, 1, 0).astype(BF))
    from_left = place.along(projected[:, row_count - LEFT :, width:], 1)
    from_right = place.along(projected[:, :RIGHT, width:], -1)
    from_right = jnp.pad(from_right, ((0, 0), (0, LEFT - RIGHT), (0, 0)))
    relative = jnp.pad(
        jnp.concatenate([rel_key[0], rel_key[0]], 1), ((0, SPAN - rel_key.shape[1]), (0, 0))
    )
    base = jnp.reshape(first_row, (1,))
    attended, probs = attend(clip_ends, tie(base, firsts[2]), projected, from_left, from_right, relative)
    attended = flat2(attended)
    after_attn, normed = joined(after_ffn, 1.0, pair2(dot(attended, w_out, 1, 0)), 2, seconds[2], firsts[3])
    conv_input = flat2(place.both(normed))
    spread_pre = pair2(dot(conv_input, w_first, 1, 0))
    value_part, gate_sig = spread_pre[..., :width], jax.nn.sigmoid(spread_pre[..., width:])
    gated_low = (value_part * gate_sig).astype(BF)
    from_prev = place.along(gated_low[:, row_count - EDGE :], 1)
    tap_rows = jnp.pad(tap_values, ((0, EDGE - KERNEL), (0, 0)))
    filtered = taps_forward(clip_ends, base, from_prev, gated_low, tap_rows)
    normed_conv, depth_norm = split_layer_norm(place, filtered, gain3, bias3)
    swished = (normed_conv * jax.nn.sigmoid(normed_conv)).astype(BF)
    after_conv, normed = joined(after_attn, 1.0, pair2(dot(flat2(swished), w_second, 1, 0)), 4)
    branch, ffn_second = feed_forward(normed, 1)
    fourth, result = joined(after_conv, 0.5, branch, 5)
    outputs = result[None]

    def summed(terms):
        return jnp.sum(place.swap_seq(terms).astype(F32), 0)

    def scatter_early(terms, after):
        terms = jnp.concatenate(terms, 1)
        terms = row_major(terms.reshape(seq_size, chips * rows, terms.shape[1]))
        part = lax.psum_scatter(terms, "plane", scatter_dimension=1, tiled=True)
        return summed(tie(row_major(part), after))

    def plane_sums(pair):
        parts, marks = [], []
        for turn, terms in enumerate(pair):
            blocks = terms.reshape(seq_size, chips, rows, -1)
            parts.append(scatter_plane(place, blocks, turn, marks))
        return jnp.concatenate(parts, -1), marks[:: place.bits]

    gain_grads = [None] * 6
    bias_grads = [None] * 6

    def back_to(norm_index, stream_at, branch, through, share, *marks):
        received = None if through is None else place.from_sibling(branch)
        gain = tie(gains[norm_index], *marks)
        grad, low, gain_grads[norm_index], bias_grads[norm_index] = norm_and_add_back(
            stream_at, branch, received, gain, through, share
        )
        return grad, low

    def feed_back(low, net, cached):
        normed_low, pres, acts = cached
        branch_grad = flat2(place.both(low))
        pre_grads, normed_grad = [], 0.0
        for part in range(2):
            act_grad = dot(branch_grad, weights_of(net, part)[1], 1, 0)
            pre_grads.append((act_grad * swish_slope(pres[part])).astype(BF))
        for part in range(2):
            normed_grad = normed_grad + dot(pre_grads[part], weights_of(net, part)[0], 1, 1)
        return pair2(normed_grad), pre_grads, acts, normed_low, branch_grad

    def exchanged(wide):
        received = place.sibling(place.core_part(wide, 1, other))
        return place.by_core(place.core_part(wide, 1, core), received, 0)

    grad_fourth, low = back_to(5, fourth, cotangent[0], None, 0.5)
    branch, pre_grads, acts, normed_low, branch_grad = feed_back(low, 1, ffn_second)
    second_terms = [products(normed_low, branch_grad, pre_grads + acts)]
    grad_conv_out, low = back_to(4, after_conv, branch, grad_fourth, 1.0)
    branch_grad = flat2(place.both(low))
    conv_out_terms = exchanged(dot(flat2(swished), branch_grad, 0, 0).astype(BF))
    swish_grad = pair2(dot(branch_grad, w_second, 1, 1))
    swish_grad = swish_grad * swish_slope(normed_conv)
    sums = split_norm_sums(place, swish_grad, depth_norm[0], gain3)
    gated_grad, to_prev, tap_grads, gain3_grad, bias3_grad = taps_back(
        clip_ends, base, from_prev, gated_low, tap_rows, swish_grad, *depth_norm, sums, gain3[None]
    )
    to_prev = place.along(to_prev, -1).astype(F32)
    gated_grad = gated_grad + jnp.pad(to_prev, ((0, 0), (row_count - EDGE, 0), (0, 0)))
    spread_grad = flat2(
        jnp.concatenate(
            [gated_grad * gate_sig, gated_grad * value_part * gate_sig * (1.0 - gate_sig)], axis=2
        ).astype(BF)
    )
    branch = pair2(dot(spread_grad, w_first, 1, 1))
    conv_in_terms = dot(conv_input, spread_grad, 0, 0).astype(BF)
    grad_attn_out, low = back_to(2, after_attn, branch, grad_conv_out, 1.0)
    branch_grad = flat2(place.both(low))
    out_terms = exchanged(dot(attended, branch_grad, 0, 0).astype(BF))
    attended_grad = pair2(dot(branch_grad, w_out, 1, 1).astype(BF))
    query_grad, key_grad, value_grad, kl, vl, kr, vr, relative_grad = attend_back(
        projected, from_left, from_right, relative, attended_grad, probs
    )
    second_sum = scatter_early(second_terms, tip(query_grad))
    to_left = place.along(jnp.concatenate([kl, vl], 2), -1).astype(F32)
    to_right = place.along(jnp.concatenate([kr[:, :RIGHT], vr[:, :RIGHT]], 2), 1).astype(F32)
    own_grad = (
        jnp.concatenate([key_grad, value_grad], 2)
        + jnp.pad(to_left, ((0, 0), (row_count - LEFT, 0), (0, 0)))
        + jnp.pad(to_right, ((0, 0), (0, row_count - RIGHT), (0, 0)))
    )
    projected_grad = flat2(jnp.concatenate([query_grad, own_grad.astype(BF)], axis=2))
    branch = pair2(dot(projected_grad, w_qkv, 1, 1))
    qkv_terms = dot(attn_input, projected_grad, 0, 0).astype(BF)
    grad_ffn_out, low = back_to(
        1, after_ffn, branch, grad_attn_out, 0.5
    )
    branch, pre_grads, acts, normed_low, branch_grad = feed_back(low, 0, ffn_first)
    downs = [dot(branch_grad, acts[part], 0, 0).astype(BF) for part in range(2)]
    ins = [dot(normed_low, pre_grads[part], 0, 0).astype(BF) for part in range(2)]
    down_part, down_marks = plane_sums(downs)
    in_part, _ = plane_sums(ins)
    grad_input, _ = back_to(
        0, stream, branch, grad_ffn_out, 1.0, *down_marks, tip(second_sum)
    )
    down_sum = summed(tie(down_part, tip(grad_input)))
    in_sum = summed(tie(in_part, tip(grad_input)))
    attention_sum = scatter_early(
        [qkv_terms, conv_in_terms, out_terms, conv_out_terms], tip(grad_input)
    )
    offsets = LEFT + RIGHT + 1
    relative_grad = relative_grad[:offsets, :HEAD_DIM] + relative_grad[:offsets, HEAD_DIM:]

    def spread_core(half_rows):
        return place.by_core(half_rows, jnp.zeros_like(half_rows), 1)

    gain_grads[3] = spread_core(gain3_grad)
    bias_grads[3] = spread_core(bias3_grad)
    small_grads = jnp.concatenate(
        gain_grads + bias_grads + [spread_core(tap_grads[:KERNEL])], 0
    )
    small_grads = jnp.pad(small_grads, ((0, 128 - small_count), (0, 0))).T
    rel_part = jnp.pad(relative_grad, ((0, -offsets % 8), (0, 128 - HEAD_DIM)))
    rel_part = rel_part + place.sibling(rel_part)
    current = small_grads.reshape((seq_size,) + (2,) * place.bits + (rows, 128))
    for bit in range(place.bits):
        axis = place.bits - bit
        me = place.bit(bit)
        keep = lax.dynamic_slice_in_dim(current, me, 1, axis)
        sent = lax.dynamic_slice_in_dim(current, 1 - me, 1, axis)
        got = place.hop(jnp.concatenate([sent.reshape(-1, 128), rel_part], 0), bit)
        current = keep + got[: -rel_part.shape[0]].reshape(keep.shape)
        rel_part = rel_part + got[-rel_part.shape[0] :]
    rel_all = jnp.broadcast_to(rel_part[None], (seq_size,) + rel_part.shape)
    small_total = summed(
        jnp.concatenate([current.reshape(seq_size, rows, 128), rel_all], 1)
    )
    rel_total = small_total[rows : rows + offsets, :HEAD_DIM]
    small_total = small_total[:rows]
    small_sum = place.core_part(small_total, 0, core) + place.sibling(
        place.core_part(small_total, 0, other)
    )
    small_sum = small_sum[:, :small_count].T

    def own_rows(total, counts):
        received = place.sibling(place.core_part(total, 0, other))
        mine = place.core_part(total, 0, core)
        results, start = [], 0
        for count, n in counts:
            halves = [
                part[:, start : start + n].reshape(-1, count, n // count) for part in (mine, received)
            ]
            results.append(place.by_core(*halves, 2).reshape(mine.shape[0], 2 * n))
            start += n
        return results

    in_second, down_second = own_rows(second_sum, [(1, hid), (1, hid)])
    qkv_sum, first_sum, out_sum, second_sum = own_rows(
        attention_sum, [(3, 3 * width), (2, 2 * width), (1, width), (1, width)]
    )
    (down_first,) = own_rows(down_sum, [(1, hid)])
    (in_first,) = own_rows(in_sum, [(1, hid)])
    return (
        outputs,
        grad_input[None],
        jnp.stack([in_first, in_second])[None],
        jnp.swapaxes(jnp.stack([down_first, down_second]), 1, 2)[None],
        qkv_sum[None],
        out_sum[None],
        first_sum[None],
        small_sum[None, tap_first:tap_last],
        second_sum[None],
        small_sum[None, :6],
        small_sum[None, 6:12],
        rel_total[None],
    )


def solution(mesh):
    seq_size, fsdp_size = mesh.shape["seq"], mesh.shape["fsdp"]
    chips = Mesh(mesh.devices.reshape(seq_size, fsdp_size // 2, 2), ("seq", "plane", "core"))
    fsdp = ("plane", "core")
    spread = ("seq", "plane", "core")
    tokens = P(fsdp, "seq", None)
    split_rows = P(None, spread, None)
    split_last = P(None, None, spread)
    weights = (
        P(None, None, spread, None),
        P(None, None, None, spread),
        split_rows,
        split_rows,
        split_rows,
        split_last,
        split_rows,
        split_last,
        split_last,
        P(),
    )
    return jax.shard_map(
        local,
        mesh=chips,
        in_specs=(tokens, P(fsdp, None)) + weights + (tokens,),
        out_specs=(tokens, tokens) + weights,
        check_vma=False,
    )
```

time: 896 us -> 785 us (0.88)
  local copies, waits for them, and re-layouts: 211 us -> 86.8 us
  Pallas kernels: 0 us -> 116 us
  other arithmetic: 178 us -> 90.8 us
  starting transfers between devices: 142 us -> 86.9 us
  blocking collectives: 0 us -> 43.3 us
    pallas_call x0 -> x15, Pallas kernels: none -> 116 us  [the longest x1 23.5 us: attend_back(): pl.pallas_call(attend_back_kernel, grid=(groups, pairs), in_specs=specs[2...]
    reshape x13 -> x6, local copies, waits for them, and re-layouts: 49.9 us -> 0.61 us  [the longest x4 0.51 us: own_rows(): part[:, start:start + n].reshape(-1, count, n // count)]
    all_to_all x0 -> x1, blocking collectives: none -> 43.3 us  [swap_seq(): return lax.all_to_all(blocks, 'seq', 0, 0, tiled=True)]
    all_to_all x13 -> x8, starting transfers between devices: 61.8 us -> 33.6 us  [swap_seq(): return lax.all_to_all(blocks, 'seq', 0, 0, tiled=True)]
    reduce_sum x36 -> x5, other arithmetic: 27.4 us -> 1.87 us  [summed(): return jnp.sum(place.swap_seq(terms).astype(F32), 0)]
    ppermute x78 -> x56, starting transfers between devices: 62.6 us -> 37.6 us  [the longest x26 32.8 us: hop(): lax.ppermute(shard, 'plane', [(i, i ^ 1 << bit) for i in range(self.chips)])]
    convert_element_type x24 -> x7, other arithmetic: 27.3 us -> 6.35 us  [the longest x4 4.09 us: scatter_plane(): current = (keep.astype(F32) + got.astype(F32)).astype(full.dtype)]
    dot_general x8 -> x0, matrix products: 18.1 us -> none  [the longest x1 4.8 us: local(): jnp.einsum('hij,hid->hjd', backward_probs_low, attended_grad, preferred_e...]
  transfers between devices with their start and end apart: 97 -> 73, of which waited for: 28 -> 33; matrix products, arithmetic and copies ran while one was open for 47% -> 26% of each run, Pallas kernels for 0% -> 12%
where the time goes in v2:
time: 785 us; the launch traced here: 775 us
  waiting for transfers between devices  244 us (31%)
  Pallas kernels  116 us (15%)
  other arithmetic  90.8 us (12%)
  starting transfers between devices  86.9 us (11%)
  local copies, waits for them, and re-layouts  86.8 us (11%)
  matrix products  70.7 us (9%)
  blocking collectives  43.3 us (6%)
  between operations  36.6 us (5%)
    ppermute x26, waiting for transfers between devices, hop(): lax.ppermute(shard, 'plane', [(i, i ^ 1 << bit) for i in range(self.chips)])  139 us
    all_to_all x8, waiting for transfers between devices, swap_seq(): return lax.all_to_all(blocks, 'seq', 0, 0, tiled=True)  76.6 us
    dot_general x32, matrix products, dot(): lax.dot_general(left, right, (((left_axis,), (right_axis,)), ((), ())), p...  70.7 us
    all_to_all x1, blocking collectives, swap_seq(): return lax.all_to_all(blocks, 'seq', 0, 0, tiled=True)  43.3 us
    all_to_all x8, starting transfers between devices, swap_seq(): return lax.all_to_all(blocks, 'seq', 0, 0, tiled=True)  33.6 us
    ppermute x26, starting transfers between devices, hop(): lax.ppermute(shard, 'plane', [(i, i ^ 1 << bit) for i in range(self.chips)])  32.8 us
    select_n x16, other arithmetic, gather_plane(): jnp.where(place.bit(bit) == 0, jnp.concatenate([current, other], axis), j...  31.8 us
    unnamed x297, local copies, waits for them, and re-layouts  31.2 us
  transfers between devices with their start and end apart: 73, of which 33 were waited for; matrix products, arithmetic and copies ran while one was open for 26% of the time, Pallas kernels for 12%

profile of v2, /device:TPU:0, one launch (start us, length us, event | category | flops | bytes accessed | tf_op | source)
XLA Modules:
  0.0 775.0 jit_solution(1885285795066574235)
XLA Ops:
  15.1 43.3 %all_to_all.45 = bf16[4,64,2176]{2,1,0:T(8,128)(2,1)S(1)} all-to-all(bf16[4,64,2176]{2,1,0:T(8,128)(2,1)S(1)} %broadcast_in_dim.56), channel_id=1, replica_groups=mesh['seq'=4,'plane'=4,'core'=2] {'seq'}, dimensions={0} | all-to-all | bytes 2228224 | tf_op jit(solution)/shard_map/all_to_all | solution.py:43
  64.6 4.3 all-to-all-start.1
  68.9 8.9 %collective-permute-done.4 = bf16[4,1,1,64,1024]{4,3,0,2,1:T(8,128)(2,1)} collective-permute-done((bf16[4,1,1,64,1024]{4,3,0,2,1:T(8,128)(2,1)S(1)}, bf16[4,1,1,64,1024]{4,3,0,2,1:T(8,128)(2,1)}, u32[]{:S(2)}, u32[]{:S(2)}) %collective-permute-start.4) | collective-permute-done | bytes 524320 | tf_op jit(solution)/shard_map/ppermute | solution.py:36
  80.8 5.7 collective-permute-done.1
  90.7 17.5 %collective-permute-done.5 = bf16[4,2,1,64,1024]{4,3,0,2,1:T(8,128)(2,1)S(1)} collective-permute-done((bf16[4,2,1,64,1024]{4,3,0,2,1:T(8,128)(2,1)S(1)}, bf16[4,2,1,64,1024]{4,3,0,2,1:T(8,128)(2,1)S(1)}, u32[]{:S(2)}, u32[]{:S(2)}) %collective-permute-start.5) | collective-permute-done | bytes 1048608 | tf_op jit(solution)/shard_map/ppermute | solution.py:36
  115.2 10.2 %collective-permute-done.2 = bf16[4,1,2,64,1152]{4,3,0,2,1:T(8,128)(2,1)} collective-permute-done((bf16[4,1,2,64,1152]{4,3,0,2,1:T(8,128)(2,1)S(1)}, bf16[4,1,2,64,1152]{4,3,0,2,1:T(8,128)(2,1)}, u32[]{:S(2)}, u32[]{:S(2)}) %collective-permute-start.2) | collective-permute-done | bytes 1179680 | tf_op jit(solution)/shard_map/ppermute | solution.py:36
  158.5 4.4 all-to-all-start.2
  162.9 11.3 %collective-permute-done.8 = bf16[4,1,2,64,1024]{4,3,0,2,1:T(8,128)(2,1)} collective-permute-done((bf16[4,1,2,64,1024]{4,3,0,2,1:T(8,128)(2,1)S(1)}, bf16[4,1,2,64,1024]{4,3,0,2,1:T(8,128)(2,1)}, u32[]{:S(2)}, u32[]{:S(2)}) %collective-permute-start.8) | collective-permute-done | bytes 1048608 | tf_op jit(solution)/shard_map/ppermute | solution.py:36
  222.2 12.5 %collective-permute-done.19 = bf16[4,2,1,64,1024]{4,3,0,2,1:T(8,128)(2,1)S(1)} collective-permute-done((bf16[4,2,1,64,1024]{4,3,0,2,1:T(8,128)(2,1)S(1)}, bf16[4,2,1,64,1024]{4,3,0,2,1:T(8,128)(2,1)S(1)}, u32[]{:S(2)}, u32[]{:S(2)}) %collective-permute-start.19) | collective-permute-done | bytes 1048608 | tf_op jit(solution)/shard_map/ppermute | solution.py:36
  253.3 14.8 %attend.1 = (bf16[2,256,512]{2,1,0:T(8,128)(2,1)}, bf16[2,4,2,2,128,256]{5,4,3,2,1,0:T(8,128)(2,1)}) custom-call(s32[2,3]{1,0:T(2,128)} %copy.176.ends_ref, s32[1]{0:T(128)S(6)} %select_n.637.base_ref, bf16[2,256,1536]{2,1,0:T(8,128)(2,1)} %bitcast.259, bf16[2,256,1536]{2,1,0:T(8,128)(2,1)} %bitcast.260, bf16[2,256,1536]{2,1,0:T(8,128)(2,1)} %bitcast.261, ...), custom_call_target="tpu_custom_call" | custom-call | tf_op jit(solution)/shard_map/attend/pallas_call | solution.py:270
  303.7 8.3 %taps.1 = f32[2,256,512]{2,1,0:T(8,128)} custom-call(s32[2,3]{1,0:T(2,128)} %copy.176.ends_ref, s32[1]{0:T(128)} %bitcast.41.base_ref, bf16[2,32,512]{2,1,0:T(8,128)(2,1)} %copy-done.96, bf16[2,256,512]{2,1,0:T(8,128)(2,1)} %copy-done.5, f32[32,512]{1,0:T(8,128)} %pad.54.taps_ref), custom_call_target="tpu_custom_call" | custom-call | tf_op jit(solution)/shard_map/taps/pallas_call | solution.py:561
  336.4 6.6 collective-permute-done.29
  362.3 4.5 norm_back.5
  370.2 4.5 multiply_convert_fusion.3.refs_0_
  377.3 11.5 %products.1 = bf16[1024,4096]{1,0:T(8,128)(2,1)} custom-call(bf16[512,1024]{1,0:T(8,128)(2,1)} %bitcast.269, bf16[512,1024]{1,0:T(8,128)(2,1)} %bitcast.272, bf16[512,1024]{1,0:T(8,128)(2,1)} %multiply_convert_fusion.3.refs_0_, bf16[512,1024]{1,0:T(8,128)(2,1)} %multiply_convert_fusion.2.refs_1_, bf16[512,1024]{1,0:T(8,128)(2,1)} %copy-done.58, ...), custom_call_target="tpu_custom_call" | custom-call | tf_op jit(solution)/shard_map/products/pallas_call | solution.py:343
  396.4 4.6 norm_back.6
  403.3 4.1 multiply_reduce_fusion.2
  410.3 15.2 %taps_back.1 = (f32[2,256,512]{2,1,0:T(8,128)}, bf16[2,32,512]{2,1,0:T(8,128)(2,1)}, f32[32,512]{1,0:T(8,128)}, f32[1,512]{1,0:T(1,128)}, f32[1,512]{1,0:T(1,128)}) custom-call(s32[2,3]{1,0:T(2,128)} %copy.176.ends_ref, s32[1]{0:T(128)} %bitcast.41.base_ref, bf16[2,32,512]{2,1,0:T(8,128)(2,1)} %copy-done.96, bf16[2,256,512]{2,1,0:T(8,128)(2,1)} %copy-done.5, ...), custom_call_target="tpu_custom_call" | custom-call | tf_op jit(solution)/shard_map/taps_back/pallas_call | solution.py:579
  426.9 5.4 collective-permute-done.36
  440.2 4.6 norm_back.7
  453.2 23.5 %attend_back.1 = (bf16[2,256,512]{2,1,0:T(8,128)(2,1)}, f32[2,256,512]{2,1,0:T(8,128)}, f32[2,256,512]{2,1,0:T(8,128)}, bf16[2,64,512]{2,1,0:T(8,128)(2,1)}, bf1...) custom-call(bf16[2,256,1536]{2,1,0:T(8,128)(2,1)} %bitcast.262, ...), custom_call_target="tpu_custom_call" | custom-call | tf_op jit(solution)/shard_map/attend_back/pallas_call | solution.py:293
  483.3 4.5 collective-permute-start.40
  503.4 4.7 norm_back.8
  527.4 5.9 all-to-all-start.4
  545.1 21.7 %collective-permute-done.44 = bf16[4,2,1,64,1024]{4,3,0,2,1:T(8,128)(2,1)} collective-permute-done((bf16[4,2,1,64,1024]{4,3,0,2,1:T(8,128)(2,1)}, bf16[4,2,1,64,1024]{4,3,0,2,1:T(8,128)(2,1)}, u32[]{:S(2)}, u32[]{:S(2)}) %collective-permute-start.44) | collective-permute-done | bytes 1048608 | tf_op jit(solution)/shard_map/ppermute | solution.py:36
  578.5 19.9 %collective-permute-done.46 = bf16[4,2,1,64,1024]{4,3,0,2,1:T(8,128)(2,1)S(1)} collective-permute-done((bf16[4,2,1,64,1024]{4,3,0,2,1:T(8,128)(2,1)S(1)}, bf16[4,2,1,64,1024]{4,3,0,2,1:T(8,128)(2,1)S(1)}, u32[]{:S(2)}, u32[]{:S(2)}) %collective-permute-start.46) | collective-permute-done | bytes 1048608 | tf_op jit(solution)/shard_map/ppermute | solution.py:36
  606.8 4.5 norm_back.9
  624.8 13.1 %collective-permute-done.59 = f32[592,128]{1,0:T(8,128)S(1)} collective-permute-done((f32[592,128]{1,0:T(8,128)S(1)}, f32[592,128]{1,0:T(8,128)S(1)}, u32[]{:S(2)}, u32[]{:S(2)}) %collective-permute-start.59) | collective-permute-done | bytes 303136 | tf_op jit(solution)/shard_map/ppermute | solution.py:36
  645.1 4.4 all-to-all-start.8
  667.6 18.3 %all-to-all-done.6 = bf16[4,64,2048]{2,1,0:T(8,128)(2,1)S(1)} async-done(((bf16[4,64,2048]{2,1,0:T(8,128)(2,1)}), bf16[4,64,2048]{2,1,0:T(8,128)(2,1)S(1)}, u32[]{:S(2)}, u32[]{:S(2)}) %all-to-all-start.6) | async-done | bytes 1048608 | tf_op jit(solution)/shard_map/all_to_all | solution.py:43
  693.2 21.4 %all-to-all-done.5 = bf16[4,64,2048]{2,1,0:T(8,128)(2,1)S(1)} async-done(((bf16[4,64,2048]{2,1,0:T(8,128)(2,1)}), bf16[4,64,2048]{2,1,0:T(8,128)(2,1)S(1)}, u32[]{:S(2)}, u32[]{:S(2)}) %all-to-all-start.5) | async-done | bytes 1048608 | tf_op jit(solution)/shard_map/all_to_all | solution.py:43
  726.6 34.9 %all-to-all-done.7 = bf16[4,64,3584]{2,1,0:T(8,128)(2,1)S(1)} async-done(((bf16[4,64,3584]{2,1,0:T(8,128)(2,1)}), bf16[4,64,3584]{2,1,0:T(8,128)(2,1)S(1)}, u32[]{:S(2)}, u32[]{:S(2)}) %all-to-all-start.7) | async-done | bytes 1835040 | tf_op jit(solution)/shard_map/all_to_all | solution.py:43
  (679 shorter events, 359.4 us)
Async XLA Ops:
  7.2 206.2 %all-gather.2.cloned.1.call-start = ((), (), s32[]{:S(2)}) async-start(), calls=%async_computation.11 | async-start | bytes 7798784 | tf_op jit(solution)/shard_map/all_gather | solution.py:671
  58.5 28.0 %collective-permute-start.1 = (bf16[4,1,1,64,1152]{4,3,0,2,1:T(8,128)(2,1)S(1)}, bf16[4,1,1,64,1152]{4,3,0,2,1:T(8,128)(2,1)}, u32[]{:S(2)}, u32[]{:S(2)}) collective-permute-start(bf16[4,1,1,64,1152]{4,3,0,2,1:T(8,128)(2,1)S(1)} %slice_bitcast_fusion), channel_id=1, source_target_pairs={{0,2},{2,0},{4,6},{6,4},{1,3},{3,1},{5,7},{7,5},{8,10},{10,8},{12,... | collective-permute-start | bytes 1769480 | tf_op jit(solution)/shard_map/ppermute | solution.py:36
  64.6 46.3 %all-to-all-start.1 = ((bf16[4,64,2048]{2,1,0:T(8,128)(2,1)}), bf16[4,64,2048]{2,1,0:T(8,128)(2,1)}, u32[]{:S(2)}, u32[]{:S(2)}) async-start(bf16[4,64,2048]{2,1,0:T(8,128)(2,1)} %broadcast_in_dim.57), calls=%async_computation.1 | async-start | bytes 2097152 | tf_op jit(solution)/shard_map/all_to_all | solution.py:43
  79.2 28.9 %collective-permute-start.5 = (bf16[4,2,1,64,1024]{4,3,0,2,1:T(8,128)(2,1)S(1)}, bf16[4,2,1,64,1024]{4,3,0,2,1:T(8,128)(2,1)S(1)}, u32[]{:S(2)}, u32[]{:S(2)}) collective-permute-start(bf16[4,2,1,64,1024]{4,3,0,2,1:T(8,128)(2,1)S(1)} %maximum_select_fusion.10), channel_id=1, source_target_pairs={{0,2},{2,0},{4,6},{6,4},{1,3},{3,1},{5,7},{7,5},{8,10},{10,8},{12,... | collective-permute-start | bytes 3145736 | tf_op jit(solution)/shard_map/ppermute | solution.py:36
  88.1 37.4 %collective-permute-start.2 = (bf16[4,1,2,64,1152]{4,3,0,2,1:T(8,128)(2,1)S(1)}, bf16[4,1,2,64,1152]{4,3,0,2,1:T(8,128)(2,1)}, u32[]{:S(2)}, u32[]{:S(2)}) collective-permute-start(bf16[4,1,2,64,1152]{4,3,0,2,1:T(8,128)(2,1)S(1)} %maximum_select_fusion.9), channel_id=1, source_target_pairs={{0,4},{2,6},{4,0},{6,2},{1,5},{3,7},{5,1},{7,3},{8,12},{10,14},{12... | collective-permute-start | bytes 3538952 | tf_op jit(solution)/shard_map/ppermute | solution.py:36
  113.2 32.1 %collective-permute-start.9 = (bf16[4,1,1,64,1024]{4,3,0,2,1:T(8,128)(2,1)}, bf16[4,1,1,64,1024]{4,3,0,2,1:T(8,128)(2,1)}, u32[]{:S(2)}, u32[]{:S(2)}) collective-permute-start(bf16[4,1,1,64,1024]{4,3,0,2,1:T(8,128)(2,1)} %get-tuple-element.149), channel_id=1, source_target_pairs={{0,4},{2,6},{4,0},{6,2},{1,5},{3,7},{5,1},{7,3},{8,12},{10,14},{12... | collective-permute-start | bytes 1572872 | tf_op jit(solution)/shard_map/ppermute | solution.py:36
  114.7 32.5 %collective-permute-start.7 = (bf16[4,1,1,64,1024]{4,3,0,2,1:T(8,128)(2,1)}, bf16[4,1,1,64,1024]{4,3,0,2,1:T(8,128)(2,1)}, u32[]{:S(2)}, u32[]{:S(2)}) collective-permute-start(bf16[4,1,1,64,1024]{4,3,0,2,1:T(8,128)(2,1)} %get-tuple-element.148), channel_id=1, source_target_pairs={{0,2},{2,0},{4,6},{6,4},{1,3},{3,1},{5,7},{7,5},{8,10},{10,8},{12,... | collective-permute-start | bytes 1572872 | tf_op jit(solution)/shard_map/ppermute | solution.py:36
  147.1 29.3 %collective-permute-start.10 = (bf16[4,2,1,64,1024]{4,3,0,2,1:T(8,128)(2,1)S(1)}, bf16[4,2,1,64,1024]{4,3,0,2,1:T(8,128)(2,1)}, u32[]{:S(2)}, u32[]{:S(2)}) collective-permute-start(bf16[4,2,1,64,1024]{4,3,0,2,1:T(8,128)(2,1)S(1)} %maximum_select_fusion.12), channel_id=1, source_target_pairs={{0,2},{2,0},{4,6},{6,4},{1,3},{3,1},{5,7},{7,5},{8,10},{10,8},{12,... | collective-permute-start | bytes 3145736 | tf_op jit(solution)/shard_map/ppermute | solution.py:36
  158.5 30.8 %all-to-all-start.2 = ((bf16[4,64,2048]{2,1,0:T(8,128)(2,1)}), bf16[4,64,2048]{2,1,0:T(8,128)(2,1)}, u32[]{:S(2)}, u32[]{:S(2)}) async-start(bf16[4,64,2048]{2,1,0:T(8,128)(2,1)} %broadcast_in_dim.105), calls=%async_computation.2 | async-start | bytes 2097152 | tf_op jit(solution)/shard_map/all_to_all | solution.py:43
  203.0 41.5 %all-to-all-start.3 = ((bf16[4,64,2048]{2,1,0:T(8,128)(2,1)}), bf16[4,64,2048]{2,1,0:T(8,128)(2,1)S(1)}, u32[]{:S(2)}, u32[]{:S(2)}) async-start(bf16[4,64,2048]{2,1,0:T(8,128)(2,1)} %broadcast_in_dim.106), calls=%async_computation.3 | async-start | bytes 2097152 | tf_op jit(solution)/shard_map/all_to_all | solution.py:43
  206.7 317.6 %reduce-scatter.3.cloned.1.call-start = ((), (), s32[]{:S(2)}) async-start(), calls=%async_computation.12 | async-start | bytes 10485760 | tf_op jit(solution)/shard_map/reduce_scatter | solution.py:789
  217.6 50.5 %collective-permute-start.17 = (bf16[512,1024]{1,0:T(8,128)(2,1)}, bf16[512,1024]{1,0:T(8,128)(2,1)}, u32[]{:S(2)}, u32[]{:S(2)}) collective-permute-start(bf16[512,1024]{1,0:T(8,128)(2,1)} %constant_dynamic-slice_fusion.27), channel_id=1, source_target_pairs={{0,1},{1,0},{2,3},{3,2},{4,5},{5,4},{6,7},{7,6},{8,9},{9,8},{10,11... | collective-permute-start | bytes 3145736 | tf_op jit(solution)/shard_map/ppermute | solution.py:33
  245.4 28.4 %collective-permute-start.20 = (bf16[4,1,1,64,1024]{4,3,0,2,1:T(8,128)(2,1)S(1)}, bf16[4,1,1,64,1024]{4,3,0,2,1:T(8,128)(2,1)}, u32[]{:S(2)}, u32[]{:S(2)}) collective-permute-start(bf16[4,1,1,64,1024]{4,3,0,2,1:T(8,128)(2,1)S(1)} %get-tuple-element.145), channel_id=1, source_target_pairs={{0,4},{2,6},{4,0},{6,2},{1,5},{3,7},{5,1},{7,3},{8,12},{10,14},{12... | collective-permute-start | bytes 1572872 | tf_op jit(solution)/shard_map/ppermute | solution.py:36
  288.8 40.1 %collective-permute-start.27 = (bf16[4,1,2,64,1024]{4,3,0,2,1:T(8,128)(2,1)}, bf16[4,1,2,64,1024]{4,3,0,2,1:T(8,128)(2,1)}, u32[]{:S(2)}, u32[]{:S(2)}) collective-permute-start(bf16[4,1,2,64,1024]{4,3,0,2,1:T(8,128)(2,1)} %maximum_select_fusion.16), channel_id=1, source_target_pairs={{0,4},{2,6},{4,0},{6,2},{1,5},{3,7},{5,1},{7,3},{8,12},{10,14},{12... | collective-permute-start | bytes 3145736 | tf_op jit(solution)/shard_map/ppermute | solution.py:36
  301.4 30.9 %collective-permute-start.30 = (bf16[4,2,1,64,1024]{4,3,0,2,1:T(8,128)(2,1)}, bf16[4,2,1,64,1024]{4,3,0,2,1:T(8,128)(2,1)}, u32[]{:S(2)}, u32[]{:S(2)}) collective-permute-start(bf16[4,2,1,64,1024]{4,3,0,2,1:T(8,128)(2,1)} %maximum_select_fusion.18), channel_id=1, source_target_pairs={{0,2},{2,0},{4,6},{6,4},{1,3},{3,1},{5,7},{7,5},{8,10},{10,8},{12,... | collective-permute-start | bytes 3145736 | tf_op jit(solution)/shard_map/ppermute | solution.py:36
  388.8 273.9 %reduce-scatter.5.cloned.1.call-start = ((), (), s32[]{:S(2)}) async-start(), calls=%async_computation.13 | async-start | bytes 9175040 | tf_op jit(solution)/shard_map/reduce_scatter | solution.py:789
  447.9 39.9 %collective-permute-start.56 = (bf16[512,512]{1,0:T(8,128)(2,1)}, bf16[512,512]{1,0:T(8,128)(2,1)S(1)}, u32[]{:S(2)}, u32[]{:S(2)}) collective-permute-start(bf16[512,512]{1,0:T(8,128)(2,1)} %get-tuple-element.139), channel_id=1, source_target_pairs={{0,1},{1,0},{2,3},{3,2},{4,5},{5,4},{6,7},{7,6},{8,9},{9,8},{10,11... | collective-permute-start | bytes 1572872 | tf_op jit(solution)/shard_map/ppermute | solution.py:33
  514.5 54.0 %collective-permute-start.45 = (bf16[4,1,2,64,1024]{4,3,0,2,1:T(8,128)(2,1)}, bf16[4,1,2,64,1024]{4,3,0,2,1:T(8,128)(2,1)}, u32[]{:S(2)}, u32[]{:S(2)}) collective-permute-start(bf16[4,1,2,64,1024]{4,3,0,2,1:T(8,128)(2,1)} %copy.218), channel_id=1, source_target_pairs={{0,4},{2,6},{4,0},{6,2},{1,5},{3,7},{5,1},{7,3},{8,12},{10,14},{12... | collective-permute-start | bytes 3145736 | tf_op jit(solution)/shard_map/ppermute | solution.py:36
  518.0 48.8 %collective-permute-start.44 = (bf16[4,2,1,64,1024]{4,3,0,2,1:T(8,128)(2,1)}, bf16[4,2,1,64,1024]{4,3,0,2,1:T(8,128)(2,1)}, u32[]{:S(2)}, u32[]{:S(2)}) collective-permute-start(bf16[4,2,1,64,1024]{4,3,0,2,1:T(8,128)(2,1)} %copy.217), channel_id=1, source_target_pairs={{0,2},{2,0},{4,6},{6,4},{1,3},{3,1},{5,7},{7,5},{8,10},{10,8},{12,... | collective-permute-start | bytes 3145736 | tf_op jit(solution)/shard_map/ppermute | solution.py:36
  527.4 75.8 %all-to-all-start.4 = ((bf16[4,64,4096]{2,1,0:T(8,128)(2,1)}), bf16[4,64,4096]{2,1,0:T(8,128)(2,1)S(1)}, u32[]{:S(2)}, u32[]{:S(2)}) async-start(bf16[4,64,4096]{2,1,0:T(8,128)(2,1)} %broadcast_select_fusion), calls=%async_computation.5 | async-start | bytes 4194304 | tf_op jit(solution)/shard_map/all_to_all | solution.py:43
  538.5 59.8 %collective-permute-start.46 = (bf16[4,2,1,64,1024]{4,3,0,2,1:T(8,128)(2,1)S(1)}, bf16[4,2,1,64,1024]{4,3,0,2,1:T(8,128)(2,1)S(1)}, u32[]{:S(2)}, u32[]{:S(2)}) collective-permute-start(bf16[4,2,1,64,1024]{4,3,0,2,1:T(8,128)(2,1)S(1)} %copy.220), channel_id=1, source_target_pairs={{0,2},{2,0},{4,6},{6,4},{1,3},{3,1},{5,7},{7,5},{8,10},{10,8},{12,... | collective-permute-start | bytes 3145736 | tf_op jit(solution)/shard_map/ppermute | solution.py:36
  543.3 63.4 %collective-permute-start.43 = (bf16[256,1024]{1,0:T(8,128)(2,1)}, bf16[256,1024]{1,0:T(8,128)(2,1)}, u32[]{:S(2)}, u32[]{:S(2)}) collective-permute-start(bf16[256,1024]{1,0:T(8,128)(2,1)} %slice.704), channel_id=1, source_target_pairs={{0,1},{1,0},{2,3},{3,2},{4,5},{5,4},{6,7},{7,6},{8,9},{9,8},{10,11... | collective-permute-start | bytes 1572872 | tf_op jit(solution)/shard_map/ppermute | solution.py:33
  543.6 57.7 %collective-permute-start.48 = (bf16[4,1,2,64,1024]{4,3,0,2,1:T(8,128)(2,1)S(1)}, bf16[4,1,2,64,1024]{4,3,0,2,1:T(8,128)(2,1)S(1)}, u32[]{:S(2)}, u32[]{:S(2)}) collective-permute-start(bf16[4,1,2,64,1024]{4,3,0,2,1:T(8,128)(2,1)S(1)} %copy.222), channel_id=1, source_target_pairs={{0,4},{2,6},{4,0},{6,2},{1,5},{3,7},{5,1},{7,3},{8,12},{10,14},{12... | collective-permute-start | bytes 3145736 | tf_op jit(solution)/shard_map/ppermute | solution.py:36
  574.3 46.2 %collective-permute-start.52 = (bf16[4,1,1,64,1024]{4,3,2,1,0:T(8,128)(2,1)}, bf16[4,1,1,64,1024]{4,3,2,1,0:T(8,128)(2,1)}, u32[]{:S(2)}, u32[]{:S(2)}) collective-permute-start(bf16[4,1,1,64,1024]{4,3,2,1,0:T(8,128)(2,1)} %constant_dynamic-slice_fusion.13), channel_id=1, source_target_pairs={{0,4},{2,6},{4,0},{6,2},{1,5},{3,7},{5,1},{7,3},{8,12},{10,14},{12... | collective-permute-start | bytes 1572872 | tf_op jit(solution)/shard_map/ppermute | solution.py:36
  578.3 44.2 %collective-permute-start.53 = (bf16[4,1,1,64,1024]{4,3,0,2,1:T(8,128)(2,1)}, bf16[4,1,1,64,1024]{4,3,0,2,1:T(8,128)(2,1)}, u32[]{:S(2)}, u32[]{:S(2)}) collective-permute-start(bf16[4,1,1,64,1024]{4,3,0,2,1:T(8,128)(2,1)} %constant_dynamic-slice_fusion.11), channel_id=1, source_target_pairs={{0,2},{2,0},{4,6},{6,4},{1,3},{3,1},{5,7},{7,5},{8,10},{10,8},{12,... | collective-permute-start | bytes 1572872 | tf_op jit(solution)/shard_map/ppermute | solution.py:36
  599.7 39.9 %collective-permute-start.47 = (bf16[4,1,1,64,1024]{4,3,0,2,1:T(8,128)(2,1)}, bf16[4,1,1,64,1024]{4,3,0,2,1:T(8,128)(2,1)}, u32[]{:S(2)}, u32[]{:S(2)}) collective-permute-start(bf16[4,1,1,64,1024]{4,3,0,2,1:T(8,128)(2,1)} %constant_dynamic-slice_fusion.19), channel_id=1, source_target_pairs={{0,4},{2,6},{4,0},{6,2},{1,5},{3,7},{5,1},{7,3},{8,12},{10,14},{12... | collective-permute-start | bytes 1572872 | tf_op jit(solution)/shard_map/ppermute | solution.py:36
  602.8 46.8 %collective-permute-start.49 = (bf16[4,1,1,64,1024]{4,3,0,2,1:T(8,128)(2,1)}, bf16[4,1,1,64,1024]{4,3,0,2,1:T(8,128)(2,1)}, u32[]{:S(2)}, u32[]{:S(2)}) collective-permute-start(bf16[4,1,1,64,1024]{4,3,0,2,1:T(8,128)(2,1)} %constant_dynamic-slice_fusion.16), channel_id=1, source_target_pairs={{0,2},{2,0},{4,6},{6,4},{1,3},{3,1},{5,7},{7,5},{8,10},{10,8},{12,... | collective-permute-start | bytes 1572872 | tf_op jit(solution)/shard_map/ppermute | solution.py:36
  658.4 27.6 %all-to-all-start.6 = ((bf16[4,64,2048]{2,1,0:T(8,128)(2,1)}), bf16[4,64,2048]{2,1,0:T(8,128)(2,1)S(1)}, u32[]{:S(2)}, u32[]{:S(2)}) async-start(bf16[4,64,2048]{2,1,0:T(8,128)(2,1)} %maximum_select_fusion.20), calls=%async_computation.7 | async-start | bytes 2097152 | tf_op jit(solution)/shard_map/all_to_all | solution.py:43
  662.7 26.7 %collective-permute-start.51 = (f32[32,4096]{1,0:T(8,128)}, f32[32,4096]{1,0:T(8,128)}, u32[]{:S(2)}, u32[]{:S(2)}) collective-permute-start(f32[32,4096]{1,0:T(8,128)} %constant_dynamic-slice_fusion.14), channel_id=1, source_target_pairs={{0,1},{1,0},{2,3},{3,2},{4,5},{5,4},{6,7},{7,6},{8,9},{9,8},{10,11... | collective-permute-start | bytes 1572872 | tf_op jit(solution)/shard_map/ppermute | solution.py:33
  685.9 28.7 %all-to-all-start.5 = ((bf16[4,64,2048]{2,1,0:T(8,128)(2,1)}), bf16[4,64,2048]{2,1,0:T(8,128)(2,1)S(1)}, u32[]{:S(2)}, u32[]{:S(2)}) async-start(bf16[4,64,2048]{2,1,0:T(8,128)(2,1)} %maximum_select_fusion.19), calls=%async_computation.6 | async-start | bytes 2097152 | tf_op jit(solution)/shard_map/all_to_all | solution.py:43
  692.4 27.0 %collective-permute-start.61 = (f32[32,128]{1,0:T(8,128)S(1)}, f32[32,128]{1,0:T(8,128)S(1)}, u32[]{:S(2)}, u32[]{:S(2)}) collective-permute-start(f32[32,128]{1,0:T(8,128)S(1)} %constant_dynamic-slice_fusion.2), channel_id=1, source_target_pairs={{0,1},{1,0},{2,3},{3,2},{4,5},{5,4},{6,7},{7,6},{8,9},{9,8},{10,11... | collective-permute-start | bytes 49160 | tf_op jit(solution)/shard_map/ppermute | solution.py:33
  715.6 45.9 %all-to-all-start.7 = ((bf16[4,64,3584]{2,1,0:T(8,128)(2,1)}), bf16[4,64,3584]{2,1,0:T(8,128)(2,1)S(1)}, u32[]{:S(2)}, u32[]{:S(2)}) async-start(bf16[4,64,3584]{2,1,0:T(8,128)(2,1)} %broadcast_select_fusion.1), calls=%async_computation.9 | async-start | bytes 3670016 | tf_op jit(solution)/shard_map/all_to_all | solution.py:43
  (175 other events, 1075.3 us)
Sparse Core Ops, SparseCore 0:
  13.2 158.5 all-gather.1
  388.9 85.5 reduce-scatter.2
  496.4 125.5 reduce-scatter.4

commit v3 on v2

--- a/solution.py
+++ b/solution.py
@@ -93,7 +93,7 @@
     return current.reshape((part.shape[0], place.chips) + part.shape[1:])
 
 
-def scatter_plane(place, full, turn, marks):
+def scatter_plane(place, full, turn, waits, start):
     bits = place.bits
     current = full.reshape((full.shape[0],) + (2,) * bits + full.shape[2:])
     for step in range(bits):
@@ -102,8 +102,7 @@
         me = place.bit(bit)
         keep = lax.dynamic_slice_in_dim(current, me, 1, axis)
         sent = lax.dynamic_slice_in_dim(current, 1 - me, 1, axis)
-        got = place.hop(sent, bit)
-        marks.append(tip(got))
+        got = place.hop(tie(sent, *(waits if step == 1 else start if step == 0 else ())), bit)
         current = (keep.astype(F32) + got.astype(F32)).astype(full.dtype)
     return current.reshape((full.shape[0],) + full.shape[2:])
 
@@ -397,7 +396,7 @@
 
 
 def row_specs(dim):
-    step = 64
+    step = 128
     rows = pl.BlockSpec((step, dim), lambda i: (i, 0))
     first = pl.BlockSpec((1, step, dim), lambda i: (0, i, 0))
     line = pl.BlockSpec((1, dim), lambda i: (0, 0))
@@ -783,18 +782,17 @@
     def summed(terms):
         return jnp.sum(place.swap_seq(terms).astype(F32), 0)
 
-    def scatter_early(terms, after):
+    def scatter_early(terms):
         terms = jnp.concatenate(terms, 1)
         terms = row_major(terms.reshape(seq_size, chips * rows, terms.shape[1]))
-        part = lax.psum_scatter(terms, "plane", scatter_dimension=1, tiled=True)
-        return summed(tie(row_major(part), after))
-
-    def plane_sums(pair):
-        parts, marks = [], []
+        return row_major(lax.psum_scatter(terms, "plane", scatter_dimension=1, tiled=True))
+
+    def plane_sums(pair, waits=(), start=()):
+        parts = []
         for turn, terms in enumerate(pair):
             blocks = terms.reshape(seq_size, chips, rows, -1)
-            parts.append(scatter_plane(place, blocks, turn, marks))
-        return jnp.concatenate(parts, -1), marks[:: place.bits]
+            parts.append(scatter_plane(place, blocks, turn, waits, start))
+        return jnp.concatenate(parts, -1)
 
     gain_grads = [None] * 6
     bias_grads = [None] * 6
@@ -850,7 +848,7 @@
     query_grad, key_grad, value_grad, kl, vl, kr, vr, relative_grad = attend_back(
         projected, from_left, from_right, relative, attended_grad, probs
     )
-    second_sum = scatter_early(second_terms, tip(query_grad))
+    second_sum = summed(tie(scatter_early(second_terms), tip(query_grad)))
     to_left = place.along(jnp.concatenate([kl, vl], 2), -1).astype(F32)
     to_right = place.along(jnp.concatenate([kr[:, :RIGHT], vr[:, :RIGHT]], 2), 1).astype(F32)
     own_grad = (
@@ -867,16 +865,11 @@
     branch, pre_grads, acts, normed_low, branch_grad = feed_back(low, 0, ffn_first)
     downs = [dot(branch_grad, acts[part], 0, 0).astype(BF) for part in range(2)]
     ins = [dot(normed_low, pre_grads[part], 0, 0).astype(BF) for part in range(2)]
-    down_part, down_marks = plane_sums(downs)
-    in_part, _ = plane_sums(ins)
-    grad_input, _ = back_to(
-        0, stream, branch, grad_ffn_out, 1.0, *down_marks, tip(second_sum)
-    )
-    down_sum = summed(tie(down_part, tip(grad_input)))
-    in_sum = summed(tie(in_part, tip(grad_input)))
-    attention_sum = scatter_early(
-        [qkv_terms, conv_in_terms, out_terms, conv_out_terms], tip(grad_input)
-    )
+    attention_part = scatter_early([qkv_terms, conv_in_terms, out_terms, conv_out_terms])
+    grad_input, _ = back_to(0, stream, branch, grad_ffn_out, 1.0)
+    down_part = plane_sums(downs, (tip(ins[1]), tip(grad_input)))
+    in_part = plane_sums(ins, start=(tip(down_part),))
+    down_sum = summed(tie(down_part, tip(second_sum)))
     offsets = LEFT + RIGHT + 1
     relative_grad = relative_grad[:offsets, :HEAD_DIM] + relative_grad[:offsets, HEAD_DIM:]
 
@@ -902,8 +895,10 @@
         rel_part = rel_part + got[-rel_part.shape[0] :]
     rel_all = jnp.broadcast_to(rel_part[None], (seq_size,) + rel_part.shape)
     small_total = summed(
-        jnp.concatenate([current.reshape(seq_size, rows, 128), rel_all], 1)
-    )
+        tie(jnp.concatenate([current.reshape(seq_size, rows, 128), rel_all], 1), tip(down_sum))
+    )
+    attention_sum = summed(tie(attention_part, tip(small_total)))
+    in_sum = summed(tie(in_part, tip(attention_sum)))
     rel_total = small_total[rows : rows + offsets, :HEAD_DIM]
     small_total = small_total[:rows]
     small_sum = place.core_part(small_total, 0, core) + place.sibling(
@@ -924,10 +919,10 @@
         return results
 
     in_second, down_second = own_rows(second_sum, [(1, hid), (1, hid)])
+    (down_first,) = own_rows(down_sum, [(1, hid)])
     qkv_sum, first_sum, out_sum, second_sum = own_rows(
         attention_sum, [(3, 3 * width), (2, 2 * width), (1, width), (1, width)]
     )
-    (down_first,) = own_rows(down_sum, [(1, hid)])
     (in_first,) = own_rows(in_sum, [(1, hid)])
     return (
         outputs,

time: 785 us -> 766 us (0.976)
  waiting for transfers between devices: 244 us -> 231 us
  Pallas kernels: 116 us -> 104 us
    all_to_all x8, waiting for transfers between devices: 76.6 us -> 58.2 us  [swap_seq(): return lax.all_to_all(blocks, 'seq', 0, 0, tiled=True)]
    unnamed x297 -> x285, local copies, waits for them, and re-layouts: 31.2 us -> 29 us
  transfers between devices with their start and end apart: 73 -> 73, of which waited for: 33 -> 36; matrix products, arithmetic and copies ran while one was open for 26% -> 27% of each run, Pallas kernels for 12% -> 11%
where the time goes in v3:
time: 766 us; the launch traced here: 757 us
  waiting for transfers between devices  231 us (30%)
  Pallas kernels  104 us (14%)
  starting transfers between devices  90.4 us (12%)
  other arithmetic  88.1 us (12%)
  local copies, waits for them, and re-layouts  86.7 us (11%)
  matrix products  72.8 us (10%)
  blocking collectives  43.3 us (6%)
  between operations  40.3 us (5%)
    ppermute x26, waiting for transfers between devices, hop(): lax.ppermute(shard, 'plane', [(i, i ^ 1 << bit) for i in range(self.chips)])  145 us
    dot_general x32, matrix products, dot(): lax.dot_general(left, right, (((left_axis,), (right_axis,)), ((), ())), p...  72.8 us
    all_to_all x8, waiting for transfers between devices, swap_seq(): return lax.all_to_all(blocks, 'seq', 0, 0, tiled=True)  58.2 us
    all_to_all x1, blocking collectives, swap_seq(): return lax.all_to_all(blocks, 'seq', 0, 0, tiled=True)  43.3 us
    all_to_all x8, starting transfers between devices, swap_seq(): return lax.all_to_all(blocks, 'seq', 0, 0, tiled=True)  36.2 us
    ppermute x26, starting transfers between devices, hop(): lax.ppermute(shard, 'plane', [(i, i ^ 1 << bit) for i in range(self.chips)])  33.4 us
    select_n x16, other arithmetic, gather_plane(): jnp.where(place.bit(bit) == 0, jnp.concatenate([current, other], axis), j...  31.6 us
    unnamed x285, local copies, waits for them, and re-layouts  29 us
  transfers between devices with their start and end apart: 73, of which 36 were waited for; matrix products, arithmetic and copies ran while one was open for 27% of the time, Pallas kernels for 11%

profile of v3, /device:TPU:0, one launch (start us, length us, event | category | flops | bytes accessed | tf_op | source)
XLA Modules:
  0.0 756.7 jit_solution(11013855782997567868)
XLA Ops:
  15.2 43.3 %all_to_all.45 = bf16[4,64,2176]{2,1,0:T(8,128)(2,1)S(1)} all-to-all(bf16[4,64,2176]{2,1,0:T(8,128)(2,1)S(1)} %broadcast_in_dim.112), channel_id=1, replica_groups=mesh['seq'=4,'plane'=4,'core'=2] {'seq'}, dimensions={0} | all-to-all | bytes 2228224 | tf_op jit(solution)/shard_map/all_to_all | solution.py:43
  64.7 4.3 all-to-all-start.1
  69.0 8.9 %collective-permute-done.4 = bf16[4,1,1,64,1024]{4,3,0,2,1:T(8,128)(2,1)} collective-permute-done((bf16[4,1,1,64,1024]{4,3,0,2,1:T(8,128)(2,1)S(1)}, bf16[4,1,1,64,1024]{4,3,0,2,1:T(8,128)(2,1)}, u32[]{:S(2)}, u32[]{:S(2)}) %collective-permute-start.4) | collective-permute-done | bytes 524320 | tf_op jit(solution)/shard_map/ppermute | solution.py:36
  80.8 5.7 collective-permute-done.1
  90.7 17.5 %collective-permute-done.5 = bf16[4,2,1,64,1024]{4,3,0,2,1:T(8,128)(2,1)S(1)} collective-permute-done((bf16[4,2,1,64,1024]{4,3,0,2,1:T(8,128)(2,1)S(1)}, bf16[4,2,1,64,1024]{4,3,0,2,1:T(8,128)(2,1)S(1)}, u32[]{:S(2)}, u32[]{:S(2)}) %collective-permute-start.5) | collective-permute-done | bytes 1048608 | tf_op jit(solution)/shard_map/ppermute | solution.py:36
  115.3 10.0 %collective-permute-done.2 = bf16[4,1,2,64,1152]{4,3,0,2,1:T(8,128)(2,1)} collective-permute-done((bf16[4,1,2,64,1152]{4,3,0,2,1:T(8,128)(2,1)S(1)}, bf16[4,1,2,64,1152]{4,3,0,2,1:T(8,128)(2,1)}, u32[]{:S(2)}, u32[]{:S(2)}) %collective-permute-start.2) | collective-permute-done | bytes 1179680 | tf_op jit(solution)/shard_map/ppermute | solution.py:36
  140.6 4.5 collective-permute-done.9
  158.1 4.4 all-to-all-start.2
  162.6 11.6 %collective-permute-done.8 = bf16[4,1,2,64,1024]{4,3,0,2,1:T(8,128)(2,1)} collective-permute-done((bf16[4,1,2,64,1024]{4,3,0,2,1:T(8,128)(2,1)S(1)}, bf16[4,1,2,64,1024]{4,3,0,2,1:T(8,128)(2,1)}, u32[]{:S(2)}, u32[]{:S(2)}) %collective-permute-start.8) | collective-permute-done | bytes 1048608 | tf_op jit(solution)/shard_map/ppermute | solution.py:36
  207.7 4.2 collective-permute-start.19
  222.1 12.3 %collective-permute-done.19 = bf16[4,2,1,64,1024]{4,3,0,2,1:T(8,128)(2,1)S(1)} collective-permute-done((bf16[4,2,1,64,1024]{4,3,0,2,1:T(8,128)(2,1)S(1)}, bf16[4,2,1,64,1024]{4,3,0,2,1:T(8,128)(2,1)S(1)}, u32[]{:S(2)}, u32[]{:S(2)}) %collective-permute-start.19) | collective-permute-done | bytes 1048608 | tf_op jit(solution)/shard_map/ppermute | solution.py:36
  253.0 14.8 %attend.1 = (bf16[2,256,512]{2,1,0:T(8,128)(2,1)}, bf16[2,4,2,2,128,256]{5,4,3,2,1,0:T(8,128)(2,1)}) custom-call(s32[2,3]{1,0:T(2,128)} %copy.168.ends_ref, s32[1]{0:T(128)S(6)} %select_n.665.base_ref, bf16[2,256,1536]{2,1,0:T(8,128)(2,1)} %bitcast.262, bf16[2,256,1536]{2,1,0:T(8,128)(2,1)} %bitcast.263, bf16[2,256,1536]{2,1,0:T(8,128)(2,1)} %bitcast.264, ...), custom_call_target="tpu_custom_call" | custom-call | tf_op jit(solution)/shard_map/attend/pallas_call | solution.py:269
  282.1 4.1 collective-permute-done.26
  303.4 8.3 %taps.1 = f32[2,256,512]{2,1,0:T(8,128)} custom-call(s32[2,3]{1,0:T(2,128)} %copy.168.ends_ref, s32[1]{0:T(128)} %bitcast.41.base_ref, bf16[2,32,512]{2,1,0:T(8,128)(2,1)} %copy-done.93, bf16[2,256,512]{2,1,0:T(8,128)(2,1)} %copy-done.5, f32[32,512]{1,0:T(8,128)} %pad.54.taps_ref), custom_call_target="tpu_custom_call" | custom-call | tf_op jit(solution)/shard_map/taps/pallas_call | solution.py:560
  334.8 7.8 %collective-permute-done.29 = bf16[4,1,2,64,1024]{4,3,0,2,1:T(8,128)(2,1)} collective-permute-done((bf16[4,1,2,64,1024]{4,3,0,2,1:T(8,128)(2,1)S(1)}, bf16[4,1,2,64,1024]{4,3,0,2,1:T(8,128)(2,1)}, u32[]{:S(2)}, u32[]{:S(2)}) %collective-permute-start.29) | collective-permute-done | bytes 1048608 | tf_op jit(solution)/shard_map/ppermute | solution.py:36
  367.5 4.6 multiply_convert_fusion.3.refs_0_
  374.6 11.5 %products.1 = bf16[1024,4096]{1,0:T(8,128)(2,1)} custom-call(bf16[512,1024]{1,0:T(8,128)(2,1)} %bitcast.272, bf16[512,1024]{1,0:T(8,128)(2,1)} %bitcast.275, bf16[512,1024]{1,0:T(8,128)(2,1)} %multiply_convert_fusion.3.refs_0_, bf16[512,1024]{1,0:T(8,128)(2,1)} %multiply_convert_fusion.2.refs_1_, bf16[512,1024]{1,0:T(8,128)(2,1)} %copy-done.54, ...), custom_call_target="tpu_custom_call" | custom-call | tf_op jit(solution)/shard_map/products/pallas_call | solution.py:342
  406.4 15.4 %taps_back.1 = (f32[2,256,512]{2,1,0:T(8,128)}, bf16[2,32,512]{2,1,0:T(8,128)(2,1)}, f32[32,512]{1,0:T(8,128)}, f32[1,512]{1,0:T(1,128)}, f32[1,512]{1,0:T(1,128)}) custom-call(s32[2,3]{1,0:T(2,128)} %copy.168.ends_ref, s32[1]{0:T(128)} %bitcast.41.base_ref, bf16[2,32,512]{2,1,0:T(8,128)(2,1)} %copy-done.93, bf16[2,256,512]{2,1,0:T(8,128)(2,1)} %copy-done.5, ...), custom_call_target="tpu_custom_call" | custom-call | tf_op jit(solution)/shard_map/taps_back/pallas_call | solution.py:578
  423.2 5.5 collective-permute-done.36
  448.5 23.5 %attend_back.1 = (bf16[2,256,512]{2,1,0:T(8,128)(2,1)}, f32[2,256,512]{2,1,0:T(8,128)}, f32[2,256,512]{2,1,0:T(8,128)}, bf16[2,64,512]{2,1,0:T(8,128)(2,1)}, bf1...) custom-call(bf16[2,256,1536]{2,1,0:T(8,128)(2,1)} %bitcast.265, ...), custom_call_target="tpu_custom_call" | custom-call | tf_op jit(solution)/shard_map/attend_back/pallas_call | solution.py:292
  478.4 4.3 collective-permute-start.40
  535.1 6.0 all-to-all-start.4
  554.6 15.3 %collective-permute-done.49 = f32[592,128]{1,0:T(8,128)S(1)} collective-permute-done((f32[592,128]{1,0:T(8,128)S(1)}, f32[592,128]{1,0:T(8,128)S(1)}, u32[]{:S(2)}, u32[]{:S(2)}) %collective-permute-start.49) | collective-permute-done | bytes 303136 | tf_op jit(solution)/shard_map/ppermute | solution.py:36
  573.2 7.9 %collective-permute-done.46 = bf16[4,1,2,64,1024]{4,3,0,2,1:T(8,128)(2,1)S(1)} collective-permute-done((bf16[4,1,2,64,1024]{4,3,0,2,1:T(8,128)(2,1)S(1)}, bf16[4,1,2,64,1024]{4,3,0,2,1:T(8,128)(2,1)S(1)}, u32[]{:S(2)}, u32[]{:S(2)}) %collective-permute-start.46) | collective-permute-done | bytes 1048608 | tf_op jit(solution)/shard_map/ppermute | solution.py:36
  582.1 19.9 %collective-permute-done.45 = bf16[4,1,1,64,1024]{4,3,0,2,1:T(8,128)(2,1)S(1)} collective-permute-done((bf16[4,1,1,64,1024]{4,3,0,2,1:T(8,128)(2,1)S(1)}, bf16[4,1,1,64,1024]{4,3,0,2,1:T(8,128)(2,1)S(1)}, u32[]{:S(2)}, u32[]{:S(2)}) %collective-permute-start.45) | collective-permute-done | bytes 524320 | tf_op jit(solution)/shard_map/ppermute | solution.py:36
  613.5 5.3 all-to-all-start.5
  618.8 7.0 collective-permute-done.53
  629.7 6.5 collective-permute-done.55
  651.7 5.3 all-to-all-start.6
  658.6 5.5 all-to-all-done.6
  677.6 34.2 %all-to-all-done.7 = bf16[4,64,3584]{2,1,0:T(8,128)(2,1)S(1)} async-done(((bf16[4,64,3584]{2,1,0:T(8,128)(2,1)}), bf16[4,64,3584]{2,1,0:T(8,128)(2,1)S(1)}, u32[]{:S(2)}, u32[]{:S(2)}) %all-to-all-start.7) | async-done | bytes 1835040 | tf_op jit(solution)/shard_map/all_to_all | solution.py:43
  726.3 18.5 %all-to-all-done.8 = bf16[4,64,2048]{2,1,0:T(8,128)(2,1)S(1)} async-done(((bf16[4,64,2048]{2,1,0:T(8,128)(2,1)}), bf16[4,64,2048]{2,1,0:T(8,128)(2,1)S(1)}, u32[]{:S(2)}, u32[]{:S(2)}) %all-to-all-start.8) | async-done | bytes 1048608 | tf_op jit(solution)/shard_map/all_to_all | solution.py:43
  (670 shorter events, 358.3 us)
Async XLA Ops:
  7.2 206.1 %all-gather.2.cloned.1.call-start = ((), (), s32[]{:S(2)}) async-start(), calls=%async_computation.11 | async-start | bytes 7798784 | tf_op jit(solution)/shard_map/all_gather | solution.py:670
  58.5 28.0 %collective-permute-start.1 = (bf16[4,1,1,64,1152]{4,3,0,2,1:T(8,128)(2,1)S(1)}, bf16[4,1,1,64,1152]{4,3,0,2,1:T(8,128)(2,1)}, u32[]{:S(2)}, u32[]{:S(2)}) collective-permute-start(bf16[4,1,1,64,1152]{4,3,0,2,1:T(8,128)(2,1)S(1)} %slice_bitcast_fusion), channel_id=1, source_target_pairs={{0,2},{2,0},{4,6},{6,4},{1,3},{3,1},{5,7},{7,5},{8,10},{10,8},{12,... | collective-permute-start | bytes 1769480 | tf_op jit(solution)/shard_map/ppermute | solution.py:36
  64.7 46.3 %all-to-all-start.1 = ((bf16[4,64,2048]{2,1,0:T(8,128)(2,1)}), bf16[4,64,2048]{2,1,0:T(8,128)(2,1)}, u32[]{:S(2)}, u32[]{:S(2)}) async-start(bf16[4,64,2048]{2,1,0:T(8,128)(2,1)} %broadcast_in_dim.113), calls=%async_computation.1 | async-start | bytes 2097152 | tf_op jit(solution)/shard_map/all_to_all | solution.py:43
  79.3 28.9 %collective-permute-start.5 = (bf16[4,2,1,64,1024]{4,3,0,2,1:T(8,128)(2,1)S(1)}, bf16[4,2,1,64,1024]{4,3,0,2,1:T(8,128)(2,1)S(1)}, u32[]{:S(2)}, u32[]{:S(2)}) collective-permute-start(bf16[4,2,1,64,1024]{4,3,0,2,1:T(8,128)(2,1)S(1)} %maximum_select_fusion.10), channel_id=1, source_target_pairs={{0,2},{2,0},{4,6},{6,4},{1,3},{3,1},{5,7},{7,5},{8,10},{10,8},{12,... | collective-permute-start | bytes 3145736 | tf_op jit(solution)/shard_map/ppermute | solution.py:36
  88.0 37.3 %collective-permute-start.2 = (bf16[4,1,2,64,1152]{4,3,0,2,1:T(8,128)(2,1)S(1)}, bf16[4,1,2,64,1152]{4,3,0,2,1:T(8,128)(2,1)}, u32[]{:S(2)}, u32[]{:S(2)}) collective-permute-start(bf16[4,1,2,64,1152]{4,3,0,2,1:T(8,128)(2,1)S(1)} %maximum_select_fusion.9), channel_id=1, source_target_pairs={{0,4},{2,6},{4,0},{6,2},{1,5},{3,7},{5,1},{7,3},{8,12},{10,14},{12... | collective-permute-start | bytes 3538952 | tf_op jit(solution)/shard_map/ppermute | solution.py:36
  113.2 31.9 %collective-permute-start.9 = (bf16[4,1,1,64,1024]{4,3,0,2,1:T(8,128)(2,1)}, bf16[4,1,1,64,1024]{4,3,0,2,1:T(8,128)(2,1)}, u32[]{:S(2)}, u32[]{:S(2)}) collective-permute-start(bf16[4,1,1,64,1024]{4,3,0,2,1:T(8,128)(2,1)} %get-tuple-element.149), channel_id=1, source_target_pairs={{0,4},{2,6},{4,0},{6,2},{1,5},{3,7},{5,1},{7,3},{8,12},{10,14},{12... | collective-permute-start | bytes 1572872 | tf_op jit(solution)/shard_map/ppermute | solution.py:36
  114.7 32.3 %collective-permute-start.7 = (bf16[4,1,1,64,1024]{4,3,0,2,1:T(8,128)(2,1)}, bf16[4,1,1,64,1024]{4,3,0,2,1:T(8,128)(2,1)}, u32[]{:S(2)}, u32[]{:S(2)}) collective-permute-start(bf16[4,1,1,64,1024]{4,3,0,2,1:T(8,128)(2,1)} %get-tuple-element.148), channel_id=1, source_target_pairs={{0,2},{2,0},{4,6},{6,4},{1,3},{3,1},{5,7},{7,5},{8,10},{10,8},{12,... | collective-permute-start | bytes 1572872 | tf_op jit(solution)/shard_map/ppermute | solution.py:36
  146.9 29.4 %collective-permute-start.10 = (bf16[4,2,1,64,1024]{4,3,0,2,1:T(8,128)(2,1)S(1)}, bf16[4,2,1,64,1024]{4,3,0,2,1:T(8,128)(2,1)}, u32[]{:S(2)}, u32[]{:S(2)}) collective-permute-start(bf16[4,2,1,64,1024]{4,3,0,2,1:T(8,128)(2,1)S(1)} %maximum_select_fusion.12), channel_id=1, source_target_pairs={{0,2},{2,0},{4,6},{6,4},{1,3},{3,1},{5,7},{7,5},{8,10},{10,8},{12,... | collective-permute-start | bytes 3145736 | tf_op jit(solution)/shard_map/ppermute | solution.py:36
  148.8 25.3 %collective-permute-start.8 = (bf16[4,1,2,64,1024]{4,3,0,2,1:T(8,128)(2,1)S(1)}, bf16[4,1,2,64,1024]{4,3,0,2,1:T(8,128)(2,1)}, u32[]{:S(2)}, u32[]{:S(2)}) collective-permute-start(bf16[4,1,2,64,1024]{4,3,0,2,1:T(8,128)(2,1)S(1)} %maximum_select_fusion.11), channel_id=1, source_target_pairs={{0,4},{2,6},{4,0},{6,2},{1,5},{3,7},{5,1},{7,3},{8,12},{10,14},{12... | collective-permute-start | bytes 3145736 | tf_op jit(solution)/shard_map/ppermute | solution.py:36
  158.1 31.0 %all-to-all-start.2 = ((bf16[4,64,2048]{2,1,0:T(8,128)(2,1)}), bf16[4,64,2048]{2,1,0:T(8,128)(2,1)}, u32[]{:S(2)}, u32[]{:S(2)}) async-start(bf16[4,64,2048]{2,1,0:T(8,128)(2,1)} %broadcast_in_dim.117), calls=%async_computation.2 | async-start | bytes 2097152 | tf_op jit(solution)/shard_map/all_to_all | solution.py:43
  201.8 42.5 %all-to-all-start.3 = ((bf16[4,64,2048]{2,1,0:T(8,128)(2,1)}), bf16[4,64,2048]{2,1,0:T(8,128)(2,1)S(1)}, u32[]{:S(2)}, u32[]{:S(2)}) async-start(bf16[4,64,2048]{2,1,0:T(8,128)(2,1)} %broadcast_in_dim.118), calls=%async_computation.3 | async-start | bytes 2097152 | tf_op jit(solution)/shard_map/all_to_all | solution.py:43
  205.5 326.6 %reduce-scatter.3.cloned.1.call-start = ((), (), s32[]{:S(2)}) async-start(), calls=%async_computation.12 | async-start | bytes 10485760 | tf_op jit(solution)/shard_map/reduce_scatter | solution.py:788
  207.7 26.7 %collective-permute-start.19 = (bf16[4,2,1,64,1024]{4,3,0,2,1:T(8,128)(2,1)S(1)}, bf16[4,2,1,64,1024]{4,3,0,2,1:T(8,128)(2,1)S(1)}, u32[]{:S(2)}, u32[]{:S(2)}) collective-permute-start(bf16[4,2,1,64,1024]{4,3,0,2,1:T(8,128)(2,1)S(1)} %maximum_select_fusion.14), channel_id=1, source_target_pairs={{0,2},{2,0},{4,6},{6,4},{1,3},{3,1},{5,7},{7,5},{8,10},{10,8},{12,... | collective-permute-start | bytes 3145736 | tf_op jit(solution)/shard_map/ppermute | solution.py:36
  217.5 50.3 %collective-permute-start.17 = (bf16[512,1024]{1,0:T(8,128)(2,1)}, bf16[512,1024]{1,0:T(8,128)(2,1)}, u32[]{:S(2)}, u32[]{:S(2)}) collective-permute-start(bf16[512,1024]{1,0:T(8,128)(2,1)} %constant_dynamic-slice_fusion.24), channel_id=1, source_target_pairs={{0,1},{1,0},{2,3},{3,2},{4,5},{5,4},{6,7},{7,6},{8,9},{9,8},{10,11... | collective-permute-start | bytes 3145736 | tf_op jit(solution)/shard_map/ppermute | solution.py:33
  245.2 28.3 %collective-permute-start.20 = (bf16[4,1,1,64,1024]{4,3,0,2,1:T(8,128)(2,1)S(1)}, bf16[4,1,1,64,1024]{4,3,0,2,1:T(8,128)(2,1)}, u32[]{:S(2)}, u32[]{:S(2)}) collective-permute-start(bf16[4,1,1,64,1024]{4,3,0,2,1:T(8,128)(2,1)S(1)} %get-tuple-element.145), channel_id=1, source_target_pairs={{0,4},{2,6},{4,0},{6,2},{1,5},{3,7},{5,1},{7,3},{8,12},{10,14},{12... | collective-permute-start | bytes 1572872 | tf_op jit(solution)/shard_map/ppermute | solution.py:36
  288.5 38.9 %collective-permute-start.27 = (bf16[4,1,2,64,1024]{4,3,0,2,1:T(8,128)(2,1)}, bf16[4,1,2,64,1024]{4,3,0,2,1:T(8,128)(2,1)}, u32[]{:S(2)}, u32[]{:S(2)}) collective-permute-start(bf16[4,1,2,64,1024]{4,3,0,2,1:T(8,128)(2,1)} %maximum_select_fusion.16), channel_id=1, source_target_pairs={{0,4},{2,6},{4,0},{6,2},{1,5},{3,7},{5,1},{7,3},{8,12},{10,14},{12... | collective-permute-start | bytes 3145736 | tf_op jit(solution)/shard_map/ppermute | solution.py:36
  290.0 25.6 %collective-permute-start.28 = (bf16[4,1,1,64,1024]{4,3,0,2,1:T(8,128)(2,1)}, bf16[4,1,1,64,1024]{4,3,0,2,1:T(8,128)(2,1)}, u32[]{:S(2)}, u32[]{:S(2)}) collective-permute-start(bf16[4,1,1,64,1024]{4,3,0,2,1:T(8,128)(2,1)} %get-tuple-element.144), channel_id=1, source_target_pairs={{0,2},{2,0},{4,6},{6,4},{1,3},{3,1},{5,7},{7,5},{8,10},{10,8},{12,... | collective-permute-start | bytes 1572872 | tf_op jit(solution)/shard_map/ppermute | solution.py:36
  301.1 29.6 %collective-permute-start.30 = (bf16[4,2,1,64,1024]{4,3,0,2,1:T(8,128)(2,1)}, bf16[4,2,1,64,1024]{4,3,0,2,1:T(8,128)(2,1)}, u32[]{:S(2)}, u32[]{:S(2)}) collective-permute-start(bf16[4,2,1,64,1024]{4,3,0,2,1:T(8,128)(2,1)} %maximum_select_fusion.18), channel_id=1, source_target_pairs={{0,2},{2,0},{4,6},{6,4},{1,3},{3,1},{5,7},{7,5},{8,10},{10,8},{12,... | collective-permute-start | bytes 3145736 | tf_op jit(solution)/shard_map/ppermute | solution.py:36
  317.4 25.3 %collective-permute-start.29 = (bf16[4,1,2,64,1024]{4,3,0,2,1:T(8,128)(2,1)S(1)}, bf16[4,1,2,64,1024]{4,3,0,2,1:T(8,128)(2,1)}, u32[]{:S(2)}, u32[]{:S(2)}) collective-permute-start(bf16[4,1,2,64,1024]{4,3,0,2,1:T(8,128)(2,1)S(1)} %maximum_select_fusion.17), channel_id=1, source_target_pairs={{0,4},{2,6},{4,0},{6,2},{1,5},{3,7},{5,1},{7,3},{8,12},{10,14},{12... | collective-permute-start | bytes 3145736 | tf_op jit(solution)/shard_map/ppermute | solution.py:36
  386.2 279.7 %reduce-scatter.5.cloned.1.call-start = ((), (), s32[]{:S(2)}) async-start(), calls=%async_computation.13 | async-start | bytes 9175040 | tf_op jit(solution)/shard_map/reduce_scatter | solution.py:788
  443.2 39.5 %collective-permute-start.52 = (bf16[512,512]{1,0:T(8,128)(2,1)}, bf16[512,512]{1,0:T(8,128)(2,1)S(1)}, u32[]{:S(2)}, u32[]{:S(2)}) collective-permute-start(bf16[512,512]{1,0:T(8,128)(2,1)} %get-tuple-element.141), channel_id=1, source_target_pairs={{0,1},{1,0},{2,3},{3,2},{4,5},{5,4},{6,7},{7,6},{8,9},{9,8},{10,11... | collective-permute-start | bytes 1572872 | tf_op jit(solution)/shard_map/ppermute | solution.py:33
  518.1 51.9 %collective-permute-start.44 = (bf16[4,2,1,64,1024]{4,3,0,2,1:T(8,128)(2,1)}, bf16[4,2,1,64,1024]{4,3,0,2,1:T(8,128)(2,1)}, u32[]{:S(2)}, u32[]{:S(2)}) collective-permute-start(bf16[4,2,1,64,1024]{4,3,0,2,1:T(8,128)(2,1)} %copy.208), channel_id=1, source_target_pairs={{0,2},{2,0},{4,6},{6,4},{1,3},{3,1},{5,7},{7,5},{8,10},{10,8},{12,... | collective-permute-start | bytes 3145736 | tf_op jit(solution)/shard_map/ppermute | solution.py:36
  535.1 75.1 %all-to-all-start.4 = ((bf16[4,64,4096]{2,1,0:T(8,128)(2,1)}), bf16[4,64,4096]{2,1,0:T(8,128)(2,1)S(1)}, u32[]{:S(2)}, u32[]{:S(2)}) async-start(bf16[4,64,4096]{2,1,0:T(8,128)(2,1)} %broadcast_select_fusion), calls=%async_computation.5 | async-start | bytes 4194304 | tf_op jit(solution)/shard_map/all_to_all | solution.py:43
  545.0 24.9 %collective-permute-start.49 = (f32[592,128]{1,0:T(8,128)S(1)}, f32[592,128]{1,0:T(8,128)S(1)}, u32[]{:S(2)}, u32[]{:S(2)}) collective-permute-start(f32[592,128]{1,0:T(8,128)S(1)} %pad_maximum_fusion.14), channel_id=1, source_target_pairs={{0,2},{2,0},{4,6},{6,4},{1,3},{3,1},{5,7},{7,5},{8,10},{10,8},{12,... | collective-permute-start | bytes 909320 | tf_op jit(solution)/shard_map/ppermute | solution.py:36
  548.1 33.0 %collective-permute-start.46 = (bf16[4,1,2,64,1024]{4,3,0,2,1:T(8,128)(2,1)S(1)}, bf16[4,1,2,64,1024]{4,3,0,2,1:T(8,128)(2,1)S(1)}, u32[]{:S(2)}, u32[]{:S(2)}) collective-permute-start(bf16[4,1,2,64,1024]{4,3,0,2,1:T(8,128)(2,1)S(1)} %copy.210), channel_id=1, source_target_pairs={{0,4},{2,6},{4,0},{6,2},{1,5},{3,7},{5,1},{7,3},{8,12},{10,14},{12... | collective-permute-start | bytes 3145736 | tf_op jit(solution)/shard_map/ppermute | solution.py:36
  571.6 30.3 %collective-permute-start.45 = (bf16[4,1,1,64,1024]{4,3,0,2,1:T(8,128)(2,1)S(1)}, bf16[4,1,1,64,1024]{4,3,0,2,1:T(8,128)(2,1)S(1)}, u32[]{:S(2)}, u32[]{:S(2)}) collective-permute-start(bf16[4,1,1,64,1024]{4,3,0,2,1:T(8,128)(2,1)S(1)} %dynamic-slice_select_fusion.2), channel_id=1, source_target_pairs={{0,4},{2,6},{4,0},{6,2},{1,5},{3,7},{5,1},{7,3},{8,12},{10,14},{12... | collective-permute-start | bytes 1572872 | tf_op jit(solution)/shard_map/ppermute | solution.py:36
  581.6 27.6 %collective-permute-start.47 = (bf16[4,1,1,64,1024]{4,3,0,2,1:T(8,128)(2,1)S(1)}, bf16[4,1,1,64,1024]{4,3,0,2,1:T(8,128)(2,1)S(1)}, u32[]{:S(2)}, u32[]{:S(2)}) collective-permute-start(bf16[4,1,1,64,1024]{4,3,0,2,1:T(8,128)(2,1)S(1)} %dynamic-slice_select_fusion.1), channel_id=1, source_target_pairs={{0,2},{2,0},{4,6},{6,4},{1,3},{3,1},{5,7},{7,5},{8,10},{10,8},{12,... | collective-permute-start | bytes 1572872 | tf_op jit(solution)/shard_map/ppermute | solution.py:36
  606.1 33.6 %collective-permute-start.50 = (f32[336,128]{1,0:T(8,128)}, f32[336,128]{1,0:T(8,128)}, u32[]{:S(2)}, u32[]{:S(2)}) collective-permute-start(f32[336,128]{1,0:T(8,128)} %pad_maximum_fusion.19), channel_id=1, source_target_pairs={{0,4},{2,6},{4,0},{6,2},{1,5},{3,7},{5,1},{7,3},{8,12},{10,14},{12... | collective-permute-start | bytes 516104 | tf_op jit(solution)/shard_map/ppermute | solution.py:36
  608.4 27.8 %collective-permute-start.55 = (bf16[4,1,2,64,1024]{4,3,2,1,0:T(8,128)(2,1)}, bf16[4,1,2,64,1024]{4,3,2,1,0:T(8,128)(2,1)}, u32[]{:S(2)}, u32[]{:S(2)}) collective-permute-start(bf16[4,1,2,64,1024]{4,3,2,1,0:T(8,128)(2,1)} %dynamic-slice_select_fusion), channel_id=1, source_target_pairs={{0,4},{2,6},{4,0},{6,2},{1,5},{3,7},{5,1},{7,3},{8,12},{10,14},{12... | collective-permute-start | bytes 3145736 | tf_op jit(solution)/shard_map/ppermute | solution.py:36
  613.5 34.6 %all-to-all-start.5 = ((bf16[4,64,2048]{2,1,0:T(8,128)(2,1)}), bf16[4,64,2048]{2,1,0:T(8,128)(2,1)S(1)}, u32[]{:S(2)}, u32[]{:S(2)}) async-start(bf16[4,64,2048]{2,1,0:T(8,128)(2,1)} %maximum_select_fusion.19), calls=%async_computation.6 | async-start | bytes 2097152 | tf_op jit(solution)/shard_map/all_to_all | solution.py:43
  668.8 43.0 %all-to-all-start.7 = ((bf16[4,64,3584]{2,1,0:T(8,128)(2,1)}), bf16[4,64,3584]{2,1,0:T(8,128)(2,1)S(1)}, u32[]{:S(2)}, u32[]{:S(2)}) async-start(bf16[4,64,3584]{2,1,0:T(8,128)(2,1)} %broadcast_select_fusion.1), calls=%async_computation.9 | async-start | bytes 3670016 | tf_op jit(solution)/shard_map/all_to_all | solution.py:43
  716.1 28.7 %all-to-all-start.8 = ((bf16[4,64,2048]{2,1,0:T(8,128)(2,1)}), bf16[4,64,2048]{2,1,0:T(8,128)(2,1)S(1)}, u32[]{:S(2)}, u32[]{:S(2)}) async-start(bf16[4,64,2048]{2,1,0:T(8,128)(2,1)} %maximum_select_fusion.22), calls=%async_computation.10 | async-start | bytes 2097152 | tf_op jit(solution)/shard_map/all_to_all | solution.py:43
  (170 other events, 943.9 us)
Sparse Core Ops, SparseCore 0:
  13.2 161.5 all-gather.1
  386.3 85.4 reduce-scatter.2
  491.5 113.9 reduce-scatter.4

commit v4 on v3

--- a/solution.py
+++ b/solution.py
@@ -330,7 +330,7 @@
 
 def products(first, second, rights):
     count, dim = first.shape
-    step = 512
+    step = 1024
     steps = rights[0].shape[1] // step
     whole = pl.BlockSpec((count, dim), lambda i: (0, 0))
 

time: 766 us -> 765 us (level)
  no operation moved by 1% of the time
where the time goes in v4:
time: 765 us; the launch traced here: 756 us
  waiting for transfers between devices  232 us (30%)
  Pallas kernels  103 us (13%)
  starting transfers between devices  90.1 us (12%)
  other arithmetic  88.1 us (12%)
  local copies, waits for them, and re-layouts  86.4 us (11%)
  matrix products  72.9 us (10%)
  blocking collectives  43.3 us (6%)
  between operations  40.1 us (5%)
    ppermute x26, waiting for transfers between devices, hop(): lax.ppermute(shard, 'plane', [(i, i ^ 1 << bit) for i in range(self.chips)])  145 us
    dot_general x32, matrix products, dot(): lax.dot_general(left, right, (((left_axis,), (right_axis,)), ((), ())), p...  72.9 us
    all_to_all x8, waiting for transfers between devices, swap_seq(): return lax.all_to_all(blocks, 'seq', 0, 0, tiled=True)  58.2 us
    all_to_all x1, blocking collectives, swap_seq(): return lax.all_to_all(blocks, 'seq', 0, 0, tiled=True)  43.3 us
    all_to_all x8, starting transfers between devices, swap_seq(): return lax.all_to_all(blocks, 'seq', 0, 0, tiled=True)  36.2 us
    ppermute x26, starting transfers between devices, hop(): lax.ppermute(shard, 'plane', [(i, i ^ 1 << bit) for i in range(self.chips)])  33.1 us
    select_n x16, other arithmetic, gather_plane(): jnp.where(place.bit(bit) == 0, jnp.concatenate([current, other], axis), j...  31.6 us
    unnamed x285, local copies, waits for them, and re-layouts  28.7 us
  transfers between devices with their start and end apart: 73, of which 36 were waited for; matrix products, arithmetic and copies ran while one was open for 27% of the time, Pallas kernels for 11%

profile of v4, /device:TPU:0, one launch (start us, length us, event | category | flops | bytes accessed | tf_op | source)
XLA Modules:
  0.0 755.5 jit_solution(14355680718375927207)
XLA Ops:
  15.2 43.3 %all_to_all.45 = bf16[4,64,2176]{2,1,0:T(8,128)(2,1)S(1)} all-to-all(bf16[4,64,2176]{2,1,0:T(8,128)(2,1)S(1)} %broadcast_in_dim.112), channel_id=1, replica_groups=mesh['seq'=4,'plane'=4,'core'=2] {'seq'}, dimensions={0} | all-to-all | bytes 2228224 | tf_op jit(solution)/shard_map/all_to_all | solution.py:43
  64.7 4.3 all-to-all-start.1
  69.0 8.9 %collective-permute-done.4 = bf16[4,1,1,64,1024]{4,3,0,2,1:T(8,128)(2,1)} collective-permute-done((bf16[4,1,1,64,1024]{4,3,0,2,1:T(8,128)(2,1)S(1)}, bf16[4,1,1,64,1024]{4,3,0,2,1:T(8,128)(2,1)}, u32[]{:S(2)}, u32[]{:S(2)}) %collective-permute-start.4) | collective-permute-done | bytes 524320 | tf_op jit(solution)/shard_map/ppermute | solution.py:36
  80.8 5.7 collective-permute-done.1
  90.7 17.5 %collective-permute-done.5 = bf16[4,2,1,64,1024]{4,3,0,2,1:T(8,128)(2,1)S(1)} collective-permute-done((bf16[4,2,1,64,1024]{4,3,0,2,1:T(8,128)(2,1)S(1)}, bf16[4,2,1,64,1024]{4,3,0,2,1:T(8,128)(2,1)S(1)}, u32[]{:S(2)}, u32[]{:S(2)}) %collective-permute-start.5) | collective-permute-done | bytes 1048608 | tf_op jit(solution)/shard_map/ppermute | solution.py:36
  115.3 10.0 %collective-permute-done.2 = bf16[4,1,2,64,1152]{4,3,0,2,1:T(8,128)(2,1)} collective-permute-done((bf16[4,1,2,64,1152]{4,3,0,2,1:T(8,128)(2,1)S(1)}, bf16[4,1,2,64,1152]{4,3,0,2,1:T(8,128)(2,1)}, u32[]{:S(2)}, u32[]{:S(2)}) %collective-permute-start.2) | collective-permute-done | bytes 1179680 | tf_op jit(solution)/shard_map/ppermute | solution.py:36
  140.6 4.5 collective-permute-done.9
  158.1 4.7 all-to-all-start.2
  162.9 11.3 %collective-permute-done.8 = bf16[4,1,2,64,1024]{4,3,0,2,1:T(8,128)(2,1)} collective-permute-done((bf16[4,1,2,64,1024]{4,3,0,2,1:T(8,128)(2,1)S(1)}, bf16[4,1,2,64,1024]{4,3,0,2,1:T(8,128)(2,1)}, u32[]{:S(2)}, u32[]{:S(2)}) %collective-permute-start.8) | collective-permute-done | bytes 1048608 | tf_op jit(solution)/shard_map/ppermute | solution.py:36
  207.7 4.2 collective-permute-start.19
  222.1 12.3 %collective-permute-done.19 = bf16[4,2,1,64,1024]{4,3,0,2,1:T(8,128)(2,1)S(1)} collective-permute-done((bf16[4,2,1,64,1024]{4,3,0,2,1:T(8,128)(2,1)S(1)}, bf16[4,2,1,64,1024]{4,3,0,2,1:T(8,128)(2,1)S(1)}, u32[]{:S(2)}, u32[]{:S(2)}) %collective-permute-start.19) | collective-permute-done | bytes 1048608 | tf_op jit(solution)/shard_map/ppermute | solution.py:36
  253.0 14.8 %attend.1 = (bf16[2,256,512]{2,1,0:T(8,128)(2,1)}, bf16[2,4,2,2,128,256]{5,4,3,2,1,0:T(8,128)(2,1)}) custom-call(s32[2,3]{1,0:T(2,128)} %copy.168.ends_ref, s32[1]{0:T(128)S(6)} %select_n.665.base_ref, bf16[2,256,1536]{2,1,0:T(8,128)(2,1)} %bitcast.262, bf16[2,256,1536]{2,1,0:T(8,128)(2,1)} %bitcast.263, bf16[2,256,1536]{2,1,0:T(8,128)(2,1)} %bitcast.264, ...), custom_call_target="tpu_custom_call" | custom-call | tf_op jit(solution)/shard_map/attend/pallas_call | solution.py:269
  282.1 4.1 collective-permute-done.26
  303.4 8.3 %taps.1 = f32[2,256,512]{2,1,0:T(8,128)} custom-call(s32[2,3]{1,0:T(2,128)} %copy.168.ends_ref, s32[1]{0:T(128)} %bitcast.41.base_ref, bf16[2,32,512]{2,1,0:T(8,128)(2,1)} %copy-done.93, bf16[2,256,512]{2,1,0:T(8,128)(2,1)} %copy-done.5, f32[32,512]{1,0:T(8,128)} %pad.54.taps_ref), custom_call_target="tpu_custom_call" | custom-call | tf_op jit(solution)/shard_map/taps/pallas_call | solution.py:560
  334.8 7.8 %collective-permute-done.29 = bf16[4,1,2,64,1024]{4,3,0,2,1:T(8,128)(2,1)} collective-permute-done((bf16[4,1,2,64,1024]{4,3,0,2,1:T(8,128)(2,1)S(1)}, bf16[4,1,2,64,1024]{4,3,0,2,1:T(8,128)(2,1)}, u32[]{:S(2)}, u32[]{:S(2)}) %collective-permute-start.29) | collective-permute-done | bytes 1048608 | tf_op jit(solution)/shard_map/ppermute | solution.py:36
  367.5 4.6 multiply_convert_fusion.3.refs_0_
  374.6 10.0 %products.1 = bf16[1024,4096]{1,0:T(8,128)(2,1)} custom-call(bf16[512,1024]{1,0:T(8,128)(2,1)} %bitcast.272, bf16[512,1024]{1,0:T(8,128)(2,1)} %bitcast.275, bf16[512,1024]{1,0:T(8,128)(2,1)} %multiply_convert_fusion.3.refs_0_, bf16[512,1024]{1,0:T(8,128)(2,1)} %multiply_convert_fusion.2.refs_1_, bf16[512,1024]{1,0:T(8,128)(2,1)} %copy-done.54, ...), custom_call_target="tpu_custom_call" | custom-call | tf_op jit(solution)/shard_map/products/pallas_call | solution.py:342
  405.1 15.3 %taps_back.1 = (f32[2,256,512]{2,1,0:T(8,128)}, bf16[2,32,512]{2,1,0:T(8,128)(2,1)}, f32[32,512]{1,0:T(8,128)}, f32[1,512]{1,0:T(1,128)}, f32[1,512]{1,0:T(1,128)}) custom-call(s32[2,3]{1,0:T(2,128)} %copy.168.ends_ref, s32[1]{0:T(128)} %bitcast.41.base_ref, bf16[2,32,512]{2,1,0:T(8,128)(2,1)} %copy-done.93, bf16[2,256,512]{2,1,0:T(8,128)(2,1)} %copy-done.5, ...), custom_call_target="tpu_custom_call" | custom-call | tf_op jit(solution)/shard_map/taps_back/pallas_call | solution.py:578
  421.7 5.6 collective-permute-done.36
  447.0 23.5 %attend_back.1 = (bf16[2,256,512]{2,1,0:T(8,128)(2,1)}, f32[2,256,512]{2,1,0:T(8,128)}, f32[2,256,512]{2,1,0:T(8,128)}, bf16[2,64,512]{2,1,0:T(8,128)(2,1)}, bf1...) custom-call(bf16[2,256,1536]{2,1,0:T(8,128)(2,1)} %bitcast.265, ...), custom_call_target="tpu_custom_call" | custom-call | tf_op jit(solution)/shard_map/attend_back/pallas_call | solution.py:292
  477.0 4.3 collective-permute-start.40
  533.9 5.9 all-to-all-start.4
  553.4 15.4 %collective-permute-done.49 = f32[592,128]{1,0:T(8,128)S(1)} collective-permute-done((f32[592,128]{1,0:T(8,128)S(1)}, f32[592,128]{1,0:T(8,128)S(1)}, u32[]{:S(2)}, u32[]{:S(2)}) %collective-permute-start.49) | collective-permute-done | bytes 303136 | tf_op jit(solution)/shard_map/ppermute | solution.py:36
  572.1 8.2 %collective-permute-done.46 = bf16[4,1,2,64,1024]{4,3,0,2,1:T(8,128)(2,1)S(1)} collective-permute-done((bf16[4,1,2,64,1024]{4,3,0,2,1:T(8,128)(2,1)S(1)}, bf16[4,1,2,64,1024]{4,3,0,2,1:T(8,128)(2,1)S(1)}, u32[]{:S(2)}, u32[]{:S(2)}) %collective-permute-start.46) | collective-permute-done | bytes 1048608 | tf_op jit(solution)/shard_map/ppermute | solution.py:36
  581.2 20.0 %collective-permute-done.45 = bf16[4,1,1,64,1024]{4,3,0,2,1:T(8,128)(2,1)S(1)} collective-permute-done((bf16[4,1,1,64,1024]{4,3,0,2,1:T(8,128)(2,1)S(1)}, bf16[4,1,1,64,1024]{4,3,0,2,1:T(8,128)(2,1)S(1)}, u32[]{:S(2)}, u32[]{:S(2)}) %collective-permute-start.45) | collective-permute-done | bytes 524320 | tf_op jit(solution)/shard_map/ppermute | solution.py:36
  612.7 5.3 all-to-all-start.5
  618.0 7.0 collective-permute-done.53
  628.3 7.1 collective-permute-done.55
  650.9 5.2 all-to-all-start.6
  657.7 5.5 all-to-all-done.6
  676.7 34.2 %all-to-all-done.7 = bf16[4,64,3584]{2,1,0:T(8,128)(2,1)S(1)} async-done(((bf16[4,64,3584]{2,1,0:T(8,128)(2,1)}), bf16[4,64,3584]{2,1,0:T(8,128)(2,1)S(1)}, u32[]{:S(2)}, u32[]{:S(2)}) %all-to-all-start.7) | async-done | bytes 1835040 | tf_op jit(solution)/shard_map/all_to_all | solution.py:43
  725.3 18.5 %all-to-all-done.8 = bf16[4,64,2048]{2,1,0:T(8,128)(2,1)S(1)} async-done(((bf16[4,64,2048]{2,1,0:T(8,128)(2,1)}), bf16[4,64,2048]{2,1,0:T(8,128)(2,1)S(1)}, u32[]{:S(2)}, u32[]{:S(2)}) %all-to-all-start.8) | async-done | bytes 1048608 | tf_op jit(solution)/shard_map/all_to_all | solution.py:43
  (670 shorter events, 358.1 us)
Async XLA Ops:
  7.2 206.1 %all-gather.2.cloned.1.call-start = ((), (), s32[]{:S(2)}) async-start(), calls=%async_computation.11 | async-start | bytes 7798784 | tf_op jit(solution)/shard_map/all_gather | solution.py:670
  58.5 28.0 %collective-permute-start.1 = (bf16[4,1,1,64,1152]{4,3,0,2,1:T(8,128)(2,1)S(1)}, bf16[4,1,1,64,1152]{4,3,0,2,1:T(8,128)(2,1)}, u32[]{:S(2)}, u32[]{:S(2)}) collective-permute-start(bf16[4,1,1,64,1152]{4,3,0,2,1:T(8,128)(2,1)S(1)} %slice_bitcast_fusion), channel_id=1, source_target_pairs={{0,2},{2,0},{4,6},{6,4},{1,3},{3,1},{5,7},{7,5},{8,10},{10,8},{12,... | collective-permute-start | bytes 1769480 | tf_op jit(solution)/shard_map/ppermute | solution.py:36
  64.7 46.3 %all-to-all-start.1 = ((bf16[4,64,2048]{2,1,0:T(8,128)(2,1)}), bf16[4,64,2048]{2,1,0:T(8,128)(2,1)}, u32[]{:S(2)}, u32[]{:S(2)}) async-start(bf16[4,64,2048]{2,1,0:T(8,128)(2,1)} %broadcast_in_dim.113), calls=%async_computation.1 | async-start | bytes 2097152 | tf_op jit(solution)/shard_map/all_to_all | solution.py:43
  79.3 28.9 %collective-permute-start.5 = (bf16[4,2,1,64,1024]{4,3,0,2,1:T(8,128)(2,1)S(1)}, bf16[4,2,1,64,1024]{4,3,0,2,1:T(8,128)(2,1)S(1)}, u32[]{:S(2)}, u32[]{:S(2)}) collective-permute-start(bf16[4,2,1,64,1024]{4,3,0,2,1:T(8,128)(2,1)S(1)} %maximum_select_fusion.10), channel_id=1, source_target_pairs={{0,2},{2,0},{4,6},{6,4},{1,3},{3,1},{5,7},{7,5},{8,10},{10,8},{12,... | collective-permute-start | bytes 3145736 | tf_op jit(solution)/shard_map/ppermute | solution.py:36
  88.0 37.3 %collective-permute-start.2 = (bf16[4,1,2,64,1152]{4,3,0,2,1:T(8,128)(2,1)S(1)}, bf16[4,1,2,64,1152]{4,3,0,2,1:T(8,128)(2,1)}, u32[]{:S(2)}, u32[]{:S(2)}) collective-permute-start(bf16[4,1,2,64,1152]{4,3,0,2,1:T(8,128)(2,1)S(1)} %maximum_select_fusion.9), channel_id=1, source_target_pairs={{0,4},{2,6},{4,0},{6,2},{1,5},{3,7},{5,1},{7,3},{8,12},{10,14},{12... | collective-permute-start | bytes 3538952 | tf_op jit(solution)/shard_map/ppermute | solution.py:36
  113.2 31.9 %collective-permute-start.9 = (bf16[4,1,1,64,1024]{4,3,0,2,1:T(8,128)(2,1)}, bf16[4,1,1,64,1024]{4,3,0,2,1:T(8,128)(2,1)}, u32[]{:S(2)}, u32[]{:S(2)}) collective-permute-start(bf16[4,1,1,64,1024]{4,3,0,2,1:T(8,128)(2,1)} %get-tuple-element.149), channel_id=1, source_target_pairs={{0,4},{2,6},{4,0},{6,2},{1,5},{3,7},{5,1},{7,3},{8,12},{10,14},{12... | collective-permute-start | bytes 1572872 | tf_op jit(solution)/shard_map/ppermute | solution.py:36
  114.7 32.3 %collective-permute-start.7 = (bf16[4,1,1,64,1024]{4,3,0,2,1:T(8,128)(2,1)}, bf16[4,1,1,64,1024]{4,3,0,2,1:T(8,128)(2,1)}, u32[]{:S(2)}, u32[]{:S(2)}) collective-permute-start(bf16[4,1,1,64,1024]{4,3,0,2,1:T(8,128)(2,1)} %get-tuple-element.148), channel_id=1, source_target_pairs={{0,2},{2,0},{4,6},{6,4},{1,3},{3,1},{5,7},{7,5},{8,10},{10,8},{12,... | collective-permute-start | bytes 1572872 | tf_op jit(solution)/shard_map/ppermute | solution.py:36
  146.9 29.4 %collective-permute-start.10 = (bf16[4,2,1,64,1024]{4,3,0,2,1:T(8,128)(2,1)S(1)}, bf16[4,2,1,64,1024]{4,3,0,2,1:T(8,128)(2,1)}, u32[]{:S(2)}, u32[]{:S(2)}) collective-permute-start(bf16[4,2,1,64,1024]{4,3,0,2,1:T(8,128)(2,1)S(1)} %maximum_select_fusion.12), channel_id=1, source_target_pairs={{0,2},{2,0},{4,6},{6,4},{1,3},{3,1},{5,7},{7,5},{8,10},{10,8},{12,... | collective-permute-start | bytes 3145736 | tf_op jit(solution)/shard_map/ppermute | solution.py:36
  148.8 25.3 %collective-permute-start.8 = (bf16[4,1,2,64,1024]{4,3,0,2,1:T(8,128)(2,1)S(1)}, bf16[4,1,2,64,1024]{4,3,0,2,1:T(8,128)(2,1)}, u32[]{:S(2)}, u32[]{:S(2)}) collective-permute-start(bf16[4,1,2,64,1024]{4,3,0,2,1:T(8,128)(2,1)S(1)} %maximum_select_fusion.11), channel_id=1, source_target_pairs={{0,4},{2,6},{4,0},{6,2},{1,5},{3,7},{5,1},{7,3},{8,12},{10,14},{12... | collective-permute-start | bytes 3145736 | tf_op jit(solution)/shard_map/ppermute | solution.py:36
  158.1 31.0 %all-to-all-start.2 = ((bf16[4,64,2048]{2,1,0:T(8,128)(2,1)}), bf16[4,64,2048]{2,1,0:T(8,128)(2,1)}, u32[]{:S(2)}, u32[]{:S(2)}) async-start(bf16[4,64,2048]{2,1,0:T(8,128)(2,1)} %broadcast_in_dim.117), calls=%async_computation.2 | async-start | bytes 2097152 | tf_op jit(solution)/shard_map/all_to_all | solution.py:43
  201.8 42.5 %all-to-all-start.3 = ((bf16[4,64,2048]{2,1,0:T(8,128)(2,1)}), bf16[4,64,2048]{2,1,0:T(8,128)(2,1)S(1)}, u32[]{:S(2)}, u32[]{:S(2)}) async-start(bf16[4,64,2048]{2,1,0:T(8,128)(2,1)} %broadcast_in_dim.118), calls=%async_computation.3 | async-start | bytes 2097152 | tf_op jit(solution)/shard_map/all_to_all | solution.py:43
  205.4 325.4 %reduce-scatter.3.cloned.1.call-start = ((), (), s32[]{:S(2)}) async-start(), calls=%async_computation.12 | async-start | bytes 10485760 | tf_op jit(solution)/shard_map/reduce_scatter | solution.py:788
  207.7 26.7 %collective-permute-start.19 = (bf16[4,2,1,64,1024]{4,3,0,2,1:T(8,128)(2,1)S(1)}, bf16[4,2,1,64,1024]{4,3,0,2,1:T(8,128)(2,1)S(1)}, u32[]{:S(2)}, u32[]{:S(2)}) collective-permute-start(bf16[4,2,1,64,1024]{4,3,0,2,1:T(8,128)(2,1)S(1)} %maximum_select_fusion.14), channel_id=1, source_target_pairs={{0,2},{2,0},{4,6},{6,4},{1,3},{3,1},{5,7},{7,5},{8,10},{10,8},{12,... | collective-permute-start | bytes 3145736 | tf_op jit(solution)/shard_map/ppermute | solution.py:36
  217.5 50.4 %collective-permute-start.17 = (bf16[512,1024]{1,0:T(8,128)(2,1)}, bf16[512,1024]{1,0:T(8,128)(2,1)}, u32[]{:S(2)}, u32[]{:S(2)}) collective-permute-start(bf16[512,1024]{1,0:T(8,128)(2,1)} %constant_dynamic-slice_fusion.24), channel_id=1, source_target_pairs={{0,1},{1,0},{2,3},{3,2},{4,5},{5,4},{6,7},{7,6},{8,9},{9,8},{10,11... | collective-permute-start | bytes 3145736 | tf_op jit(solution)/shard_map/ppermute | solution.py:33
  245.2 28.4 %collective-permute-start.20 = (bf16[4,1,1,64,1024]{4,3,0,2,1:T(8,128)(2,1)S(1)}, bf16[4,1,1,64,1024]{4,3,0,2,1:T(8,128)(2,1)}, u32[]{:S(2)}, u32[]{:S(2)}) collective-permute-start(bf16[4,1,1,64,1024]{4,3,0,2,1:T(8,128)(2,1)S(1)} %get-tuple-element.145), channel_id=1, source_target_pairs={{0,4},{2,6},{4,0},{6,2},{1,5},{3,7},{5,1},{7,3},{8,12},{10,14},{12... | collective-permute-start | bytes 1572872 | tf_op jit(solution)/shard_map/ppermute | solution.py:36
  288.6 38.9 %collective-permute-start.27 = (bf16[4,1,2,64,1024]{4,3,0,2,1:T(8,128)(2,1)}, bf16[4,1,2,64,1024]{4,3,0,2,1:T(8,128)(2,1)}, u32[]{:S(2)}, u32[]{:S(2)}) collective-permute-start(bf16[4,1,2,64,1024]{4,3,0,2,1:T(8,128)(2,1)} %maximum_select_fusion.16), channel_id=1, source_target_pairs={{0,4},{2,6},{4,0},{6,2},{1,5},{3,7},{5,1},{7,3},{8,12},{10,14},{12... | collective-permute-start | bytes 3145736 | tf_op jit(solution)/shard_map/ppermute | solution.py:36
  290.0 25.6 %collective-permute-start.28 = (bf16[4,1,1,64,1024]{4,3,0,2,1:T(8,128)(2,1)}, bf16[4,1,1,64,1024]{4,3,0,2,1:T(8,128)(2,1)}, u32[]{:S(2)}, u32[]{:S(2)}) collective-permute-start(bf16[4,1,1,64,1024]{4,3,0,2,1:T(8,128)(2,1)} %get-tuple-element.144), channel_id=1, source_target_pairs={{0,2},{2,0},{4,6},{6,4},{1,3},{3,1},{5,7},{7,5},{8,10},{10,8},{12,... | collective-permute-start | bytes 1572872 | tf_op jit(solution)/shard_map/ppermute | solution.py:36
  301.1 29.7 %collective-permute-start.30 = (bf16[4,2,1,64,1024]{4,3,0,2,1:T(8,128)(2,1)}, bf16[4,2,1,64,1024]{4,3,0,2,1:T(8,128)(2,1)}, u32[]{:S(2)}, u32[]{:S(2)}) collective-permute-start(bf16[4,2,1,64,1024]{4,3,0,2,1:T(8,128)(2,1)} %maximum_select_fusion.18), channel_id=1, source_target_pairs={{0,2},{2,0},{4,6},{6,4},{1,3},{3,1},{5,7},{7,5},{8,10},{10,8},{12,... | collective-permute-start | bytes 3145736 | tf_op jit(solution)/shard_map/ppermute | solution.py:36
  317.3 25.3 %collective-permute-start.29 = (bf16[4,1,2,64,1024]{4,3,0,2,1:T(8,128)(2,1)S(1)}, bf16[4,1,2,64,1024]{4,3,0,2,1:T(8,128)(2,1)}, u32[]{:S(2)}, u32[]{:S(2)}) collective-permute-start(bf16[4,1,2,64,1024]{4,3,0,2,1:T(8,128)(2,1)S(1)} %maximum_select_fusion.17), channel_id=1, source_target_pairs={{0,4},{2,6},{4,0},{6,2},{1,5},{3,7},{5,1},{7,3},{8,12},{10,14},{12... | collective-permute-start | bytes 3145736 | tf_op jit(solution)/shard_map/ppermute | solution.py:36
  384.7 280.3 %reduce-scatter.5.cloned.1.call-start = ((), (), s32[]{:S(2)}) async-start(), calls=%async_computation.13 | async-start | bytes 9175040 | tf_op jit(solution)/shard_map/reduce_scatter | solution.py:788
  441.9 39.4 %collective-permute-start.52 = (bf16[512,512]{1,0:T(8,128)(2,1)}, bf16[512,512]{1,0:T(8,128)(2,1)S(1)}, u32[]{:S(2)}, u32[]{:S(2)}) collective-permute-start(bf16[512,512]{1,0:T(8,128)(2,1)} %get-tuple-element.141), channel_id=1, source_target_pairs={{0,1},{1,0},{2,3},{3,2},{4,5},{5,4},{6,7},{7,6},{8,9},{9,8},{10,11... | collective-permute-start | bytes 1572872 | tf_op jit(solution)/shard_map/ppermute | solution.py:33
  516.8 52.1 %collective-permute-start.44 = (bf16[4,2,1,64,1024]{4,3,0,2,1:T(8,128)(2,1)}, bf16[4,2,1,64,1024]{4,3,0,2,1:T(8,128)(2,1)}, u32[]{:S(2)}, u32[]{:S(2)}) collective-permute-start(bf16[4,2,1,64,1024]{4,3,0,2,1:T(8,128)(2,1)} %copy.208), channel_id=1, source_target_pairs={{0,2},{2,0},{4,6},{6,4},{1,3},{3,1},{5,7},{7,5},{8,10},{10,8},{12,... | collective-permute-start | bytes 3145736 | tf_op jit(solution)/shard_map/ppermute | solution.py:36
  533.9 75.5 %all-to-all-start.4 = ((bf16[4,64,4096]{2,1,0:T(8,128)(2,1)}), bf16[4,64,4096]{2,1,0:T(8,128)(2,1)S(1)}, u32[]{:S(2)}, u32[]{:S(2)}) async-start(bf16[4,64,4096]{2,1,0:T(8,128)(2,1)} %broadcast_select_fusion), calls=%async_computation.5 | async-start | bytes 4194304 | tf_op jit(solution)/shard_map/all_to_all | solution.py:43
  543.6 25.3 %collective-permute-start.49 = (f32[592,128]{1,0:T(8,128)S(1)}, f32[592,128]{1,0:T(8,128)S(1)}, u32[]{:S(2)}, u32[]{:S(2)}) collective-permute-start(f32[592,128]{1,0:T(8,128)S(1)} %pad_maximum_fusion.14), channel_id=1, source_target_pairs={{0,2},{2,0},{4,6},{6,4},{1,3},{3,1},{5,7},{7,5},{8,10},{10,8},{12,... | collective-permute-start | bytes 909320 | tf_op jit(solution)/shard_map/ppermute | solution.py:36
  546.8 33.5 %collective-permute-start.46 = (bf16[4,1,2,64,1024]{4,3,0,2,1:T(8,128)(2,1)S(1)}, bf16[4,1,2,64,1024]{4,3,0,2,1:T(8,128)(2,1)S(1)}, u32[]{:S(2)}, u32[]{:S(2)}) collective-permute-start(bf16[4,1,2,64,1024]{4,3,0,2,1:T(8,128)(2,1)S(1)} %copy.210), channel_id=1, source_target_pairs={{0,4},{2,6},{4,0},{6,2},{1,5},{3,7},{5,1},{7,3},{8,12},{10,14},{12... | collective-permute-start | bytes 3145736 | tf_op jit(solution)/shard_map/ppermute | solution.py:36
  570.6 30.5 %collective-permute-start.45 = (bf16[4,1,1,64,1024]{4,3,0,2,1:T(8,128)(2,1)S(1)}, bf16[4,1,1,64,1024]{4,3,0,2,1:T(8,128)(2,1)S(1)}, u32[]{:S(2)}, u32[]{:S(2)}) collective-permute-start(bf16[4,1,1,64,1024]{4,3,0,2,1:T(8,128)(2,1)S(1)} %dynamic-slice_select_fusion.2), channel_id=1, source_target_pairs={{0,4},{2,6},{4,0},{6,2},{1,5},{3,7},{5,1},{7,3},{8,12},{10,14},{12... | collective-permute-start | bytes 1572872 | tf_op jit(solution)/shard_map/ppermute | solution.py:36
  580.8 27.5 %collective-permute-start.47 = (bf16[4,1,1,64,1024]{4,3,0,2,1:T(8,128)(2,1)S(1)}, bf16[4,1,1,64,1024]{4,3,0,2,1:T(8,128)(2,1)S(1)}, u32[]{:S(2)}, u32[]{:S(2)}) collective-permute-start(bf16[4,1,1,64,1024]{4,3,0,2,1:T(8,128)(2,1)S(1)} %dynamic-slice_select_fusion.1), channel_id=1, source_target_pairs={{0,2},{2,0},{4,6},{6,4},{1,3},{3,1},{5,7},{7,5},{8,10},{10,8},{12,... | collective-permute-start | bytes 1572872 | tf_op jit(solution)/shard_map/ppermute | solution.py:36
  605.3 33.6 %collective-permute-start.50 = (f32[336,128]{1,0:T(8,128)}, f32[336,128]{1,0:T(8,128)}, u32[]{:S(2)}, u32[]{:S(2)}) collective-permute-start(f32[336,128]{1,0:T(8,128)} %pad_maximum_fusion.19), channel_id=1, source_target_pairs={{0,4},{2,6},{4,0},{6,2},{1,5},{3,7},{5,1},{7,3},{8,12},{10,14},{12... | collective-permute-start | bytes 516104 | tf_op jit(solution)/shard_map/ppermute | solution.py:36
  607.8 27.6 %collective-permute-start.55 = (bf16[4,1,2,64,1024]{4,3,2,1,0:T(8,128)(2,1)}, bf16[4,1,2,64,1024]{4,3,2,1,0:T(8,128)(2,1)}, u32[]{:S(2)}, u32[]{:S(2)}) collective-permute-start(bf16[4,1,2,64,1024]{4,3,2,1,0:T(8,128)(2,1)} %dynamic-slice_select_fusion), channel_id=1, source_target_pairs={{0,4},{2,6},{4,0},{6,2},{1,5},{3,7},{5,1},{7,3},{8,12},{10,14},{12... | collective-permute-start | bytes 3145736 | tf_op jit(solution)/shard_map/ppermute | solution.py:36
  612.7 34.6 %all-to-all-start.5 = ((bf16[4,64,2048]{2,1,0:T(8,128)(2,1)}), bf16[4,64,2048]{2,1,0:T(8,128)(2,1)S(1)}, u32[]{:S(2)}, u32[]{:S(2)}) async-start(bf16[4,64,2048]{2,1,0:T(8,128)(2,1)} %maximum_select_fusion.19), calls=%async_computation.6 | async-start | bytes 2097152 | tf_op jit(solution)/shard_map/all_to_all | solution.py:43
  667.9 43.0 %all-to-all-start.7 = ((bf16[4,64,3584]{2,1,0:T(8,128)(2,1)}), bf16[4,64,3584]{2,1,0:T(8,128)(2,1)S(1)}, u32[]{:S(2)}, u32[]{:S(2)}) async-start(bf16[4,64,3584]{2,1,0:T(8,128)(2,1)} %broadcast_select_fusion.1), calls=%async_computation.9 | async-start | bytes 3670016 | tf_op jit(solution)/shard_map/all_to_all | solution.py:43
  715.2 28.7 %all-to-all-start.8 = ((bf16[4,64,2048]{2,1,0:T(8,128)(2,1)}), bf16[4,64,2048]{2,1,0:T(8,128)(2,1)S(1)}, u32[]{:S(2)}, u32[]{:S(2)}) async-start(bf16[4,64,2048]{2,1,0:T(8,128)(2,1)} %maximum_select_fusion.22), calls=%async_computation.10 | async-start | bytes 2097152 | tf_op jit(solution)/shard_map/all_to_all | solution.py:43
  (170 other events, 943.7 us)
Sparse Core Ops, SparseCore 0:
  13.2 161.2 all-gather.1
  384.8 85.4 reduce-scatter.2
  490.0 114.0 reduce-scatter.4

commit v5 on v4

--- a/solution.py
+++ b/solution.py
@@ -897,8 +897,8 @@
     small_total = summed(
         tie(jnp.concatenate([current.reshape(seq_size, rows, 128), rel_all], 1), tip(down_sum))
     )
-    attention_sum = summed(tie(attention_part, tip(small_total)))
-    in_sum = summed(tie(in_part, tip(attention_sum)))
+    last_sum = summed(tie(jnp.concatenate([in_part, attention_part], -1), tip(small_total)))
+    in_sum, attention_sum = last_sum[:, :hid], last_sum[:, hid:]
     rel_total = small_total[rows : rows + offsets, :HEAD_DIM]
     small_total = small_total[:rows]
     small_sum = place.core_part(small_total, 0, core) + place.sibling(

time: 765 us -> 759 us (level)
  waiting for transfers between devices: 232 us -> 223 us
    all_to_all x8 -> x7, waiting for transfers between devices: 58.2 us -> 44.2 us  [swap_seq(): return lax.all_to_all(blocks, 'seq', 0, 0, tiled=True)]
    all_to_all x8 -> x7, starting transfers between devices: 36.2 us -> 30.8 us  [swap_seq(): return lax.all_to_all(blocks, 'seq', 0, 0, tiled=True)]
    unnamed x285 -> x286, local copies, waits for them, and re-layouts: 28.7 us -> 28.6 us
  transfers between devices with their start and end apart: 73 -> 72, of which waited for: 36 -> 33; matrix products, arithmetic and copies ran while one was open for 27% -> 27% of each run, Pallas kernels for 11% -> 12%
where the time goes in v5:
time: 759 us; the launch traced here: 749 us
  waiting for transfers between devices  223 us (29%)
  Pallas kernels  102 us (13%)
  other arithmetic  92.7 us (12%)
  local copies, waits for them, and re-layouts  89.8 us (12%)
  starting transfers between devices  86.1 us (11%)
  matrix products  73 us (10%)
  blocking collectives  43.3 us (6%)
  between operations  38.7 us (5%)
    ppermute x26, waiting for transfers between devices, hop(): lax.ppermute(shard, 'plane', [(i, i ^ 1 << bit) for i in range(self.chips)])  148 us
    dot_general x32, matrix products, dot(): lax.dot_general(left, right, (((left_axis,), (right_axis,)), ((), ())), p...  73 us
    all_to_all x7, waiting for transfers between devices, swap_seq(): return lax.all_to_all(blocks, 'seq', 0, 0, tiled=True)  44.2 us
    all_to_all x1, blocking collectives, swap_seq(): return lax.all_to_all(blocks, 'seq', 0, 0, tiled=True)  43.3 us
    ppermute x26, starting transfers between devices, hop(): lax.ppermute(shard, 'plane', [(i, i ^ 1 << bit) for i in range(self.chips)])  33.6 us
    select_n x16, other arithmetic, gather_plane(): jnp.where(place.bit(bit) == 0, jnp.concatenate([current, other], axis), j...  33.2 us
    all_to_all x7, starting transfers between devices, swap_seq(): return lax.all_to_all(blocks, 'seq', 0, 0, tiled=True)  30.8 us
    unnamed x286, local copies, waits for them, and re-layouts  28.6 us
  transfers between devices with their start and end apart: 72, of which 33 were waited for; matrix products, arithmetic and copies ran while one was open for 27% of the time, Pallas kernels for 12%

profile of v5, /device:TPU:0, one launch (start us, length us, event | category | flops | bytes accessed | tf_op | source)
XLA Modules:
  0.0 749.1 jit_solution(7238023451408791528)
XLA Ops:
  15.2 43.3 %all_to_all.40 = bf16[4,64,2176]{2,1,0:T(8,128)(2,1)S(1)} all-to-all(bf16[4,64,2176]{2,1,0:T(8,128)(2,1)S(1)} %broadcast_in_dim.115), channel_id=1, replica_groups=mesh['seq'=4,'plane'=4,'core'=2] {'seq'}, dimensions={0} | all-to-all | bytes 2228224 | tf_op jit(solution)/shard_map/all_to_all | solution.py:43
  64.7 4.3 all-to-all-start.1
  69.0 8.9 %collective-permute-done.4 = bf16[4,1,1,64,1024]{4,3,0,2,1:T(8,128)(2,1)} collective-permute-done((bf16[4,1,1,64,1024]{4,3,0,2,1:T(8,128)(2,1)S(1)}, bf16[4,1,1,64,1024]{4,3,0,2,1:T(8,128)(2,1)}, u32[]{:S(2)}, u32[]{:S(2)}) %collective-permute-start.4) | collective-permute-done | bytes 524320 | tf_op jit(solution)/shard_map/ppermute | solution.py:36
  80.8 5.7 collective-permute-done.1
  90.7 17.5 %collective-permute-done.5 = bf16[4,2,1,64,1024]{4,3,0,2,1:T(8,128)(2,1)S(1)} collective-permute-done((bf16[4,2,1,64,1024]{4,3,0,2,1:T(8,128)(2,1)S(1)}, bf16[4,2,1,64,1024]{4,3,0,2,1:T(8,128)(2,1)S(1)}, u32[]{:S(2)}, u32[]{:S(2)}) %collective-permute-start.5) | collective-permute-done | bytes 1048608 | tf_op jit(solution)/shard_map/ppermute | solution.py:36
  115.3 10.0 %collective-permute-done.2 = bf16[4,1,2,64,1152]{4,3,0,2,1:T(8,128)(2,1)} collective-permute-done((bf16[4,1,2,64,1152]{4,3,0,2,1:T(8,128)(2,1)S(1)}, bf16[4,1,2,64,1152]{4,3,0,2,1:T(8,128)(2,1)}, u32[]{:S(2)}, u32[]{:S(2)}) %collective-permute-start.2) | collective-permute-done | bytes 1179680 | tf_op jit(solution)/shard_map/ppermute | solution.py:36
  140.6 4.6 collective-permute-done.9
  158.2 4.4 all-to-all-start.2
  162.7 11.5 %collective-permute-done.8 = bf16[4,1,2,64,1024]{4,3,0,2,1:T(8,128)(2,1)} collective-permute-done((bf16[4,1,2,64,1024]{4,3,0,2,1:T(8,128)(2,1)S(1)}, bf16[4,1,2,64,1024]{4,3,0,2,1:T(8,128)(2,1)}, u32[]{:S(2)}, u32[]{:S(2)}) %collective-permute-start.8) | collective-permute-done | bytes 1048608 | tf_op jit(solution)/shard_map/ppermute | solution.py:36
  207.7 4.3 collective-permute-start.19
  221.1 13.5 %collective-permute-done.19 = bf16[4,2,1,64,1024]{4,3,0,2,1:T(8,128)(2,1)} collective-permute-done((bf16[4,2,1,64,1024]{4,3,0,2,1:T(8,128)(2,1)S(1)}, bf16[4,2,1,64,1024]{4,3,0,2,1:T(8,128)(2,1)}, u32[]{:S(2)}, u32[]{:S(2)}) %collective-permute-start.19) | collective-permute-done | bytes 1048608 | tf_op jit(solution)/shard_map/ppermute | solution.py:36
  253.9 14.8 %attend.1 = (bf16[2,256,512]{2,1,0:T(8,128)(2,1)}, bf16[2,4,2,2,128,256]{5,4,3,2,1,0:T(8,128)(2,1)}) custom-call(s32[2,3]{1,0:T(2,128)} %copy.172.ends_ref, s32[1]{0:T(128)S(6)} %select_n.659.base_ref, bf16[2,256,1536]{2,1,0:T(8,128)(2,1)} %bitcast.265, bf16[2,256,1536]{2,1,0:T(8,128)(2,1)} %bitcast.266, bf16[2,256,1536]{2,1,0:T(8,128)(2,1)} %bitcast.267, ...), custom_call_target="tpu_custom_call" | custom-call | tf_op jit(solution)/shard_map/attend/pallas_call | solution.py:269
  283.1 4.0 collective-permute-done.26
  304.3 8.3 %taps.1 = f32[2,256,512]{2,1,0:T(8,128)} custom-call(s32[2,3]{1,0:T(2,128)} %copy.172.ends_ref, s32[1]{0:T(128)} %bitcast.41.base_ref, bf16[2,32,512]{2,1,0:T(8,128)(2,1)} %copy-done.93, bf16[2,256,512]{2,1,0:T(8,128)(2,1)} %copy-done.5, f32[32,512]{1,0:T(8,128)} %pad.54.taps_ref), custom_call_target="tpu_custom_call" | custom-call | tf_op jit(solution)/shard_map/taps/pallas_call | solution.py:560
  332.9 3.8 maximum_select_fusion.8
  336.9 6.7 collective-permute-done.29
  368.4 4.6 multiply_convert_fusion.3.refs_0_
  375.5 10.2 %products.1 = bf16[1024,4096]{1,0:T(8,128)(2,1)} custom-call(bf16[512,1024]{1,0:T(8,128)(2,1)} %bitcast.275, bf16[512,1024]{1,0:T(8,128)(2,1)} %bitcast.278, bf16[512,1024]{1,0:T(8,128)(2,1)} %multiply_convert_fusion.3.refs_0_, bf16[512,1024]{1,0:T(8,128)(2,1)} %multiply_convert_fusion.2.refs_1_, bf16[512,1024]{1,0:T(8,128)(2,1)} %copy-done.54, ...), custom_call_target="tpu_custom_call" | custom-call | tf_op jit(solution)/shard_map/products/pallas_call | solution.py:342
  399.1 3.9 multiply_reduce_fusion.2
  405.9 15.4 %taps_back.1 = (f32[2,256,512]{2,1,0:T(8,128)}, bf16[2,32,512]{2,1,0:T(8,128)(2,1)}, f32[32,512]{1,0:T(8,128)}, f32[1,512]{1,0:T(1,128)}, f32[1,512]{1,0:T(1,128)}) custom-call(s32[2,3]{1,0:T(2,128)} %copy.172.ends_ref, s32[1]{0:T(128)} %bitcast.41.base_ref, bf16[2,32,512]{2,1,0:T(8,128)(2,1)} %copy-done.93, bf16[2,256,512]{2,1,0:T(8,128)(2,1)} %copy-done.5, ...), custom_call_target="tpu_custom_call" | custom-call | tf_op jit(solution)/shard_map/taps_back/pallas_call | solution.py:578
  422.6 5.6 collective-permute-done.36
  448.0 23.5 %attend_back.1 = (bf16[2,256,512]{2,1,0:T(8,128)(2,1)}, f32[2,256,512]{2,1,0:T(8,128)}, f32[2,256,512]{2,1,0:T(8,128)}, bf16[2,64,512]{2,1,0:T(8,128)(2,1)}, bf1...) custom-call(bf16[2,256,1536]{2,1,0:T(8,128)(2,1)} %bitcast.268, ...), custom_call_target="tpu_custom_call" | custom-call | tf_op jit(solution)/shard_map/attend_back/pallas_call | solution.py:292
  477.9 4.7 collective-permute-start.40
  527.8 5.3 all-to-all-start.4
  555.7 36.9 %collective-permute-done.49 = f32[592,128]{1,0:T(8,128)S(1)} collective-permute-done((f32[592,128]{1,0:T(8,128)S(1)}, f32[592,128]{1,0:T(8,128)S(1)}, u32[]{:S(2)}, u32[]{:S(2)}) %collective-permute-start.49) | collective-permute-done | bytes 303136 | tf_op jit(solution)/shard_map/ppermute | solution.py:36
  599.4 9.6 %collective-permute-done.45 = bf16[4,1,1,64,1024]{4,3,2,1,0:T(8,128)(2,1)S(1)} collective-permute-done((bf16[4,1,1,64,1024]{4,3,2,1,0:T(8,128)(2,1)S(1)}, bf16[4,1,1,64,1024]{4,3,2,1,0:T(8,128)(2,1)S(1)}, u32[]{:S(2)}, u32[]{:S(2)}) %collective-permute-start.45) | collective-permute-done | bytes 524320 | tf_op jit(solution)/shard_map/ppermute | solution.py:36
  617.9 4.6 all-to-all-start.5
  627.4 7.0 collective-permute-done.51
  638.2 11.8 %collective-permute-done.53 = bf16[4,1,2,64,1024]{4,3,0,2,1:T(8,128)(2,1)} collective-permute-done((bf16[4,1,2,64,1024]{4,3,0,2,1:T(8,128)(2,1)}, bf16[4,1,2,64,1024]{4,3,0,2,1:T(8,128)(2,1)}, u32[]{:S(2)}, u32[]{:S(2)}) %collective-permute-start.53) | collective-permute-done | bytes 1048608 | tf_op jit(solution)/shard_map/ppermute | solution.py:36
  658.0 4.9 all-to-all-start.6
  665.4 4.7 all-to-all-done.6
  693.1 39.5 %all-to-all-done.7 = bf16[4,64,5632]{2,1,0:T(8,128)(2,1)S(1)} async-done(((bf16[4,64,5632]{2,1,0:T(8,128)(2,1)}), bf16[4,64,5632]{2,1,0:T(8,128)(2,1)S(1)}, u32[]{:S(2)}, u32[]{:S(2)}) %all-to-all-start.7) | async-done | bytes 2883616 | tf_op jit(solution)/shard_map/all_to_all | solution.py:43
  (669 shorter events, 352.6 us)
Async XLA Ops:
  7.2 206.2 %all-gather.2.cloned.1.call-start = ((), (), s32[]{:S(2)}) async-start(), calls=%async_computation.10 | async-start | bytes 7798784 | tf_op jit(solution)/shard_map/all_gather | solution.py:670
  58.5 28.0 %collective-permute-start.1 = (bf16[4,1,1,64,1152]{4,3,0,2,1:T(8,128)(2,1)S(1)}, bf16[4,1,1,64,1152]{4,3,0,2,1:T(8,128)(2,1)}, u32[]{:S(2)}, u32[]{:S(2)}) collective-permute-start(bf16[4,1,1,64,1152]{4,3,0,2,1:T(8,128)(2,1)S(1)} %slice_bitcast_fusion), channel_id=1, source_target_pairs={{0,2},{2,0},{4,6},{6,4},{1,3},{3,1},{5,7},{7,5},{8,10},{10,8},{12,... | collective-permute-start | bytes 1769480 | tf_op jit(solution)/shard_map/ppermute | solution.py:36
  64.7 46.3 %all-to-all-start.1 = ((bf16[4,64,2048]{2,1,0:T(8,128)(2,1)}), bf16[4,64,2048]{2,1,0:T(8,128)(2,1)}, u32[]{:S(2)}, u32[]{:S(2)}) async-start(bf16[4,64,2048]{2,1,0:T(8,128)(2,1)} %broadcast_in_dim.116), calls=%async_computation.1 | async-start | bytes 2097152 | tf_op jit(solution)/shard_map/all_to_all | solution.py:43
  79.3 28.9 %collective-permute-start.5 = (bf16[4,2,1,64,1024]{4,3,0,2,1:T(8,128)(2,1)S(1)}, bf16[4,2,1,64,1024]{4,3,0,2,1:T(8,128)(2,1)S(1)}, u32[]{:S(2)}, u32[]{:S(2)}) collective-permute-start(bf16[4,2,1,64,1024]{4,3,0,2,1:T(8,128)(2,1)S(1)} %maximum_select_fusion.11), channel_id=1, source_target_pairs={{0,2},{2,0},{4,6},{6,4},{1,3},{3,1},{5,7},{7,5},{8,10},{10,8},{12,... | collective-permute-start | bytes 3145736 | tf_op jit(solution)/shard_map/ppermute | solution.py:36
  88.0 37.3 %collective-permute-start.2 = (bf16[4,1,2,64,1152]{4,3,0,2,1:T(8,128)(2,1)S(1)}, bf16[4,1,2,64,1152]{4,3,0,2,1:T(8,128)(2,1)}, u32[]{:S(2)}, u32[]{:S(2)}) collective-permute-start(bf16[4,1,2,64,1152]{4,3,0,2,1:T(8,128)(2,1)S(1)} %maximum_select_fusion.10), channel_id=1, source_target_pairs={{0,4},{2,6},{4,0},{6,2},{1,5},{3,7},{5,1},{7,3},{8,12},{10,14},{12... | collective-permute-start | bytes 3538952 | tf_op jit(solution)/shard_map/ppermute | solution.py:36
  113.2 31.9 %collective-permute-start.9 = (bf16[4,1,1,64,1024]{4,3,0,2,1:T(8,128)(2,1)}, bf16[4,1,1,64,1024]{4,3,0,2,1:T(8,128)(2,1)}, u32[]{:S(2)}, u32[]{:S(2)}) collective-permute-start(bf16[4,1,1,64,1024]{4,3,0,2,1:T(8,128)(2,1)} %get-tuple-element.149), channel_id=1, source_target_pairs={{0,4},{2,6},{4,0},{6,2},{1,5},{3,7},{5,1},{7,3},{8,12},{10,14},{12... | collective-permute-start | bytes 1572872 | tf_op jit(solution)/shard_map/ppermute | solution.py:36
  114.7 32.3 %collective-permute-start.7 = (bf16[4,1,1,64,1024]{4,3,0,2,1:T(8,128)(2,1)}, bf16[4,1,1,64,1024]{4,3,0,2,1:T(8,128)(2,1)}, u32[]{:S(2)}, u32[]{:S(2)}) collective-permute-start(bf16[4,1,1,64,1024]{4,3,0,2,1:T(8,128)(2,1)} %get-tuple-element.148), channel_id=1, source_target_pairs={{0,2},{2,0},{4,6},{6,4},{1,3},{3,1},{5,7},{7,5},{8,10},{10,8},{12,... | collective-permute-start | bytes 1572872 | tf_op jit(solution)/shard_map/ppermute | solution.py:36
  146.9 29.4 %collective-permute-start.10 = (bf16[4,2,1,64,1024]{4,3,0,2,1:T(8,128)(2,1)S(1)}, bf16[4,2,1,64,1024]{4,3,0,2,1:T(8,128)(2,1)}, u32[]{:S(2)}, u32[]{:S(2)}) collective-permute-start(bf16[4,2,1,64,1024]{4,3,0,2,1:T(8,128)(2,1)S(1)} %maximum_select_fusion.13), channel_id=1, source_target_pairs={{0,2},{2,0},{4,6},{6,4},{1,3},{3,1},{5,7},{7,5},{8,10},{10,8},{12,... | collective-permute-start | bytes 3145736 | tf_op jit(solution)/shard_map/ppermute | solution.py:36
  148.8 25.3 %collective-permute-start.8 = (bf16[4,1,2,64,1024]{4,3,0,2,1:T(8,128)(2,1)S(1)}, bf16[4,1,2,64,1024]{4,3,0,2,1:T(8,128)(2,1)}, u32[]{:S(2)}, u32[]{:S(2)}) collective-permute-start(bf16[4,1,2,64,1024]{4,3,0,2,1:T(8,128)(2,1)S(1)} %maximum_select_fusion.12), channel_id=1, source_target_pairs={{0,4},{2,6},{4,0},{6,2},{1,5},{3,7},{5,1},{7,3},{8,12},{10,14},{12... | collective-permute-start | bytes 3145736 | tf_op jit(solution)/shard_map/ppermute | solution.py:36
  158.2 30.9 %all-to-all-start.2 = ((bf16[4,64,2048]{2,1,0:T(8,128)(2,1)}), bf16[4,64,2048]{2,1,0:T(8,128)(2,1)}, u32[]{:S(2)}, u32[]{:S(2)}) async-start(bf16[4,64,2048]{2,1,0:T(8,128)(2,1)} %broadcast_in_dim.120), calls=%async_computation.2 | async-start | bytes 2097152 | tf_op jit(solution)/shard_map/all_to_all | solution.py:43
  201.9 43.3 %all-to-all-start.3 = ((bf16[4,64,2048]{2,1,0:T(8,128)(2,1)}), bf16[4,64,2048]{2,1,0:T(8,128)(2,1)S(1)}, u32[]{:S(2)}, u32[]{:S(2)}) async-start(bf16[4,64,2048]{2,1,0:T(8,128)(2,1)} %broadcast_in_dim.121), calls=%async_computation.3 | async-start | bytes 2097152 | tf_op jit(solution)/shard_map/all_to_all | solution.py:43
  205.5 319.1 %reduce-scatter.3.cloned.1.call-start = ((), (), s32[]{:S(2)}) async-start(), calls=%async_computation.11 | async-start | bytes 10485760 | tf_op jit(solution)/shard_map/reduce_scatter | solution.py:788
  207.7 26.9 %collective-permute-start.19 = (bf16[4,2,1,64,1024]{4,3,0,2,1:T(8,128)(2,1)S(1)}, bf16[4,2,1,64,1024]{4,3,0,2,1:T(8,128)(2,1)}, u32[]{:S(2)}, u32[]{:S(2)}) collective-permute-start(bf16[4,2,1,64,1024]{4,3,0,2,1:T(8,128)(2,1)S(1)} %maximum_select_fusion.15), channel_id=1, source_target_pairs={{0,2},{2,0},{4,6},{6,4},{1,3},{3,1},{5,7},{7,5},{8,10},{10,8},{12,... | collective-permute-start | bytes 3145736 | tf_op jit(solution)/shard_map/ppermute | solution.py:36
  217.6 51.1 %collective-permute-start.17 = (bf16[512,1024]{1,0:T(8,128)(2,1)}, bf16[512,1024]{1,0:T(8,128)(2,1)}, u32[]{:S(2)}, u32[]{:S(2)}) collective-permute-start(bf16[512,1024]{1,0:T(8,128)(2,1)} %constant_dynamic-slice_fusion.25), channel_id=1, source_target_pairs={{0,1},{1,0},{2,3},{3,2},{4,5},{5,4},{6,7},{7,6},{8,9},{9,8},{10,11... | collective-permute-start | bytes 3145736 | tf_op jit(solution)/shard_map/ppermute | solution.py:33
  246.1 28.4 %collective-permute-start.20 = (bf16[4,1,1,64,1024]{4,3,0,2,1:T(8,128)(2,1)S(1)}, bf16[4,1,1,64,1024]{4,3,0,2,1:T(8,128)(2,1)}, u32[]{:S(2)}, u32[]{:S(2)}) collective-permute-start(bf16[4,1,1,64,1024]{4,3,0,2,1:T(8,128)(2,1)S(1)} %get-tuple-element.145), channel_id=1, source_target_pairs={{0,4},{2,6},{4,0},{6,2},{1,5},{3,7},{5,1},{7,3},{8,12},{10,14},{12... | collective-permute-start | bytes 1572872 | tf_op jit(solution)/shard_map/ppermute | solution.py:36
  289.5 40.0 %collective-permute-start.27 = (bf16[4,1,2,64,1024]{4,3,0,2,1:T(8,128)(2,1)}, bf16[4,1,2,64,1024]{4,3,0,2,1:T(8,128)(2,1)}, u32[]{:S(2)}, u32[]{:S(2)}) collective-permute-start(bf16[4,1,2,64,1024]{4,3,0,2,1:T(8,128)(2,1)} %maximum_select_fusion.17), channel_id=1, source_target_pairs={{0,4},{2,6},{4,0},{6,2},{1,5},{3,7},{5,1},{7,3},{8,12},{10,14},{12... | collective-permute-start | bytes 3145736 | tf_op jit(solution)/shard_map/ppermute | solution.py:36
  290.9 25.6 %collective-permute-start.28 = (bf16[4,1,1,64,1024]{4,3,0,2,1:T(8,128)(2,1)}, bf16[4,1,1,64,1024]{4,3,0,2,1:T(8,128)(2,1)}, u32[]{:S(2)}, u32[]{:S(2)}) collective-permute-start(bf16[4,1,1,64,1024]{4,3,0,2,1:T(8,128)(2,1)} %get-tuple-element.144), channel_id=1, source_target_pairs={{0,2},{2,0},{4,6},{6,4},{1,3},{3,1},{5,7},{7,5},{8,10},{10,8},{12,... | collective-permute-start | bytes 1572872 | tf_op jit(solution)/shard_map/ppermute | solution.py:36
  302.1 30.8 %collective-permute-start.30 = (bf16[4,2,1,64,1024]{4,3,0,2,1:T(8,128)(2,1)}, bf16[4,2,1,64,1024]{4,3,0,2,1:T(8,128)(2,1)}, u32[]{:S(2)}, u32[]{:S(2)}) collective-permute-start(bf16[4,2,1,64,1024]{4,3,0,2,1:T(8,128)(2,1)} %maximum_select_fusion.19), channel_id=1, source_target_pairs={{0,2},{2,0},{4,6},{6,4},{1,3},{3,1},{5,7},{7,5},{8,10},{10,8},{12,... | collective-permute-start | bytes 3145736 | tf_op jit(solution)/shard_map/ppermute | solution.py:36
  318.3 25.3 %collective-permute-start.29 = (bf16[4,1,2,64,1024]{4,3,0,2,1:T(8,128)(2,1)S(1)}, bf16[4,1,2,64,1024]{4,3,0,2,1:T(8,128)(2,1)}, u32[]{:S(2)}, u32[]{:S(2)}) collective-permute-start(bf16[4,1,2,64,1024]{4,3,0,2,1:T(8,128)(2,1)S(1)} %maximum_select_fusion.18), channel_id=1, source_target_pairs={{0,4},{2,6},{4,0},{6,2},{1,5},{3,7},{5,1},{7,3},{8,12},{10,14},{12... | collective-permute-start | bytes 3145736 | tf_op jit(solution)/shard_map/ppermute | solution.py:36
  385.7 287.2 %reduce-scatter.5.cloned.1.call-start = ((), (), s32[]{:S(2)}) async-start(), calls=%async_computation.12 | async-start | bytes 9175040 | tf_op jit(solution)/shard_map/reduce_scatter | solution.py:788
  442.7 39.9 %collective-permute-start.56 = (bf16[512,512]{1,0:T(8,128)(2,1)}, bf16[512,512]{1,0:T(8,128)(2,1)S(1)}, u32[]{:S(2)}, u32[]{:S(2)}) collective-permute-start(bf16[512,512]{1,0:T(8,128)(2,1)} %get-tuple-element.141), channel_id=1, source_target_pairs={{0,1},{1,0},{2,3},{3,2},{4,5},{5,4},{6,7},{7,6},{8,9},{9,8},{10,11... | collective-permute-start | bytes 1572872 | tf_op jit(solution)/shard_map/ppermute | solution.py:33
  513.7 28.1 %collective-permute-start.43 = (bf16[256,1024]{1,0:T(8,128)(2,1)S(1)}, bf16[256,1024]{1,0:T(8,128)(2,1)S(1)}, u32[]{:S(2)}, u32[]{:S(2)}) collective-permute-start(bf16[256,1024]{1,0:T(8,128)(2,1)S(1)} %slice.721), channel_id=1, source_target_pairs={{0,1},{1,0},{2,3},{3,2},{4,5},{5,4},{6,7},{7,6},{8,9},{9,8},{10,11... | collective-permute-start | bytes 1572872 | tf_op jit(solution)/shard_map/ppermute | solution.py:33
  527.8 86.7 %all-to-all-start.4 = ((bf16[4,64,4096]{2,1,0:T(8,128)(2,1)}), bf16[4,64,4096]{2,1,0:T(8,128)(2,1)S(1)}, u32[]{:S(2)}, u32[]{:S(2)}) async-start(bf16[4,64,4096]{2,1,0:T(8,128)(2,1)} %broadcast_select_fusion), calls=%async_computation.5 | async-start | bytes 4194304 | tf_op jit(solution)/shard_map/all_to_all | solution.py:43
  536.9 60.4 %collective-permute-start.46 = (bf16[4,1,2,64,1024]{4,3,0,2,1:T(8,128)(2,1)}, bf16[4,1,2,64,1024]{4,3,0,2,1:T(8,128)(2,1)}, u32[]{:S(2)}, u32[]{:S(2)}) collective-permute-start(bf16[4,1,2,64,1024]{4,3,0,2,1:T(8,128)(2,1)} %copy.214), channel_id=1, source_target_pairs={{0,4},{2,6},{4,0},{6,2},{1,5},{3,7},{5,1},{7,3},{8,12},{10,14},{12... | collective-permute-start | bytes 3145736 | tf_op jit(solution)/shard_map/ppermute | solution.py:36
  541.5 51.3 %collective-permute-start.44 = (bf16[4,2,1,64,1024]{4,3,2,1,0:T(8,128)(2,1)}, bf16[4,2,1,64,1024]{4,3,2,1,0:T(8,128)(2,1)}, u32[]{:S(2)}, u32[]{:S(2)}) collective-permute-start(bf16[4,2,1,64,1024]{4,3,2,1,0:T(8,128)(2,1)} %constant_dynamic-slice_fusion.21), channel_id=1, source_target_pairs={{0,2},{2,0},{4,6},{6,4},{1,3},{3,1},{5,7},{7,5},{8,10},{10,8},{12,... | collective-permute-start | bytes 3145736 | tf_op jit(solution)/shard_map/ppermute | solution.py:36
  547.4 45.2 %collective-permute-start.49 = (f32[592,128]{1,0:T(8,128)S(1)}, f32[592,128]{1,0:T(8,128)S(1)}, u32[]{:S(2)}, u32[]{:S(2)}) collective-permute-start(f32[592,128]{1,0:T(8,128)S(1)} %pad_maximum_fusion.14), channel_id=1, source_target_pairs={{0,2},{2,0},{4,6},{6,4},{1,3},{3,1},{5,7},{7,5},{8,10},{10,8},{12,... | collective-permute-start | bytes 909320 | tf_op jit(solution)/shard_map/ppermute | solution.py:36
  596.4 28.7 %collective-permute-start.50 = (f32[336,128]{1,0:T(8,128)}, f32[336,128]{1,0:T(8,128)}, u32[]{:S(2)}, u32[]{:S(2)}) collective-permute-start(f32[336,128]{1,0:T(8,128)} %pad_maximum_fusion.19), channel_id=1, source_target_pairs={{0,4},{2,6},{4,0},{6,2},{1,5},{3,7},{5,1},{7,3},{8,12},{10,14},{12... | collective-permute-start | bytes 516104 | tf_op jit(solution)/shard_map/ppermute | solution.py:36
  613.0 21.4 %collective-permute-start.51 = (bf16[4,2,1,64,1024]{4,3,0,2,1:T(8,128)(2,1)}, bf16[4,2,1,64,1024]{4,3,0,2,1:T(8,128)(2,1)}, u32[]{:S(2)}, u32[]{:S(2)}) collective-permute-start(bf16[4,2,1,64,1024]{4,3,0,2,1:T(8,128)(2,1)} %copy_select_fusion.1), channel_id=1, source_target_pairs={{0,2},{2,0},{4,6},{6,4},{1,3},{3,1},{5,7},{7,5},{8,10},{10,8},{12,... | collective-permute-start | bytes 3145736 | tf_op jit(solution)/shard_map/ppermute | solution.py:36
  617.9 36.1 %all-to-all-start.5 = ((bf16[4,64,2048]{2,1,0:T(8,128)(2,1)}), bf16[4,64,2048]{2,1,0:T(8,128)(2,1)}, u32[]{:S(2)}, u32[]{:S(2)}) async-start(bf16[4,64,2048]{2,1,0:T(8,128)(2,1)} %maximum_select_fusion.20), calls=%async_computation.6 | async-start | bytes 2097152 | tf_op jit(solution)/shard_map/all_to_all | solution.py:43
  623.6 26.4 %collective-permute-start.53 = (bf16[4,1,2,64,1024]{4,3,0,2,1:T(8,128)(2,1)}, bf16[4,1,2,64,1024]{4,3,0,2,1:T(8,128)(2,1)}, u32[]{:S(2)}, u32[]{:S(2)}) collective-permute-start(bf16[4,1,2,64,1024]{4,3,0,2,1:T(8,128)(2,1)} %copy_select_fusion), channel_id=1, source_target_pairs={{0,4},{2,6},{4,0},{6,2},{1,5},{3,7},{5,1},{7,3},{8,12},{10,14},{12... | collective-permute-start | bytes 3145736 | tf_op jit(solution)/shard_map/ppermute | solution.py:36
  636.9 26.0 %collective-permute-start.52 = (bf16[4,1,1,64,1024]{4,3,0,2,1:T(8,128)(2,1)}, bf16[4,1,1,64,1024]{4,3,0,2,1:T(8,128)(2,1)}, u32[]{:S(2)}, u32[]{:S(2)}) collective-permute-start(bf16[4,1,1,64,1024]{4,3,0,2,1:T(8,128)(2,1)} %constant_dynamic-slice_fusion.14), channel_id=1, source_target_pairs={{0,4},{2,6},{4,0},{6,2},{1,5},{3,7},{5,1},{7,3},{8,12},{10,14},{12... | collective-permute-start | bytes 1572872 | tf_op jit(solution)/shard_map/ppermute | solution.py:36
  676.5 56.2 %all-to-all-start.7 = ((bf16[4,64,5632]{2,1,0:T(8,128)(2,1)}), bf16[4,64,5632]{2,1,0:T(8,128)(2,1)S(1)}, u32[]{:S(2)}, u32[]{:S(2)}) async-start(bf16[4,64,5632]{2,1,0:T(8,128)(2,1)} %maximum_select_fusion), calls=%async_computation.9 | async-start | bytes 5767168 | tf_op jit(solution)/shard_map/all_to_all | solution.py:43
  (170 other events, 963.1 us)
Sparse Core Ops, SparseCore 0:
  13.2 161.5 all-gather.1
  385.8 85.4 reduce-scatter.2
  490.3 98.3 reduce-scatter.4
